TPU v7x, 32 devices: a whole 2x2x4 slice. The times are simulated.
32 devices in a mesh: dp: 8 (over z, x), fsdp: 4 (over y, core).
Axes of the slice: x: 2, y: 2, z: 4, core: 2. Of those that a mesh axis runs over, the one named last changes fastest.
Arguments:
- token_ids: int32 [32, 1024], P(('dp', 'fsdp')), may hold values from 0 to 31998
- mask_flags: int32 [32, 1024], P(('dp', 'fsdp')), may hold values from 0 to 1, as said below
- time_bins: int32 [32], P(('dp', 'fsdp')), may hold values from 0 to 7
- doc_lengths: int32 [32, 4], P(('dp', 'fsdp')), may hold values from 1 to 512, 1024 in all within a row
- layer_mats: float32 [2, 768, 9216], P(None, None, ('fsdp', 'dp'))
- mats_first: float32 [2, 768, 9216], P(None, None, ('fsdp', 'dp')), may hold values from -3.8146973e-06 to 3.8146973e-06
- mats_second: float32 [2, 768, 9216], P(None, None, ('fsdp', 'dp')), may hold values from 2.0787337e-12 to 8.308616e-12
- soap_bases: float32 [2, 4, 768, 768], replicated, as said below
- soap_stats: float32 [2, 4, 768, 768], replicated, as said below
- vocab_tables: float32 [2, 32000, 768], P(None, ('fsdp', 'dp'))
- tables_first: float32 [2, 32000, 768], P(None, ('fsdp', 'dp')), may hold values from -3.8146973e-06 to 3.8146973e-06
- tables_second: float32 [2, 32000, 768], P(None, ('fsdp', 'dp')), may hold values from 2.0787337e-12 to 8.308616e-12
- norm_gains: float32 [5, 768], replicated, may hold values from 0.5 to 1.5
- gains_first: float32 [5, 768], replicated, may hold values from -1.5258789e-05 to 1.5258789e-05
- gains_second: float32 [5, 768], replicated, may hold values from 3.325026e-11 to 1.3300104e-10
Outputs:
- loss_sum: float32 [], replicated
- mask_count: float32 [], replicated
- clip_norm: float32 [], replicated
- new_mats: float32 [2, 768, 9216], P(None, None, ('fsdp', 'dp'))
- new_mats_first: float32 [2, 768, 9216], P(None, None, ('fsdp', 'dp'))
- new_mats_second: float32 [2, 768, 9216], P(None, None, ('fsdp', 'dp'))
- new_bases: float32 [2, 4, 768, 768], replicated
- new_stats: float32 [2, 4, 768, 768], replicated
- new_tables: float32 [2, 32000, 768], P(None, ('fsdp', 'dp'))
- new_tables_first: float32 [2, 32000, 768], P(None, ('fsdp', 'dp'))
- new_tables_second: float32 [2, 32000, 768], P(None, ('fsdp', 'dp'))
- new_gains: float32 [5, 768], replicated
- new_gains_first: float32 [5, 768], replicated
- new_gains_second: float32 [5, 768], replicated
Inputs may be any that keep to these rules, and one draw needn't show every extreme that they name: `mask_flags`: each row has between 1 and 256 masked positions, and in every draw some row has exactly 256. `soap_stats`: every [768, 768] statistic is symmetric positive definite. `soap_bases`: every [768, 768] basis is orthogonal.
All inputs are finite; a program needn't handle non-finite values.
Results may differ from a plain program's by a relative error of at most 0.0018.
The roundings to bfloat16 on the way count: a program that leaves them out, or rounds other values in their place, can miss the bound.
Values may be sent and summed in bfloat16 or wider, within the bound.
No kernel may reach another device: no remote copies, remote signals or barrier semaphores. Data moves between devices by JAX's collectives and lax.ppermute only.
A program may use at most 640 MiB of HBM per device.

v0:
```python
import jax
import jax.numpy as jnp
from jax import lax
from jax.sharding import PartitionSpec as P

D = 768
HEADS = 12
HD = 64
FF = 2048
V = 32000
LAYERS = 2
ROW = 1024
ROWS_DEV = 1
SLOTS = 256
BINS = 8
STEP = 10


highest = lax.Precision.HIGHEST
learn_rate = 0.05
beta_one = 0.9
beta_two = 0.95
eps_adam = 1e-08
decay_weight = 0.1
stat_decay = 0.95
clip_limit = 0.05
norm_eps = 1e-05


def joined(value, axis, join):
    pieces = jax.tree.map(lambda part: lax.all_gather(part, axis), value)
    head = jax.tree.map(lambda part: part[0], pieces)
    tail = jax.tree.map(lambda part: part[1:], pieces)
    subtotal, _ = lax.scan(lambda subtotal, slab: (join(subtotal, slab), None), head, tail)
    return subtotal


def rms_scale(values, gain):
    return values * lax.rsqrt(jnp.mean(values * values, axis=-1, keepdims=True) + norm_eps) * gain


def rotary(values, position, orientation):
    half_dim = values.shape[-1] // 2
    frequency = 10000.0 ** (-jnp.arange(half_dim, dtype=jnp.float32) / half_dim)
    angles = position[..., None].astype(jnp.float32) * frequency
    cosine = jnp.cos(angles)
    sine_part = orientation * jnp.sin(angles)
    first_half = values[..., :half_dim]
    second_half = values[..., half_dim:]
    return jnp.concatenate(
        [
            first_half * cosine - second_half * sine_part,
            second_half * cosine + first_half * sine_part,
        ],
        axis=-1,
    )


def split_heads(matrix):
    return matrix.reshape(ROWS_DEV, ROW, HEADS, HD).transpose(0, 2, 1, 3)


def merge_heads(heads_all):
    return heads_all.transpose(0, 2, 1, 3).reshape(ROWS_DEV, ROW, D)


def project(inputs, weight):
    return jnp.einsum("rsi,io->rso", inputs, weight, preferred_element_type=jnp.float32)


def activate(gate_up):
    return jax.nn.silu(gate_up[..., :FF]) * gate_up[..., FF:]


def heads_of(normed, weights, position):
    projected = project(normed, weights[:, : 3 * D])
    turned_at = position[:, None, :]
    queries = rotary(split_heads(projected[..., :D]), turned_at, 1.0).astype(jnp.bfloat16)
    keys_turned = rotary(split_heads(projected[..., D : 2 * D]), turned_at, 1.0).astype(
        jnp.bfloat16
    )
    values = split_heads(projected[..., 2 * D : 3 * D]).astype(jnp.bfloat16)
    return (queries, keys_turned, values)


def block_soft(queries, keys_turned, same_doc, start_at, block_rows):
    scores = jnp.einsum(
        "rhqd,rhkd->rhqk",
        queries[:, :, start_at : start_at + block_rows],
        keys_turned,
        preferred_element_type=jnp.float32,
    ) * HD ** (-0.5)
    scores = jnp.where(same_doc[:, None, start_at : start_at + block_rows], scores, -1000000000.0)
    return jax.nn.softmax(scores, axis=-1)


def attend(queries, keys_turned, values, same_doc):
    block_rows = min(512, ROW)
    pieces = []
    for start_at in range(0, ROW, block_rows):
        softened = block_soft(queries, keys_turned, same_doc, start_at, block_rows)
        pieces.append(
            jnp.einsum(
                "rhqk,rhkd->rhqd",
                softened.astype(jnp.bfloat16),
                values,
                preferred_element_type=jnp.float32,
            )
        )
    return jnp.concatenate(pieces, axis=2)


def attend_back(queries, keys_turned, values, grad_mixed, same_doc):
    block_rows = min(512, ROW)
    head_scale = HD ** (-0.5)
    outputs = []
    grad_queries = []
    grad_keys = jnp.zeros(keys_turned.shape, jnp.float32)
    grad_values = jnp.zeros(values.shape, jnp.float32)
    for start_at in range(0, ROW, block_rows):
        softened = block_soft(queries, keys_turned, same_doc, start_at, block_rows)
        soft_low = softened.astype(jnp.bfloat16)
        grad_block = grad_mixed[:, :, start_at : start_at + block_rows]
        outputs.append(
            jnp.einsum("rhqk,rhkd->rhqd", soft_low, values, preferred_element_type=jnp.float32)
        )
        grad_soft = jnp.einsum(
            "rhqd,rhkd->rhqk", grad_block, values, preferred_element_type=jnp.float32
        )
        grad_scores = (
            softened * (grad_soft - jnp.sum(softened * grad_soft, axis=-1, keepdims=True))
        ).astype(jnp.bfloat16)
        grad_queries.append(
            jnp.einsum(
                "rhqk,rhkd->rhqd", grad_scores, keys_turned, preferred_element_type=jnp.float32
            )
            * head_scale
        )
        grad_keys = (
            grad_keys
            + jnp.einsum(
                "rhqk,rhqd->rhkd",
                grad_scores,
                queries[:, :, start_at : start_at + block_rows],
                preferred_element_type=jnp.float32,
            )
            * head_scale
        )
        grad_values = grad_values + jnp.einsum(
            "rhqk,rhqd->rhkd", soft_low, grad_block, preferred_element_type=jnp.float32
        )
    return (
        jnp.concatenate(outputs, axis=2),
        jnp.concatenate(grad_queries, axis=2),
        grad_keys,
        grad_values,
    )


def layer_forward(residual, weights, gain_pair, same_doc, position):
    normed = rms_scale(residual, gain_pair[0]).astype(jnp.bfloat16)
    queries, keys_turned, values = heads_of(normed, weights, position)
    attended = merge_heads(attend(queries, keys_turned, values, same_doc)).astype(jnp.bfloat16)
    middle = residual + project(attended, weights[:, 3 * D : 4 * D])
    normed_ffn = rms_scale(middle, gain_pair[1]).astype(jnp.bfloat16)
    activated = activate(project(normed_ffn, weights[:, 4 * D : 4 * D + 2 * FF])).astype(
        jnp.bfloat16
    )
    return (
        middle
        + jnp.einsum(
            "rsf,df->rsd",
            activated,
            weights[:, 4 * D + 2 * FF :],
            preferred_element_type=jnp.float32,
        ),
        middle,
    )


def layer_back(residual, middle, weights, gain_pair, same_doc, position, grad_out):
    normed_full, pull_att = jax.vjp(rms_scale, residual, gain_pair[0])
    normed = normed_full.astype(jnp.bfloat16)
    queries, keys_turned, values = heads_of(normed, weights, position)
    ffn_full, pull_ffn = jax.vjp(rms_scale, middle, gain_pair[1])
    normed_ffn = ffn_full.astype(jnp.bfloat16)
    gate_up = project(normed_ffn, weights[:, 4 * D : 4 * D + 2 * FF])
    activated_full, pull_act = jax.vjp(activate, gate_up)
    activated = activated_full.astype(jnp.bfloat16)
    grad_low = grad_out.astype(jnp.bfloat16)
    down_weight = weights[:, 4 * D + 2 * FF :]
    grad_down = jnp.einsum("rsd,rsf->df", grad_low, activated, preferred_element_type=jnp.float32)
    grad_act = jnp.einsum("rsd,df->rsf", grad_low, down_weight, preferred_element_type=jnp.float32)
    grad_gate_up = pull_act(grad_act)[0].astype(jnp.bfloat16)
    grad_gu_weight = jnp.einsum(
        "rsi,rso->io", normed_ffn, grad_gate_up, preferred_element_type=jnp.float32
    )
    grad_ffn_in = jnp.einsum(
        "rso,io->rsi",
        grad_gate_up,
        weights[:, 4 * D : 4 * D + 2 * FF],
        preferred_element_type=jnp.float32,
    )
    grad_middle_part, grad_gain_ffn = pull_ffn(grad_ffn_in)
    grad_middle = grad_out + grad_middle_part
    grad_branch = grad_middle.astype(jnp.bfloat16)
    grad_mixed = split_heads(
        jnp.einsum(
            "rsd,id->rsi",
            grad_branch,
            weights[:, 3 * D : 4 * D],
            preferred_element_type=jnp.float32,
        )
    ).astype(jnp.bfloat16)
    mixed, grad_queries, grad_keys, grad_values = attend_back(
        queries, keys_turned, values, grad_mixed, same_doc
    )
    attended = merge_heads(mixed).astype(jnp.bfloat16)
    grad_out_weight = jnp.einsum(
        "rsi,rsd->id", attended, grad_branch, preferred_element_type=jnp.float32
    )
    turned_at = position[:, None, :]
    grad_projected = jnp.concatenate(
        [
            merge_heads(rotary(grad_queries, turned_at, -1.0)),
            merge_heads(rotary(grad_keys, turned_at, -1.0)),
            merge_heads(grad_values),
        ],
        axis=-1,
    ).astype(jnp.bfloat16)
    grad_qkv_weight = jnp.einsum(
        "rsi,rso->io", normed, grad_projected, preferred_element_type=jnp.float32
    )
    grad_att_in = jnp.einsum(
        "rso,io->rsi", grad_projected, weights[:, : 3 * D], preferred_element_type=jnp.float32
    )
    grad_residual_part, grad_gain_att = pull_att(grad_att_in)
    grad_weights = jnp.concatenate(
        [grad_qkv_weight, grad_out_weight, grad_gu_weight, grad_down], axis=1
    )
    return (
        grad_middle + grad_residual_part,
        grad_weights,
        jnp.stack([grad_gain_att, grad_gain_ffn]),
    )


def combine_totals(first_part, second_part):
    top_both = jnp.maximum(first_part[0], second_part[0])
    summed = first_part[1] * jnp.exp(first_part[0] - top_both) + second_part[1] * jnp.exp(
        second_part[0] - top_both
    )
    return (top_both, summed, first_part[2] + second_part[2])


def adam_update(weight, grad, first, second):
    first = beta_one * first + (1.0 - beta_one) * grad
    second = beta_two * second + (1.0 - beta_two) * grad * grad
    heading = (
        first / (1.0 - beta_one**STEP) / (jnp.sqrt(second / (1.0 - beta_two**STEP)) + eps_adam)
    )
    return (weight - learn_rate * (heading + decay_weight * weight), first, second)


def renew_basis(statistic, basis):
    product = jnp.dot(statistic, basis, precision=highest)
    gram = jnp.dot(product.T, product, precision=highest)
    lower_factor = jnp.linalg.cholesky(gram)
    return jax.scipy.linalg.solve_triangular(lower_factor, product.T, lower=True).T


def shards(
    token_ids,
    mask_flags,
    time_bins,
    doc_lengths,
    layer_mats,
    mats_first,
    mats_second,
    soap_bases,
    soap_stats,
    vocab_tables,
    tables_first,
    tables_second,
    norm_gains,
    gains_first,
    gains_second,
):
    group_mats, work_tables = (
        lax.all_gather(layer_mats.astype(jnp.bfloat16), "dp", axis=2, tiled=True),
        lax.all_gather(vocab_tables.astype(jnp.bfloat16), "dp", axis=1, tiled=True),
    )
    spots_all = jnp.arange(ROW, dtype=jnp.int32)
    ends_at = jnp.cumsum(doc_lengths, axis=1)
    passed = spots_all[None, :, None] >= ends_at[:, None, :]
    doc_index = jnp.sum(passed.astype(jnp.int32), axis=2)
    position = spots_all[None, :] - jnp.sum(jnp.where(passed, doc_lengths[:, None, :], 0), axis=2)
    same_doc = doc_index[:, :, None] == doc_index[:, None, :]
    input_ids = jnp.where(mask_flags == 1, V - 1, token_ids)
    slot_order = jnp.argsort((1 - mask_flags) * ROW + spots_all[None, :], axis=1)[:, :SLOTS]
    masked_total = jnp.sum(mask_flags, axis=1)
    time_code = jnp.where(
        jnp.arange(SLOTS)[None, :] < masked_total[:, None], time_bins[:, None] + 1, 0
    )
    targets = jnp.take_along_axis(token_ids, slot_order, axis=1)
    group_inputs, group_targets, group_codes = (
        lax.all_gather(input_ids.reshape(-1), "fsdp", axis=0, tiled=True),
        lax.all_gather(targets.reshape(-1), "fsdp", axis=0, tiled=True),
        lax.all_gather(time_code.reshape(-1), "fsdp", axis=0, tiled=True),
    )
    shard_rows = work_tables.shape[1]
    vocab_start = lax.axis_index("fsdp") * shard_rows
    local_inputs = group_inputs - vocab_start
    inside = (local_inputs >= 0) & (local_inputs < shard_rows)
    clamped = jnp.clip(local_inputs, 0, shard_rows - 1)
    picked_rows = jnp.where(inside[:, None], work_tables[0][clamped], jnp.zeros((), jnp.bfloat16))
    residual = (
        lax.psum_scatter(picked_rows, "fsdp", scatter_dimension=0, tiled=True)
        .astype(jnp.float32)
        .reshape(ROWS_DEV, ROW, D)
    )
    saved_inputs = []
    for layer_at in range(LAYERS):
        full_weights = lax.all_gather(group_mats[layer_at], "fsdp", axis=1, tiled=True)
        next_residual, middle = layer_forward(
            residual, full_weights, norm_gains[2 * layer_at : 2 * layer_at + 2], same_doc, position
        )
        saved_inputs.append((residual, middle))
        residual = next_residual
    final_full, pull_final = jax.vjp(rms_scale, residual, norm_gains[2 * LAYERS])
    chosen = (
        jnp.take_along_axis(final_full, slot_order[:, :, None], axis=1)
        .reshape(ROWS_DEV * SLOTS, D)
        .astype(jnp.bfloat16)
    )
    group_states = lax.all_gather(chosen, "fsdp", axis=0, tiled=True)
    head_rows = work_tables[1]
    logits = jnp.einsum("nd,vd->nv", group_states, head_rows, preferred_element_type=jnp.float32)
    local_targets = group_targets - vocab_start
    onehot = jnp.arange(shard_rows, dtype=jnp.int32)[None, :] == local_targets[:, None]
    local_top = jnp.max(logits, axis=1)
    local_total = jnp.sum(jnp.exp(logits - local_top[:, None]), axis=1)
    local_target = jnp.sum(jnp.where(onehot, logits, 0.0), axis=1)
    top_all, total_all, target_all = joined(
        (local_top, local_total, local_target), "fsdp", combine_totals
    )
    log_total = top_all + jnp.log(total_all)
    weight = jnp.where(group_codes > 0, BINS / jnp.maximum(group_codes, 1).astype(jnp.float32), 0.0)
    own_start = lax.axis_index("fsdp") * (ROWS_DEV * SLOTS)
    loss_part = jnp.sum(
        lax.dynamic_slice_in_dim(weight * (log_total - target_all), own_start, ROWS_DEV * SLOTS)
    )
    count_part = jnp.sum(mask_flags).astype(jnp.float32)
    grad_logits = (
        weight[:, None] * (jnp.exp(logits - log_total[:, None]) - onehot.astype(jnp.float32))
    ).astype(jnp.bfloat16)
    grad_states_group = jnp.einsum(
        "nv,vd->nd", grad_logits, head_rows, preferred_element_type=jnp.float32
    )
    grad_head = jnp.einsum(
        "nv,nd->vd", grad_logits, group_states, preferred_element_type=jnp.float32
    )
    grad_states = lax.psum_scatter(
        grad_states_group, "fsdp", scatter_dimension=0, tiled=True
    ).reshape(ROWS_DEV, SLOTS, D)
    placed = jax.vmap(
        lambda blank_rows, slot_at, slot_values: blank_rows.at[slot_at].set(slot_values)
    )(jnp.zeros((ROWS_DEV, ROW, D), jnp.float32), slot_order, grad_states)
    grad_residual, grad_final_gain = pull_final(placed)
    mat_grads = []
    pair_grads = []
    for layer_at in reversed(range(LAYERS)):
        full_weights = lax.all_gather(group_mats[layer_at], "fsdp", axis=1, tiled=True)
        grad_residual, grad_weights, grad_pair = layer_back(
            saved_inputs[layer_at][0],
            saved_inputs[layer_at][1],
            full_weights,
            norm_gains[2 * layer_at : 2 * layer_at + 2],
            same_doc,
            position,
            grad_residual,
        )
        mat_grads.insert(0, lax.psum_scatter(grad_weights, "fsdp", scatter_dimension=1, tiled=True))
        pair_grads.insert(0, grad_pair)
    gain_part = jnp.concatenate(pair_grads + [grad_final_gain[None, :]], axis=0)
    group_grads = lax.all_gather(
        grad_residual.reshape(ROWS_DEV * ROW, D), "fsdp", axis=0, tiled=True
    )
    embed_grad = jax.ops.segment_sum(
        jnp.where(inside[:, None], group_grads, 0.0), clamped, num_segments=shard_rows
    )
    own_mats, own_tables = (
        lax.psum_scatter(jnp.stack(mat_grads), "dp", scatter_dimension=2, tiled=True),
        lax.psum_scatter(jnp.stack([embed_grad, grad_head]), "dp", scatter_dimension=1, tiled=True),
    )
    own_cols = own_mats.shape[2]
    column_ids = lax.axis_index(("fsdp", "dp")) * own_cols + jnp.arange(own_cols, dtype=jnp.int32)
    kind_index = (
        (column_ids >= 3 * D).astype(jnp.int32)
        + (column_ids >= 4 * D).astype(jnp.int32)
        + (column_ids >= 4 * D + 2 * FF).astype(jnp.int32)
    )
    kind_masks = (kind_index[None, :] == jnp.arange(4, dtype=jnp.int32)[:, None]).astype(
        jnp.float32
    )
    stat_part = jnp.einsum("lic,kc,ljc->lkij", own_mats, kind_masks, own_mats, precision=highest)
    square_part = jnp.sum(own_mats * own_mats) + jnp.sum(own_tables * own_tables)
    square_sum, stat_sum, gain_sum, loss_sum, mask_count = lax.psum(
        (square_part, stat_part, gain_part, loss_part, count_part), ("dp", "fsdp")
    )
    clip_norm = jnp.sqrt(square_sum + jnp.sum(gain_sum * gain_sum)) / mask_count
    factor = jnp.minimum(1.0, clip_limit / clip_norm) / mask_count
    clipped = own_mats * factor
    turned = jnp.einsum("lkij,lic,kc->ljc", soap_bases, clipped, kind_masks, precision=highest)
    new_mats_first = beta_one * mats_first + (1.0 - beta_one) * turned
    new_mats_second = beta_two * mats_second + (1.0 - beta_two) * turned * turned
    heading = (
        new_mats_first
        / (1.0 - beta_one**STEP)
        / (jnp.sqrt(new_mats_second / (1.0 - beta_two**STEP)) + eps_adam)
    )
    direction = jnp.einsum("lkij,ljc,kc->lic", soap_bases, heading, kind_masks, precision=highest)
    new_mats = layer_mats - learn_rate * (direction + decay_weight * layer_mats)
    new_stats = stat_decay * soap_stats + (1.0 - stat_decay) * (factor * factor) * stat_sum
    new_bases = jax.vmap(renew_basis)(
        new_stats.reshape(-1, D, D), soap_bases.reshape(-1, D, D)
    ).reshape(soap_bases.shape)
    new_tables, new_tables_first, new_tables_second = adam_update(
        vocab_tables, own_tables * factor, tables_first, tables_second
    )
    new_gains, new_gains_first, new_gains_second = adam_update(
        norm_gains, gain_sum * factor, gains_first, gains_second
    )
    return (
        loss_sum,
        mask_count,
        clip_norm,
        new_mats,
        new_mats_first,
        new_mats_second,
        new_bases,
        new_stats,
        new_tables,
        new_tables_first,
        new_tables_second,
        new_gains,
        new_gains_first,
        new_gains_second,
    )


def solution(mesh):
    placed = (
        P(("dp", "fsdp"), None),
        P(("dp", "fsdp"), None),
        P(("dp", "fsdp")),
        P(("dp", "fsdp"), None),
        P(None, None, ("fsdp", "dp")),
        P(None, None, ("fsdp", "dp")),
        P(None, None, ("fsdp", "dp")),
        P(),
        P(),
        P(None, ("fsdp", "dp"), None),
        P(None, ("fsdp", "dp"), None),
        P(None, ("fsdp", "dp"), None),
        P(),
        P(),
        P(),
    )
    return jax.shard_map(
        shards,
        mesh=mesh,
        in_specs=placed,
        out_specs=(
            P(),
            P(),
            P(),
            P(None, None, ("fsdp", "dp")),
            P(None, None, ("fsdp", "dp")),
            P(None, None, ("fsdp", "dp")),
            P(),
            P(),
            P(None, ("fsdp", "dp"), None),
            P(None, ("fsdp", "dp"), None),
            P(None, ("fsdp", "dp"), None),
            P(),
            P(),
            P(),
        ),
        check_vma=False,
    )
```

profile of v0, /device:TPU:0, one launch (start us, length us, event | category | flops | bytes accessed | tf_op | source)
XLA Modules:
  0.0 5426.5 jit_solution(370139443907814525)
XLA Ops:
  24.2 460.8 %all-gather.16.cloned.1.call-done = bf16[2,8000,768]{2,1,0:T(8,128)(2,1)} async-done(((bf16[2,1000,768]{2,1,0:T(8,128)(2,1)}), bf16[2,8000,768]{2,1,0:T(8,128)(2,1)}) %all-gather.16.cloned.1.call-update) | async-done | bytes 24576016 | tf_op jit(solution)/shard_map/all_gather | solution.py:291
  535.7 60.8 %all-gather.18.cloned.1.call-done = bf16[2,768,2304]{1,2,0:T(8,128)(2,1)} async-done(((bf16[2,768,288]{1,2,0:T(8,128)(2,1)}), bf16[2,768,2304]{1,2,0:T(8,128)(2,1)}) %all-gather.18.cloned.1.call-update) | async-done | bytes 7077904 | tf_op jit(solution)/shard_map/all_gather | solution.py:290
  610.0 46.2 reduce-scatter.6.cloned.1.call-done
  658.6 90.8 %all-gather.22.cloned.1.call-done = bf16[1,768,9216]{1,2,0:T(8,128)(2,1)} async-done(((bf16[1,768,2304]{1,2,0:T(8,128)(2,1)}), bf16[1,768,9216]{1,2,0:T(8,128)(2,1)}) %all-gather.22.cloned.1.call-update) | async-done | bytes 14155792 | tf_op jit(solution)/shard_map/all_gather | solution.py:324
  797.1 34.0 fusion.325
  930.6 33.8 fusion.331
  1128.9 32.7 reduce-scatter.8.cloned.1.call-done
  1661.8 189.6 %reduce-scatter.10.cloned.1.call-done = f32[768,2304]{1,0:T(8,128)} async-done(((f32[768,9216]{1,0:T(8,128)}), f32[768,2304]{1,0:T(8,128)}) %reduce-scatter.10.cloned.1.call-update) | async-done | bytes 7077904 | tf_op jit(solution)/shard_map/reduce_scatter | solution.py:383
  1887.3 26.8 convolution_bitcast_fusion
  1960.2 38.1 scatter_custom_fusion
  1998.3 34.1 pad_maximum_fusion
  2036.0 341.3 %all-reduce.12.cloned.1.call-done = f32[2,768,2304]{1,0,2:T(2,128)} async-done(((f32[2,768,2304]{1,0,2:T(2,128)}), f32[2,768,2304]{1,0,2:T(2,128)}) %all-reduce.12.cloned.1.call-update) | async-done | bytes 14155792
  2381.2 769.8 %reduce-scatter.14.cloned.1.call-done = f32[2,1000,768]{2,1,0:T(8,128)} async-done(((f32[2,8000,768]{2,1,0:T(8,128)}), f32[2,1000,768]{2,1,0:T(8,128)}) %reduce-scatter.14.cloned.1.call-update) | async-done | bytes 6144016 | tf_op jit(solution)/shard_map/reduce_scatter | solution.py:394
  3157.2 40.0 all-reduce.6
  3204.8 34.6 fusion.47
  3243.7 29.9 divide_bitcast_fusion
  3311.6 230.5 %all-reduce.10.cloned.1.call-done = f32[2,4,768,768]{3,2,1,0:T(8,128)} async-done(((f32[2,4,768,768]{3,2,1,0:T(8,128)}), f32[2,4,768,768]{3,2,1,0:T(8,128)}) %all-reduce.10.cloned.1.call-update) | async-done | bytes 18874384 | tf_op jit(solution)/shard_map/psum | solution.py:408
  3560.7 52.4 fusion.340
  3620.0 54.7 %fusion.341 = f32[8,768,768]{2,1,0:T(8,128)} fusion(f32[8,768,768]{2,1,0:T(8,128)S(1)} %fusion.340), kind=kOutput, calls=%fused_computation.536 | convolution fusion | flops 43486543872 | bytes 37748736 | tf_op jit(solution)/shard_map/vmap()/dot_general | solution.py:267
  3712.7 93.8 %custom-call.53 = f32[8,128,128]{2,1,0:T(8,128)S(1)} custom-call(f32[8,128,128]{2,1,0:T(8,128)S(1)} %cholesky.426), custom_call_target="Cholesky" | custom-call | tf_op jit(solution)/shard_map/vmap(jit(cholesky))/cholesky | solution.py:268
  3814.6 79.0 %custom-call.54 = f32[8,1,128,128]{2,3,1,0:T(8,128)S(1)} custom-call(f32[8,1,128,128]{3,2,1,0:T(8,128)S(1)} %select_bitcast_fusion.4), custom_call_target="InvertDiagBlocksLowerTriangular" | custom-call | tf_op jit(solution)/shard_map/vmap(jit(cholesky))/cholesky | solution.py:268
  3904.4 95.2 %custom-call.55 = f32[8,128,128]{2,1,0:T(8,128)} custom-call(f32[8,128,128]{2,1,0:T(8,128)} %cholesky.430), custom_call_target="Cholesky" | custom-call | tf_op jit(solution)/shard_map/vmap(jit(cholesky))/cholesky | solution.py:268
  4001.8 80.2 %custom-call.56 = f32[8,1,128,128]{2,3,1,0:T(8,128)} custom-call(f32[8,1,128,128]{3,2,1,0:T(8,128)} %get-tuple-element.238), custom_call_target="InvertDiagBlocksLowerTriangular" | custom-call | tf_op jit(solution)/shard_map/vmap(jit(cholesky))/cholesky | solution.py:268
  4094.2 94.6 %custom-call.57 = f32[8,128,128]{2,1,0:T(8,128)S(1)} custom-call(f32[8,128,128]{2,1,0:T(8,128)} %cholesky.435), custom_call_target="Cholesky" | custom-call | tf_op jit(solution)/shard_map/vmap(jit(cholesky))/cholesky | solution.py:268
  4189.9 80.2 %custom-call.58 = f32[8,1,128,128]{2,3,1,0:T(8,128)} custom-call(f32[8,1,128,128]{3,2,1,0:T(8,128)} %get-tuple-element.236), custom_call_target="InvertDiagBlocksLowerTriangular" | custom-call | tf_op jit(solution)/shard_map/vmap(jit(cholesky))/cholesky | solution.py:268
  4282.1 94.6 %custom-call.59 = f32[8,128,128]{2,1,0:T(8,128)S(1)} custom-call(f32[8,128,128]{2,1,0:T(8,128)} %cholesky.440), custom_call_target="Cholesky" | custom-call | tf_op jit(solution)/shard_map/vmap(jit(cholesky))/cholesky | solution.py:268
  4377.9 80.4 %custom-call.60 = f32[8,1,128,128]{2,3,1,0:T(8,128)} custom-call(f32[8,1,128,128]{3,2,1,0:T(8,128)} %get-tuple-element.234), custom_call_target="InvertDiagBlocksLowerTriangular" | custom-call | tf_op jit(solution)/shard_map/vmap(jit(cholesky))/cholesky | solution.py:268
  4468.4 94.4 %custom-call.61 = f32[8,128,128]{2,1,0:T(8,128)} custom-call(f32[8,128,128]{2,1,0:T(8,128)S(1)} %cholesky.445), custom_call_target="Cholesky" | custom-call | tf_op jit(solution)/shard_map/vmap(jit(cholesky))/cholesky | solution.py:268
  4565.1 80.2 %custom-call.62 = f32[8,1,128,128]{2,3,1,0:T(8,128)} custom-call(f32[8,1,128,128]{3,2,1,0:T(8,128)} %get-tuple-element.232), custom_call_target="InvertDiagBlocksLowerTriangular" | custom-call | tf_op jit(solution)/shard_map/vmap(jit(cholesky))/cholesky | solution.py:268
  4654.3 95.2 %custom-call.63 = f32[8,128,128]{2,1,0:T(8,128)} custom-call(f32[8,128,128]{2,1,0:T(8,128)} %fusion.215), custom_call_target="Cholesky" | custom-call | tf_op jit(solution)/shard_map/vmap(jit(cholesky))/cholesky | solution.py:268
  4790.6 472.5 %custom-call.64 = f32[8,6,128,128]{2,3,1,0:T(8,128)S(1)} custom-call(f32[8,6,128,128]{3,2,1,0:T(8,128)} %bitcast.536), custom_call_target="InvertDiagBlocksLowerTriangular" | custom-call | tf_op jit(solution)/shard_map/vmap(jit(_solve_triangular))/triangular_solve | solution.py:269
  5364.3 28.0 fusion.134
  (588 shorter events, 1356.4 us)
Async XLA Ops:
  8.0 477.0 %all-gather.16.cloned.1.call-start = ((), (), s32[]{:S(2)}) async-start(), calls=%async_computation.5 | async-start | bytes 27648000 | tf_op jit(solution)/shard_map/all_gather | solution.py:291
  12.8 583.8 %all-gather.18.cloned.1.call-start = ((), (), s32[]{:S(2)}) async-start(), calls=%async_computation.7 | async-start | bytes 7962624 | tf_op jit(solution)/shard_map/all_gather | solution.py:290
  15.2 592.3 %sort.19.cloned.1.call-start = ((), (), s32[]{:S(2)}) async-start(), calls=%async_computation.18 | async-start | bytes 24608 | tf_op jit(solution)/shard_map/jit(argsort)/sort | solution.py:300
  17.2 639.1 %reduce-scatter.6.cloned.1.call-start = ((), (), s32[]{:S(2)}) async-start(), calls=%async_computation.6 | async-start | bytes 7864320 | tf_op jit(solution)/shard_map/reduce_scatter | solution.py:318
  23.5 506.0 %copy-start.86 = (pred[4096]{0:T(1024)(128)(4,1)}, pred[4096]{0:T(1024)(128)(4,1)S(1)}, u32[]{:S(2)}) copy-start(pred[4096]{0:T(1024)(128)(4,1)S(1)} %and_reduce_fusion) | copy-start | bytes 12292
  535.7 213.7 %all-gather.22.cloned.1.call-start = ((), (), s32[]{:S(2)}) async-start(), calls=%async_computation.14 | async-start | bytes 17694720 | tf_op jit(solution)/shard_map/all_gather | solution.py:324
  603.1 279.9 %all-gather.24.cloned.1.call-start = ((), (), s32[]{:S(2)}) async-start(), calls=%async_computation.15 | async-start | bytes 17694720 | tf_op jit(solution)/shard_map/all_gather | solution.py:324
  603.7 440.3 %all-gather.20.cloned.1.call-start = ((), (), s32[]{:S(2)}) async-start(), calls=%async_computation.8 | async-start | bytes 1966080 | tf_op jit(solution)/shard_map/all_gather | solution.py:336
  604.7 151.4 %copy-start.111 = (f32[768]{0:T(1024)}, f32[768]{0:T(1024)S(1)}, u32[]{:S(2)}) copy-start(f32[768]{0:T(1024)S(1)} %get-tuple-element.138) | copy-start | bytes 9220
  604.7 252.7 %copy-start.98 = (f32[768]{0:T(1024)}, f32[768]{0:T(1024)S(1)}, u32[]{:S(2)}) copy-start(f32[768]{0:T(1024)S(1)} %get-tuple-element.137) | copy-start | bytes 9220
  605.9 163.5 %copy-start.36 = (f32[1024,32]{0,1:T(8,128)}, f32[1024,32]{0,1:T(8,128)S(1)}, u32[]{:S(2)}) copy-start(f32[1024,32]{0,1:T(8,128)S(1)} %get-tuple-element.250) | copy-start | bytes 393220
  605.9 163.5 %copy-start.76 = (f32[1024,32]{0,1:T(8,128)}, f32[1024,32]{0,1:T(8,128)S(1)}, u32[]{:S(2)}) copy-start(f32[1024,32]{0,1:T(8,128)S(1)} %get-tuple-element.249) | copy-start | bytes 393220
  608.9 147.1 %copy-start.118 = (s32[1,256]{1,0:T(1,128)}, s32[1,256]{1,0:T(1,128)S(1)}, u32[]{:S(2)}) copy-start(s32[1,256]{1,0:T(1,128)S(1)} %get-tuple-element.251) | copy-start | bytes 3076
  658.6 97.4 %copy-start.114 = (f32[1024]{0:T(1024)}, f32[1024]{0:T(1024)S(1)}, u32[]{:S(2)}) copy-start(f32[1024]{0:T(1024)S(1)} %fusion.268) | copy-start | bytes 12292
  797.1 44.7 copy-start.88
  918.2 46.2 copy-start.92
  930.6 44.1 copy-start.65
  1024.4 137.2 %reduce-scatter.8.cloned.1.call-start = ((), (), s32[]{:S(2)}) async-start(), calls=%async_computation.9 | async-start | bytes 3932160 | tf_op jit(solution)/shard_map/reduce_scatter | solution.py:363
  1030.8 66.9 %copy-start.128 = (f32[4,1,256]{2,1,0:T(1,128)}, f32[4,1,256]{2,1,0:T(1,128)S(1)}, u32[]{:S(2)}) copy-start(f32[4,1,256]{2,1,0:T(1,128)S(1)} %compare_select_fusion.1) | copy-start | bytes 12292
  1038.1 59.6 %copy-start.116 = (s32[1,1024]{1,0:T(1,128)}, s32[1,1024]{1,0:T(1,128)S(1)}, u32[]{:S(2)}) copy-start(s32[1,1024]{1,0:T(1,128)S(1)} %broadcast_subtract_fusion) | copy-start | bytes 12292
  1123.5 538.3 %reduce-scatter.12.cloned.1.call-start = ((), (), s32[]{:S(2)}) async-start(), calls=%async_computation.11 | async-start | bytes 35389440 | tf_op jit(solution)/shard_map/reduce_scatter | solution.py:383
  1401.4 449.9 %reduce-scatter.10.cloned.1.call-start = ((), (), s32[]{:S(2)}) async-start(), calls=%async_computation.10 | async-start | bytes 35389440 | tf_op jit(solution)/shard_map/reduce_scatter | solution.py:383
  1415.7 36.4 copy-start.24
  1650.1 285.4 %all-gather.26.cloned.1.call-start = ((), (), s32[]{:S(2)}) async-start(), calls=%async_computation.16 | async-start | bytes 15728640 | tf_op jit(solution)/shard_map/all_gather | solution.py:386
  1661.7 715.6 %all-reduce.12.cloned.1.call-start = ((), (), s32[]{:S(2)}) async-start(), calls=%async_computation.17 | async-start | bytes 28311552
  1886.0 49.5 copy-start.87
  1886.0 1265.0 %reduce-scatter.14.cloned.1.call-start = ((), (), s32[]{:S(2)}) async-start(), calls=%async_computation.12 | async-start | bytes 55296000 | tf_op jit(solution)/shard_map/reduce_scatter | solution.py:394
  2032.5 1509.6 %all-reduce.10.cloned.1.call-start = ((), (), s32[]{:S(2)}) async-start(), calls=%async_computation.13 | async-start | bytes 37748736 | tf_op jit(solution)/shard_map/psum | solution.py:408
  3239.3 58.6 %slice-start = ((s8[6144000]{0:T(1024)(128)(4,1)}), s8[1949696]{0:T(1024)(128)(4,1)S(1)}, s32[]{:S(2)}) async-start(s8[6144000]{0:T(1024)(128)(4,1)} %bitcast.469), calls=%async_computation.20 | async-start | bytes 3899392
  3243.7 54.2 slice-start.1
  4562.8 186.8 %copy-start.56 = (f32[8,128,128]{2,1,0:T(8,128)S(1)}, f32[8,128,128]{2,1,0:T(8,128)}, u32[]{:S(2)}) copy-start(f32[8,128,128]{2,1,0:T(8,128)} %custom-call.55) | copy-start | bytes 1572868
  4647.8 104.9 %copy-start.55 = (pred[768,768]{1,0:T(8,128)(4,1)S(1)}, pred[768,768]{1,0:T(8,128)(4,1)}, u32[]{:S(2)}) copy-start(pred[768,768]{1,0:T(8,128)(4,1)} %iota_compare_fusion.1) | copy-start | bytes 1769476
  (130 other events, 1073.5 us)
Sparse Core Ops, SparseCore 0:
  12.9 472.0 all-gather.15
  487.8 108.7 all-gather.17
  599.7 56.5 reduce-scatter.5
  658.3 91.0 all-gather.21
  751.5 91.0 all-gather.23
  1024.5 19.4 all-gather.19
  1123.6 37.9 reduce-scatter.7
  1401.5 201.0 reduce-scatter.11
  1650.2 201.1 reduce-scatter.9
  1853.3 82.0 all-gather.25
  1940.1 437.1 all-reduce.11
  2381.1 769.8 reduce-scatter.13
Sparse Core Ops, SparseCore 1:
  19.5 5.6 sort.21.cloned.1.call-done
  3239.4 302.6 all-reduce.9
  (1 shorter events, 0.0 us)
where the time goes:
time: 5440 us; the launch traced here: 5430 us
  waiting for transfers between devices  2250 us (41%)
  other arithmetic  1880 us (35%)
  matrix products  938 us (17%)
  local copies, waits for them, and re-layouts  261 us (5%)
  blocking collectives  71.9 us (1%)
    another operation x26, other arithmetic, renew_basis(): lower_factor = jnp.linalg.cholesky(gram)  978 us
    reduce_scatter x1, waiting for transfers between devices, shards(): lax.psum_scatter(jnp.stack([embed_grad, grad_head]), 'dp', scatter_dimens...  770 us
    another operation x4, other arithmetic, renew_basis(): jax.scipy.linalg.solve_triangular(lower_factor, product.T, lower=True)  487 us
    all_gather x1, waiting for transfers between devices, shards(): lax.all_gather(vocab_tables.astype(jnp.bfloat16), 'dp', axis=1, tiled=True)  461 us
    unnamed x14, waiting for transfers between devices  342 us
    psum x1, waiting for transfers between devices, shards(): lax.psum((square_part, stat_part, gain_part, loss_part, count_part), ('dp...  231 us
    reduce_scatter x2, waiting for transfers between devices, shards(): lax.psum_scatter(grad_weights, 'fsdp', scatter_dimension=1, tiled=True)  190 us
    another operation x11, matrix products, renew_basis(): jax.scipy.linalg.solve_triangular(lower_factor, product.T, lower=True)  136 us
  transfers between devices with their start and end apart: 13, of which 11 were waited for; matrix products, arithmetic and copies ran while one was open for 13% of the time, Pallas kernels for 0%

commit v1 on v0

v1 whole, which is shorter than its diff:
```python
import jax
import jax.numpy as jnp
import numpy as np
from jax import lax
from jax.experimental import pallas as pl
from jax.experimental.pallas import tpu as pltpu
from jax.sharding import Mesh
from jax.sharding import PartitionSpec as P

D = 768
HEADS = 12
HD = 64
FF = 2048
V = 32000
LAYERS = 2
ROW = 1024
SLOTS = 256
BINS = 8
STEP = 10
WIDE = 9216
KINDS = 4
BOUNDS = (0, 3 * D, 4 * D, 4 * D + 2 * FF, WIDE)
CAP = 40
PAIR = 2 * HD
PAIRS = D // PAIR
BLOCK = 256
VMEM_CAP = 56 * 2**20
STEPS = 128
LIGHT = pl.CostEstimate(flops=1000, bytes_accessed=1000, transcendentals=0)
TILE = 8

bf16 = jnp.bfloat16
f32 = jnp.float32
highest = lax.Precision.HIGHEST
high = lax.Precision.HIGH
learn_rate = 0.05
beta_one = 0.9
beta_two = 0.95
eps_adam = 1e-08
decay_weight = 0.1
stat_decay = 0.95
clip_limit = 0.05
norm_eps = 1e-05

OWNERS = ("y", "c", "z", "x")
DATA = ("z", "x", "y", "c")
DP = ("z", "x")
FS = ("y", "c")
HEAD_GROUP = ("x", "y", "c")


def dot(a, b, dims, precision=None):
    return lax.dot_general(a, b, (dims, ((), ())), precision=precision, preferred_element_type=f32)


def nn(a, b, precision=None):
    return dot(a, b, ((1,), (0,)), precision)


def nt(a, b, precision=None):
    return dot(a, b, ((1,), (1,)), precision)


def tn(a, b, precision=None):
    return dot(a, b, ((0,), (0,)), precision)


def rms_scale(values, gain):
    return values * lax.rsqrt(jnp.mean(values * values, axis=-1, keepdims=True) + norm_eps) * gain


def silu_up(gate, up):
    return jax.nn.silu(gate) * up


def mm(a, b, ca, cb):
    return lax.dot_general(a, b, (((ca,), (cb,)), ((), ())), preferred_element_type=f32)


def rotate(x, cosine, sine, low_half):
    other = jnp.where(low_half, pltpu.roll(x, PAIR - HD // 2, 1), pltpu.roll(x, HD // 2, 1))
    return x * cosine + other * sine


def lane_masks():
    lane = lax.broadcasted_iota(jnp.int32, (1, PAIR), 1)
    return lane % HD < HD // 2, (lane < HD, lane >= HD)


def attend_kernel(q_ref, k_ref, v_ref, cq_ref, sq_ref, ck_ref, sk_ref, docq_ref, dock_ref,
                  out_ref, qs_ref, kt_ref, vb_ref, lse_ref):
    low_half, own = lane_masks()
    queries = rotate(q_ref[...], cq_ref[...], sq_ref[...], low_half).astype(bf16)
    qs_ref[...] = queries * jnp.asarray(HD ** (-0.5), bf16)
    keys = rotate(k_ref[...], ck_ref[...], sk_ref[...], low_half).astype(bf16)
    kt_ref[...] = keys
    values = v_ref[...]
    vb_ref[...] = values.astype(bf16)
    values_t = values.T.astype(bf16)
    dock = jnp.concatenate([dock_ref[...]] * (BLOCK // 128), axis=1)
    for at in range(0, q_ref.shape[0], BLOCK):
        rows = slice(at, at + BLOCK)
        same = dock == docq_ref[:, rows]
        outs = []
        for h in range(2):
            scores = mm(jnp.where(own[h], keys, 0), qs_ref[rows, :], 1, 1)
            scores = jnp.where(same, scores, -1000000000.0)
            top = jnp.max(scores, axis=0, keepdims=True)
            soft = jnp.exp(scores - top)
            total = jnp.sum(soft, axis=0, keepdims=True)
            lse_ref[0, h : h + 1, rows] = top + jnp.log(total)
            soft = (soft * (1.0 / total)).astype(bf16)
            outs.append(mm(values_t[h * HD : (h + 1) * HD], soft, 1, 0))
        out_ref[rows, :] = jnp.concatenate(outs, axis=0).T.astype(bf16)


def attend_back_kernel(qs_ref, k_ref, v_ref, g_ref, lse_ref, cq_ref, sq_ref, ck_ref, sk_ref, docq_ref, dock_ref,
                       dq_ref, dk_ref, dv_ref, dk_sum, dv_sum):
    low_half, own = lane_masks()
    keys, values = k_ref[...], v_ref[...]
    keys_t = keys.astype(f32).T.astype(bf16)
    dock = jnp.concatenate([dock_ref[...]] * (BLOCK // 128), axis=1)
    for at in range(0, qs_ref.shape[0], BLOCK):
        rows = slice(at, at + BLOCK)
        same = dock == docq_ref[:, rows]
        queries, grad = qs_ref[rows, :], g_ref[rows, :]
        back = []
        for h in range(2):
            scores = mm(jnp.where(own[h], keys, 0), queries, 1, 1)
            soft = jnp.exp(jnp.where(same, scores, -1000000000.0) - lse_ref[0, h : h + 1, rows])
            grad_soft = mm(jnp.where(own[h], values, 0), grad, 1, 1)
            delta = jnp.sum(soft * grad_soft, axis=0, keepdims=True)
            grad_scores = (soft * (grad_soft - delta)).astype(bf16)
            dv = mm(soft.astype(bf16), jnp.where(own[h], grad, 0), 1, 0)
            dk = mm(grad_scores, jnp.where(own[h], queries, 0), 1, 0)
            if at == 0 and h == 0:
                dv_sum[...] = dv
                dk_sum[...] = dk
            else:
                dv_sum[...] += dv
                dk_sum[...] += dk
            back.append(mm(keys_t[h * HD : (h + 1) * HD], grad_scores, 1, 0))
        dq = jnp.concatenate(back, axis=0).T * HD ** (-0.5)
        dq_ref[rows, :] = rotate(dq, cq_ref[rows, :], -sq_ref[rows, :], low_half).astype(bf16)
    dk_ref[...] = rotate(dk_sum[...], ck_ref[...], -sk_ref[...], low_half).astype(bf16)
    dv_ref[...] = dv_sum[...].astype(bf16)


def column(rows, shift=0):
    return pl.BlockSpec((rows, PAIR), lambda h: (0, h + shift))


def whole(shape):
    return pl.BlockSpec(shape, lambda h: (0,) * len(shape))


def stat_spec(rows):
    return pl.BlockSpec((1, 2, rows), lambda h: (h, 0, 0))


def attend(q, kv, turn_q, turn_k, doc_q, doc_k):
    n_q, n_k = q.shape[0], kv.shape[0]
    low = jax.ShapeDtypeStruct((n_q, D), bf16)
    low_k = jax.ShapeDtypeStruct((n_k, D), bf16)
    return pl.pallas_call(
        attend_kernel,
        grid=(PAIRS,),
        in_specs=[column(n_q), column(n_k), column(n_k, PAIRS)]
        + [whole((n_q, PAIR))] * 2 + [whole((n_k, PAIR))] * 2 + [whole((1, n_q)), whole((n_k, 128))],
        out_specs=[column(n_q), column(n_q), column(n_k), column(n_k), stat_spec(n_q)],
        out_shape=[low, low, low_k, low_k, jax.ShapeDtypeStruct((PAIRS, 2, n_q), f32)],
        compiler_params=pltpu.CompilerParams(vmem_limit_bytes=VMEM_CAP),
        cost_estimate=LIGHT,
        name="attend",
    )(q, kv, kv, *turn_q, *turn_k, doc_q, doc_k)


def attend_back(qs, k, v, grad, lse, turn_q, turn_k, doc_q, doc_k):
    n_q, n_k = qs.shape[0], k.shape[0]
    low = jax.ShapeDtypeStruct((n_q, D), bf16)
    low_k = jax.ShapeDtypeStruct((n_k, D), bf16)
    return pl.pallas_call(
        attend_back_kernel,
        grid=(PAIRS,),
        in_specs=[column(n_q), column(n_k), column(n_k), column(n_q), stat_spec(n_q)]
        + [whole((n_q, PAIR))] * 2 + [whole((n_k, PAIR))] * 2 + [whole((1, n_q)), whole((n_k, 128))],
        out_specs=[column(n_q), column(n_k), column(n_k)],
        out_shape=[low, low_k, low_k],
        scratch_shapes=[pltpu.VMEM((n_k, PAIR), f32)] * 2,
        compiler_params=pltpu.CompilerParams(vmem_limit_bytes=VMEM_CAP),
        cost_estimate=LIGHT,
        name="attend_back",
    )(qs, k, v, grad, lse, *turn_q, *turn_k, doc_q, doc_k)


def pair_tables(position):
    half = HD // 2
    frequency = 10000.0 ** (-jnp.arange(half, dtype=f32) / half)
    angles = position[:, None].astype(f32) * frequency
    cosine, sine = jnp.cos(angles), jnp.sin(angles)
    return jnp.concatenate([cosine] * 4, axis=1), jnp.concatenate([-sine, sine] * 2, axis=1)


def fm(a, b, ca, cb):
    return lax.dot_general(a, b, (((ca,), (cb,)), ((), ())), precision=highest, preferred_element_type=f32)


def inverse_factor(block):
    row_at = lax.broadcasted_iota(jnp.int32, (STEPS, STEPS), 0)
    col_at = lax.broadcasted_iota(jnp.int32, (STEPS, STEPS), 1)
    eye = jnp.where(row_at == col_at, 1.0, 0.0).astype(f32)
    sub = lax.broadcasted_iota(jnp.int32, (TILE, 1), 0)
    n = STEPS // TILE
    left = [block[i * TILE : (i + 1) * TILE] for i in range(n)]
    right = [eye[i * TILE : (i + 1) * TILE] for i in range(n)]
    for j in range(STEPS):
        at, within = divmod(j, TILE)
        row = left[at][within : within + 1]
        scale = 1.0 / row[:, j : j + 1]
        row = row * scale
        mate = right[at][within : within + 1] * scale
        for i in range(at, n):
            column = left[i][:, j : j + 1]
            if i == at:
                column = jnp.where(sub > within, column, 0.0)
            left[i] = left[i] - column * row
            right[i] = right[i] - column * mate
    upper = jnp.concatenate(left, axis=0)
    pivots = jnp.sum(jnp.where(row_at == col_at, upper, 0.0), axis=1, keepdims=True)
    return jnp.concatenate(right, axis=0) * lax.rsqrt(pivots)


def orthogonal_kernel(gram_ref, rows_ref, out_ref, rest):
    rest[...] = gram_ref[...]
    out_ref[...] = rows_ref[...]
    lane = lax.broadcasted_iota(jnp.int32, (1, D), 1)

    def body(b, _):
        start = pl.multiple_of(b * STEPS, STEPS)
        here = pl.ds(start, STEPS)
        inverse = inverse_factor(rest[here, here])
        upper = jnp.where(lane >= start + STEPS, fm(inverse, rest[here, :], 1, 0), 0.0)
        done = fm(out_ref[:, here], inverse, 1, 1)
        out_ref[...] -= fm(done, upper, 1, 0)
        out_ref[:, here] = done
        rest[...] -= fm(upper, upper, 0, 0)
        return 0

    lax.fori_loop(0, D // STEPS, body, 0)


def orthogonal_rows(gram, rows):
    return pl.pallas_call(
        orthogonal_kernel,
        out_shape=jax.ShapeDtypeStruct(rows.shape, f32),
        in_specs=[pl.BlockSpec(memory_space=pltpu.VMEM)] * 2,
        out_specs=pl.BlockSpec(memory_space=pltpu.VMEM),
        scratch_shapes=[pltpu.VMEM((D, D), f32)],
        compiler_params=pltpu.CompilerParams(vmem_limit_bytes=40 * 2**20),
        cost_estimate=LIGHT,
        name="orthogonal_rows",
    )(gram, rows)


def adam_update(weight, grad, first, second):
    first = beta_one * first + (1.0 - beta_one) * grad
    second = beta_two * second + (1.0 - beta_two) * grad * grad
    heading = (
        first / (1.0 - beta_one**STEP) / (jnp.sqrt(second / (1.0 - beta_two**STEP)) + eps_adam)
    )
    return (weight - learn_rate * (heading + decay_weight * weight), first, second)


def parts_of(weights):
    return (
        weights[: 3 * D],
        weights[3 * D : 4 * D],
        weights[4 * D : 4 * D + 2 * FF],
        weights[4 * D + 2 * FF :],
    )


def layer_forward(residual, slots, weights, gains, doc, tables):
    w_qkv, w_out, w_gu, w_down = parts_of(weights)
    normed = rms_scale(residual, gains[0]).astype(bf16)
    if slots is None:
        rows_in, normed_q, doc_q, tables_q = residual, normed, doc[0], tables
    else:
        pick, doc_q, tables_q = slots
        rows_in = nn(pick.astype(f32), residual, highest)
        normed_q = nn(pick, normed).astype(bf16)
    attended, *kept = attend(
        nt(normed_q, w_qkv[:D]), nt(normed, w_qkv[D:]), tables_q, tables, doc_q, doc[1]
    )
    middle = rows_in + nt(attended, w_out)
    normed_ffn = rms_scale(middle, gains[1]).astype(bf16)
    gate_up = nt(normed_ffn, w_gu)
    activated = silu_up(gate_up[:, :FF], gate_up[:, FF:]).astype(bf16)
    result = middle + nn(activated, w_down)
    saved = (residual, normed, normed_q, kept, attended, middle, normed_ffn, gate_up, activated)
    return result, saved


def ffn_back(grad_out, saved, weights, gains, between):
    _, _, w_gu, w_down = parts_of(weights)
    _, _, _, _, attended, middle, normed_ffn, gate_up, activated = saved
    grad_low = grad_out.astype(bf16)
    grad_down = tn(activated, grad_low)
    grad_act = nt(grad_low, w_down)
    _, pull_act = jax.vjp(silu_up, gate_up[:, :FF], gate_up[:, FF:])
    grad_gate_up = jnp.concatenate(pull_act(grad_act), axis=1).astype(bf16)
    grad_gate_up, grad_down = between((grad_gate_up, grad_down))
    grad_gu = tn(grad_gate_up, normed_ffn)
    _, pull_ffn = jax.vjp(rms_scale, middle, gains[1])
    grad_middle, grad_gain = pull_ffn(nn(grad_gate_up, w_gu))
    grad_middle = grad_out + grad_middle
    branch = grad_middle.astype(bf16)
    return grad_middle, branch, tn(branch, attended), grad_gu, grad_down, grad_gain


def attention_back(grad_middle, branch, saved, slots, weights, gains, doc, tables, before, between):
    w_qkv, w_out, _, _ = parts_of(weights)
    residual, normed, normed_q, kept, _, _, _, _, _ = saved
    grad_att = before(nn(branch, w_out).astype(bf16))
    if slots is None:
        doc_q, tables_q = doc[0], tables
    else:
        pick, doc_q, tables_q = slots
    qs, k, v, lse = kept
    grads = attend_back(qs, k, v, grad_att, lse, tables_q, tables, doc_q, doc[1])
    grad_q, grad_k, grad_v = between(grads)
    grad_qkv = jnp.concatenate([tn(grad_q, normed_q), tn(grad_k, normed), tn(grad_v, normed)], 0)
    grad_in = nn(grad_k, w_qkv[D : 2 * D]) + nn(grad_v, w_qkv[2 * D :])
    grad_in_q = nn(grad_q, w_qkv[:D])
    if slots is not None:
        grad_in_q = tn(pick.astype(f32), grad_in_q, highest)
        grad_middle = tn(pick.astype(f32), grad_middle, highest)
    _, pull_att = jax.vjp(rms_scale, residual, gains[0])
    grad_residual, grad_gain = pull_att(grad_in + grad_in_q)
    return grad_middle + grad_residual, grad_qkv, grad_gain


def renew_rows(statistic, basis, start, rows):
    product = nn(statistic, basis, highest)
    gram = tn(product, product, highest)
    return orthogonal_rows(gram, lax.dynamic_slice_in_dim(product, start, rows))


def make_shards(sizes):
    n_z, n_x, n_y, n_c = (sizes[a] for a in ("z", "x", "y", "c"))
    n_dp, n_fs = n_z * n_x, n_y * n_c
    n_dev = n_dp * n_fs
    per = V // n_dev
    cols = WIDE // n_dev
    span = WIDE // n_fs
    n_mats = LAYERS * KINDS
    stat_rows = D // n_dp
    sharing = n_dev // n_mats
    basis_rows = D // sharing
    kind_of = np.searchsorted(np.array(BOUNDS[1:]), np.arange(WIDE), side="right")
    kind_lo = [int(kind_of[f * span]) for f in range(n_fs)]
    kind_hi = [int(kind_of[(f + 1) * span - 1]) for f in range(n_fs)]
    slots_all = n_dev * CAP
    shape = (n_z, n_x, n_y, n_c)
    paired = n_x == 2 and n_y == 2 and n_c == 2 and n_dp == n_mats

    def moved(value, target):
        pairs = []
        for source in np.ndindex(n_z, n_x, n_y, n_c):
            dest = target(*source)
            if dest is not None:
                pairs.append((np.ravel_multi_index(source, shape), np.ravel_multi_index(dest, shape)))
        return lax.ppermute(value, DATA, [(int(s), int(d)) for s, d in pairs])

    def line_gather(own):
        if not paired:
            return lax.all_gather(own, "z", axis=0, tiled=True)
        at = lax.axis_index("z")
        places = jnp.zeros((2 * n_z - 1,) + own.shape, own.dtype).at[n_z - 1].set(own)
        up, down = own, own
        for k in range(1, n_z):
            up = moved(up, lambda z, x, y, c: (z + 1, x, y, c) if z + 1 < n_z else None)
            down = moved(down, lambda z, x, y, c: (z - 1, x, y, c) if z > 0 else None)
            places = places.at[n_z - 1 - k].set(up).at[n_z - 1 + k].set(down)
        return lax.dynamic_slice_in_dim(places, n_z - 1 - at, n_z, axis=0).reshape(-1, D)

    def take(value, axis, at):
        return lax.dynamic_index_in_dim(value, at, axis, keepdims=False)

    def z_line(value, inside):
        at = lax.axis_index("z")
        up, down = 0.0, 0.0
        for k in range(n_z - 1, 0, -1):
            up = value[jnp.minimum(at + k, n_z - 1)] + up
            down = value[jnp.maximum(at - k, 0)] + down
            up, down = yield (
                (up, lambda z, x, y, c: (z + 1, x, y, c) if inside(y, c) and z + k < n_z else None),
                (down, lambda z, x, y, c: (z - 1, x, y, c) if inside(y, c) and z >= k else None),
            )
        return value[at] + up + down

    def two_ways(value, cross_y, inside):
        half = value.shape[-2] // 2
        first, second = value[..., :half, :], value[..., half:, :]
        x = lax.axis_index("x")
        x_at = -3
        sent_x, sent_y = yield (
            (take(first, x_at, 1 - x), lambda z, x, y, c: (z, 1 - x, y, c) if inside(None, c) else None),
            cross_y(second),
        )
        first = take(first, x_at, x) + sent_x
        second = cross_y(second, sent_y)
        sent_x, sent_y = yield (
            (take(second, x_at, 1 - x), lambda z, x, y, c: (z, 1 - x, y, c) if inside(y, c) else None),
            cross_y(first),
        )
        first = cross_y(first, sent_y)
        second = take(second, x_at, x) + sent_x
        return (yield from z_line(jnp.concatenate([first, second], axis=-2), inside))

    def sum_all(value):
        c, y = lax.axis_index("c"), lax.axis_index("y")
        (sent,) = yield ((take(value, 1, 1 - c), lambda z, x, y, c: (z, x, y, 1 - c)),)
        value = take(value, 1, c) + sent

        def cross_y(part, sent=None):
            if sent is None:
                return take(part, 0, 1 - y), lambda z, x, y, c: (z, x, 1 - y, c)
            return take(part, 0, y) + sent

        return (yield from two_ways(value, cross_y, lambda y, c: True))

    def sum_at(value, y_at, c_at=None):
        c = lax.axis_index("c")
        if c_at is None:
            request = value[1 - c], lambda z, x, y, c: (z, x, y, 1 - c)
        else:
            request = value, lambda z, x, y, c: (z, x, y, c_at) if c != c_at else None
        (sent,) = yield (request,)
        value = (value[c] if c_at is None else value) + sent

        def inside(y, c):
            return (y is None or y == y_at) and (c_at is None or c == c_at)

        def cross_y(part, sent=None):
            if sent is None:
                return part, lambda z, x, y, c: (z, x, y_at, c) if y != y_at and inside(None, c) else None
            return part + sent

        return (yield from two_ways(value, cross_y, inside))

    class Lane:
        def __init__(self, steps):
            self.steps, self.done, self.flying = steps, False, []
            self.asks = next(steps)

        def land(self, landed):
            try:
                self.asks = self.steps.send(landed)
            except StopIteration as end:
                self.done, self.result = True, end.value

    def start(value, *lanes):
        lanes = [lane for lane in lanes if not lane.done]
        operands = [[operand for operand, _ in lane.asks] for lane in lanes]
        value, operands = lax.optimization_barrier((value, operands))
        for lane, each in zip(lanes, operands):
            lane.flying = [moved(operand, target) for operand, (_, target) in zip(each, lane.asks)]
        return value

    def tick(value, *lanes):
        lanes = [lane for lane in lanes if not lane.done]
        value, landed = lax.optimization_barrier((value, [lane.flying for lane in lanes]))
        for lane, each in zip(lanes, landed):
            lane.land(each)
        return start(value, *lanes)

    def stat_routes():
        rounds, taken = [], []
        for kind in range(KINDS):
            blocks = range(BOUNDS[kind] // cols, -(-BOUNDS[kind + 1] // cols))
            for share, part in enumerate(np.array_split(np.array(blocks), sharing)):
                for block in part:
                    r = 0
                    while r < len(rounds) and (block in taken[r] or (kind, share) in rounds[r].values()):
                        r += 1
                    if r == len(rounds):
                        rounds.append({})
                        taken.append(set())
                    rounds[r][int(block)] = (kind, share)
                    taken[r].add(block)
        masks = np.zeros((KINDS, sharing, len(rounds), cols), np.float32)
        for r, each in enumerate(rounds):
            for block, (kind, share) in each.items():
                masks[kind, share, r] = kind_of[block * cols : (block + 1) * cols] == kind
        return rounds, masks

    def gather_stat(own, layer_at):
        rounds, _ = stat_routes()
        received = []
        for each in rounds:

            def target(z, x, y, c, each=each):
                found = each.get((y * n_c + c) * n_dp + z * n_x + x)
                if found is None:
                    return None
                kind, share = found
                dp = layer_at * KINDS + kind
                return dp // n_x, dp % n_x, share // n_c, share % n_c

            received.append(moved(own, target))
        return received

    def share_stat(pieces, mask):
        columns = jnp.concatenate([piece * mask[r][:, None] for r, piece in enumerate(pieces)], axis=0)
        part = tn(columns, columns, highest)
        c = lax.axis_index("c")
        halves = part.reshape(2, D // 2, D)
        mine = take(halves, 0, c) + moved(take(halves, 0, 1 - c), lambda z, x, y, c: (z, x, y, 1 - c))
        mine = mine + moved(mine, lambda z, x, y, c: (z, x, 1 - y, c))
        other = moved(mine, lambda z, x, y, c: (z, x, y, 1 - c))
        return jnp.where(c == 0, jnp.concatenate([mine, other], 0), jnp.concatenate([other, mine], 0))

    def shards(
        token_ids,
        mask_flags,
        time_bins,
        doc_lengths,
        layer_mats,
        mats_first,
        mats_second,
        soap_bases,
        soap_stats,
        vocab_tables,
        tables_first,
        tables_second,
        norm_gains,
        gains_first,
        gains_second,
    ):
        tokens, flags, lengths = token_ids[0], mask_flags[0], doc_lengths[0]
        work_mats = layer_mats.astype(bf16).transpose(0, 2, 1)
        work_tables = vocab_tables.astype(bf16)
        spots = jnp.arange(ROW, dtype=jnp.int32)

        ids = jnp.where(flags == 1, V - 1, tokens)
        owner = ids // per
        same_id = ids[:, None] == ids[None, :]
        before = spots[None, :] < spots[:, None]
        is_first = ~jnp.any(same_id & before, axis=1)
        place = jnp.sum(
            (before & is_first[None, :] & (owner[:, None] == owner[None, :])).astype(jnp.int32), axis=1
        )
        place = jnp.sum(jnp.where(same_id & is_first[None, :], place[None, :], 0), axis=1)
        mats_0 = lax.all_gather(work_mats[0], OWNERS, axis=0, tiled=True)
        slot_ids = jnp.arange(slots_all, dtype=jnp.int32)
        row_ids = jnp.arange(per, dtype=jnp.int32)

        def plan(turn_at):
            at = place - turn_at * CAP
            slot = jnp.where((at >= 0) & (at < CAP), owner * CAP + at, -1)
            hit = slot[:, None] == slot_ids[None, :]
            asked = jnp.max(jnp.where(hit, ids[:, None] % per, -1), axis=0).reshape(n_dev, CAP)
            most = jnp.broadcast_to(jnp.max(place), (n_dev, 128 - CAP))
            asked = jnp.concatenate([asked, most], axis=1)
            asked = lax.all_to_all(asked, OWNERS, 0, 0, tiled=True)
            rows = asked[:, :CAP].reshape(-1)[:, None] == row_ids[None, :]
            return hit, rows, jnp.max(asked[:, CAP]) // CAP + 1

        def fetch(hit, rows):
            sent = nn(rows.astype(bf16), work_tables[0]).astype(bf16)
            got = lax.all_to_all(sent, OWNERS, 0, 0, tiled=True)
            return nn(hit.astype(bf16), got)

        def embed_send(hit, grad):
            return tn(hit.astype(f32), grad, high)

        def exchange(sent):
            return lax.all_to_all(sent, OWNERS, 0, 0, tiled=True)

        def embed_sum(rows, got):
            return tn(rows.astype(f32), got, high)

        def fetch_more(turn_at, residual):
            hit, rows, _ = plan(turn_at)
            return residual + fetch(hit, rows)

        def give_more(turn_at, carry):
            total, grad = carry
            hit, rows, _ = plan(turn_at)
            return total + embed_sum(rows, exchange(embed_send(hit, grad))), grad

        hit_0, rows_0, rounds = plan(0)
        residual = fetch(hit_0, rows_0)
        residual = lax.fori_loop(1, rounds, fetch_more, residual)

        at_fs = lax.axis_index(FS)
        lo = jnp.asarray(kind_lo, jnp.int32)[at_fs]
        hi = jnp.asarray(kind_hi, jnp.int32)[at_fs]
        col_ids = (at_fs * n_dp + lax.axis_index(DP)) * cols + jnp.arange(cols, dtype=jnp.int32)
        kind_ids = sum((col_ids >= b).astype(jnp.int32) for b in BOUNDS[1:-1])
        in_lo = kind_ids == lo

        def stat_scatter(own):
            part = jnp.concatenate(
                [tn(jnp.where(in_lo[:, None], own, 0.0), own, highest), tn(jnp.where(in_lo[:, None], 0.0, own), own, highest)],
                axis=0,
            ).reshape(2, D, D)
            every = jnp.stack(
                [jnp.where(lo == kind, part[0], jnp.where(hi == kind, part[1], 0.0)) for kind in range(KINDS)]
            ).reshape(KINDS * D, D)
            return lax.psum_scatter(every, DATA, scatter_dimension=0, tiled=True)

        ends = jnp.cumsum(lengths)
        passed = spots[:, None] >= ends[None, :]
        doc = jnp.sum(passed.astype(jnp.int32), axis=1)
        position = spots - jnp.sum(jnp.where(passed, lengths[None, :], 0), axis=1)
        tables = pair_tables(position)
        docs = (doc[None, :], jnp.broadcast_to(doc[:, None], (ROW, 128)))

        count = jnp.sum(flags)
        order = jnp.where(flags == 1, jnp.cumsum(flags) - 1, count + jnp.cumsum(1 - flags) - 1)
        at_slot = order[None, :] == jnp.arange(SLOTS, dtype=jnp.int32)[:, None]
        pick = at_slot.astype(bf16)

        def picked(vector):
            return jnp.sum(jnp.where(at_slot, vector[None, :], jnp.zeros((), vector.dtype)), axis=1)

        targets = picked(tokens)
        valid = jnp.arange(SLOTS, dtype=jnp.int32) < count
        code = jnp.where(valid, time_bins[0] + 1, 0)
        slots = (pick, picked(doc)[None, :], pair_tables(picked(position)))

        group_codes = lax.all_gather(jnp.stack([targets, code]), HEAD_GROUP, axis=1, tiled=True)
        group_targets, group_codes = group_codes[0], group_codes[1]

        mats_1 = lax.all_gather(work_mats[1], OWNERS, axis=0, tiled=True)
        head = line_gather(work_tables[1])

        residual, saved_0 = layer_forward(residual, None, mats_0, norm_gains[0:2], docs, tables)
        final, saved_1 = layer_forward(residual, slots, mats_1, norm_gains[2:4], docs, tables)

        chosen_full, pull_final = jax.vjp(rms_scale, final, norm_gains[2 * LAYERS])
        states = lax.all_gather(chosen_full.astype(bf16), HEAD_GROUP, axis=0, tiled=True)
        logits = nt(states, head)
        base_shard = lax.axis_index(FS) * n_dp + lax.axis_index("x")
        vocab_ids = (
            (base_shard + jnp.arange(n_z, dtype=jnp.int32) * n_x)[:, None] * per + row_ids[None, :]
        ).reshape(-1)
        onehot = vocab_ids[None, :] == group_targets[:, None]
        top = jnp.max(logits, axis=1)
        total = jnp.sum(jnp.exp(logits - top[:, None]), axis=1)
        hit_logit = jnp.sum(jnp.where(onehot, logits, 0.0), axis=1)
        each = lax.all_gather(jnp.stack([top, total, hit_logit]), HEAD_GROUP, axis=0)
        top_all = jnp.max(each[:, 0], axis=0)
        log_total = top_all + jnp.log(jnp.sum(each[:, 1] * jnp.exp(each[:, 0] - top_all), axis=0))
        target_logit = jnp.sum(each[:, 2], axis=0)
        weight = jnp.where(group_codes > 0, BINS / jnp.maximum(group_codes, 1).astype(f32), 0.0)
        own_start = lax.axis_index(HEAD_GROUP) * SLOTS
        loss_part = jnp.sum(
            lax.dynamic_slice_in_dim(weight * (log_total - target_logit), own_start, SLOTS)
        )
        grad_logits = (
            weight[:, None] * (jnp.exp(logits - log_total[:, None]) - onehot.astype(f32))
        ).astype(bf16)
        grad_states = lax.psum_scatter(nn(grad_logits, head), HEAD_GROUP, scatter_dimension=0, tiled=True)
        head_part = tn(grad_logits, states)
        grad_states, head_part = lax.optimization_barrier((grad_states, head_part))
        grad_head = lax.psum_scatter(head_part, "z", scatter_dimension=0, tiled=True)
        grad_final, grad_final_gain = pull_final(grad_states)

        def same(value):
            return value

        middle_1, branch, out_1, gu_1, down_1, gain_f1 = ffn_back(
            grad_final, saved_1, mats_1, norm_gains[2:4], same
        )
        grad_1, qkv_1, gain_a1 = attention_back(
            middle_1, branch, saved_1, slots, mats_1, norm_gains[2:4], docs, tables, same, same
        )
        all_1 = jnp.concatenate([qkv_1, out_1, gu_1, down_1], axis=0)
        if paired:
            blocks = (n_z, n_x, cols, D)
            kept_head = [grad_head]

            def land_head(value):
                value, kept_head[0] = lax.optimization_barrier((value, kept_head[0]))
                return tick(value, lane_1)

            lane_1 = Lane(sum_all(all_1.reshape((n_y, n_c) + blocks)))
            grad_1 = start(grad_1, lane_1)
            middle_0, branch, out_0, gu_0, down_0, gain_f0 = ffn_back(
                grad_1, saved_0, mats_0, norm_gains[0:2], lambda v: tick(v, lane_1)
            )
            cut = span - D
            early_2 = Lane(sum_at(jnp.concatenate([out_0, gu_0[:cut]], axis=0).reshape(blocks), 0, 1))
            early_1 = Lane(sum_at(jnp.concatenate([gu_0[cut:], down_0], axis=0).reshape((n_c,) + blocks), 1))
            middle_0, branch = start((middle_0, branch), early_1, early_2)
            grad_0, qkv_0, gain_a0 = attention_back(
                middle_0, branch, saved_0, None, mats_0, norm_gains[0:2], docs, tables,
                lambda v: tick(v, early_1, early_2), land_head,
            )
            late = Lane(sum_at(qkv_0.reshape(blocks), 0, 0))
            sent = embed_send(hit_0, grad_0)
            grad_0, sent = start((grad_0, sent), late)
            embed_got = exchange(sent)
            lanes = (late, lane_1, early_1, early_2)
            tick(grad_0, *lanes)
            while not lane_1.done:
                tick(grad_0, *lanes)
            own_1 = lane_1.result
            pieces_1 = gather_stat(own_1, 1)
            tick(grad_0, *lanes)
            embed_got, pieces_1 = lax.optimization_barrier((embed_got, pieces_1))
            while not all(lane.done for lane in lanes):
                tick(grad_0, *lanes)
            y, c = lax.axis_index("y"), lax.axis_index("c")
            own_0 = jnp.where(y == 1, early_1.result, jnp.where(c == 1, early_2.result, late.result))
            grad_head = kept_head[0]
            pieces_0 = gather_stat(own_0, 0)
        else:
            own_1 = lax.psum_scatter(all_1, OWNERS, scatter_dimension=0, tiled=True)
            middle_0, branch, out_0, gu_0, down_0, gain_f0 = ffn_back(
                grad_1, saved_0, mats_0, norm_gains[0:2], same
            )
            grad_0, qkv_0, gain_a0 = attention_back(
                middle_0, branch, saved_0, None, mats_0, norm_gains[0:2], docs, tables, same, same
            )
            all_0 = jnp.concatenate([qkv_0, out_0, gu_0, down_0], axis=0)
            own_0 = lax.psum_scatter(all_0, OWNERS, scatter_dimension=0, tiled=True)
            embed_got, stat_1 = exchange(embed_send(hit_0, grad_0)), stat_scatter(own_1)
            stat_0 = stat_scatter(own_0)
        grad_embed = embed_sum(rows_0, embed_got)
        grad_embed, _ = lax.fori_loop(1, rounds, give_more, (grad_embed, grad_0))

        gain_part = jnp.stack([gain_a0, gain_f0, gain_a1, gain_f1, grad_final_gain])
        own_mats = jnp.stack([own_0, own_1])
        square = jnp.sum(own_mats * own_mats) + jnp.sum(grad_embed * grad_embed) + jnp.sum(grad_head * grad_head)
        scalars = jnp.stack([square, loss_part, count.astype(f32)])
        small = jnp.concatenate([gain_part, jnp.broadcast_to(scalars[:, None], (3, D))], axis=0)
        small = jnp.sum(lax.all_gather(small, DATA, axis=0), axis=0)
        gain_sum = small[: 2 * LAYERS + 1]
        square_sum, loss_sum, mask_count = (small[2 * LAYERS + 1 + i, 0] for i in range(3))
        clip_norm = jnp.sqrt(square_sum + jnp.sum(gain_sum * gain_sum)) / mask_count
        factor = jnp.minimum(1.0, clip_limit / clip_norm) / mask_count

        at_dp = lax.axis_index(DP)
        stat_scale = (1.0 - stat_decay) * (factor * factor)
        own_mat = at_dp * n_mats // n_dp
        linear = at_dp * n_fs + at_fs
        basis_start = (linear % sharing) * basis_rows
        flat_stats = soap_stats.reshape(n_mats, D, D)
        if paired:
            mask = jnp.asarray(stat_routes()[1])[own_mat % KINDS, at_fs]
            own_sum = share_stat([a + b for a, b in zip(pieces_0, pieces_1)], mask)
        else:
            own_sum = jnp.concatenate(
                [lax.all_gather(part, DATA, axis=0, tiled=True) for part in (stat_0, stat_1)], axis=0
            ).reshape(n_mats, D, D)[own_mat]
        own_stat = stat_decay * flat_stats[own_mat] + stat_scale * own_sum
        stats_part = lax.dynamic_slice_in_dim(own_stat, basis_start, basis_rows)
        new_stats = lax.all_gather(stats_part, DATA, axis=0, tiled=True).reshape(soap_stats.shape)
        own_basis = soap_bases.reshape(n_mats, D, D)[own_mat]
        new_rows = renew_rows(own_stat, own_basis, basis_start, basis_rows)
        new_bases = lax.all_gather(new_rows, DATA, axis=0, tiled=True).reshape(soap_bases.shape)

        clipped = own_mats * factor
        basis_lo = jnp.take(soap_bases, lo, axis=1)
        basis_hi = jnp.take(soap_bases, hi, axis=1)

        def by_kind(form, value):
            first = jnp.einsum(form, basis_lo, value, precision=highest)
            second = jnp.einsum(form, basis_hi, value, precision=highest)
            return jnp.where(in_lo[None, None, :], first, second)

        turned = by_kind("lij,lci->ljc", clipped)
        new_mats_first = beta_one * mats_first + (1.0 - beta_one) * turned
        new_mats_second = beta_two * mats_second + (1.0 - beta_two) * turned * turned
        heading = (
            new_mats_first
            / (1.0 - beta_one**STEP)
            / (jnp.sqrt(new_mats_second / (1.0 - beta_two**STEP)) + eps_adam)
        )
        direction = by_kind("lij,ljc->lic", heading)
        new_mats = layer_mats - learn_rate * (direction + decay_weight * layer_mats)
        new_tables, new_tables_first, new_tables_second = adam_update(
            vocab_tables, jnp.stack([grad_embed, grad_head]) * factor, tables_first, tables_second
        )
        new_gains, new_gains_first, new_gains_second = adam_update(
            norm_gains, gain_sum * factor, gains_first, gains_second
        )
        return (
            loss_sum,
            mask_count,
            clip_norm,
            new_mats,
            new_mats_first,
            new_mats_second,
            new_bases,
            new_stats,
            new_tables,
            new_tables_first,
            new_tables_second,
            new_gains,
            new_gains_first,
            new_gains_second,
        )

    return shards


def solution(mesh):
    n_dp, n_fs = mesh.shape["dp"], mesh.shape["fsdp"]
    n_x = 2 ** ((n_dp.bit_length() - 1) // 2)
    fine = Mesh(mesh.devices.reshape(n_dp // n_x, n_x, n_fs // 2, 2), ("z", "x", "y", "c"))
    rows, row = P(DATA, None), P(DATA)
    mats, tables = P(None, None, OWNERS), P(None, OWNERS, None)
    return jax.shard_map(
        make_shards(dict(fine.shape)),
        mesh=fine,
        in_specs=(rows, rows, row, rows, mats, mats, mats, P(), P(), tables, tables, tables, P(), P(), P()),
        out_specs=(P(), P(), P(), mats, mats, mats, P(), P(), tables, tables, tables, P(), P(), P()),
        check_vma=False,
    )
```

time: 5440 us -> 2000 us (0.37)
  other arithmetic: 1880 us -> 226 us
  waiting for transfers between devices: 2250 us -> 644 us
  matrix products: 938 us -> 320 us
  starting transfers between devices: 1.13 us -> 325 us
  Pallas kernels: 0 us -> 207 us
  local copies, waits for them, and re-layouts: 261 us -> 173 us
    another operation x38 -> x7, other arithmetic: 1520 us -> 1.52 us  [the longest x26 978 us: renew_basis(): lower_factor = jnp.linalg.cholesky(gram)]
    reduce_scatter x5 -> x2, waiting for transfers between devices: 1040 us -> 39.6 us  [the longest x1 39.5 us: shards(): lax.psum_scatter(nn(grad_logits, head), HEAD_GROUP, scatter_dimension=0,...]
    all_gather x6 -> x5, waiting for transfers between devices: 640 us -> 206 us  [the longest x1 126 us: shards(): lax.all_gather(stats_part, DATA, axis=0, tiled=True)]
    dot_general x54 -> x52, matrix products: 723 us -> 320 us  [the longest x48 285 us: dot(): lax.dot_general(a, b, (dims, ((), ())), precision=precision, preferred_el...]
    unnamed x14 -> x7, waiting for transfers between devices: 342 us -> 0.79 us
    ppermute x0 -> x61, waiting for transfers between devices: none -> 326 us  [moved(): return lax.ppermute(value, DATA, [(int(s), int(d)) for s, d in pairs])]
    ppermute x0 -> x61, starting transfers between devices: none -> 297 us  [moved(): return lax.ppermute(value, DATA, [(int(s), int(d)) for s, d in pairs])]
    psum x1 -> x0, waiting for transfers between devices: 231 us -> none  [shards(): lax.psum((square_part, stat_part, gain_part, loss_part, count_part), ('dp...]
  transfers between devices with their start and end apart: 13 -> 71, of which waited for: 11 -> 25; matrix products, arithmetic and copies ran while one was open for 13% -> 18% of each run, Pallas kernels for 0% -> 5%
where the time goes in v1:
time: 2000 us; the launch traced here: 1990 us
  waiting for transfers between devices  644 us (32%)
  starting transfers between devices  325 us (16%)
  matrix products  320 us (16%)
  other arithmetic  226 us (11%)
  Pallas kernels  207 us (10%)
  local copies, waits for them, and re-layouts  173 us (9%)
  blocking collectives  57.2 us (3%)
  between operations  30.6 us (2%)
    ppermute x61, waiting for transfers between devices, moved(): return lax.ppermute(value, DATA, [(int(s), int(d)) for s, d in pairs])  326 us
    ppermute x61, starting transfers between devices, moved(): return lax.ppermute(value, DATA, [(int(s), int(d)) for s, d in pairs])  297 us
    dot_general x48, matrix products, dot(): lax.dot_general(a, b, (dims, ((), ())), precision=precision, preferred_el...  285 us
    all_gather x1, waiting for transfers between devices, shards(): lax.all_gather(stats_part, DATA, axis=0, tiled=True)  126 us
    pallas_call x1, Pallas kernels, orthogonal_rows(): pl.pallas_call(orthogonal_kernel, out_shape=jax.ShapeDtypeStruct(rows.sha...  82.9 us
    unnamed x321, local copies, waits for them, and re-layouts  77.2 us
    all_to_all x1, waiting for transfers between devices, fetch(): got = lax.all_to_all(sent, OWNERS, 0, 0, tiled=True)  68.8 us
    all_gather x1, waiting for transfers between devices, shards(): lax.all_gather(new_rows, DATA, axis=0, tiled=True).reshape(soap_bases.shape)  63.4 us
  transfers between devices with their start and end apart: 71, of which 25 were waited for; matrix products, arithmetic and copies ran while one was open for 18% of the time, Pallas kernels for 5%

profile of v1, /device:TPU:0, one launch (start us, length us, event | category | flops | bytes accessed | tf_op | source)
XLA Modules:
  0.0 1992.3 jit_solution(1786855658650789942)
XLA Ops:
  52.2 68.8 %all-to-all-done.5 = bf16[32,40,768]{2,1,0:T(8,128)(2,1)S(1)} async-done(((bf16[32,40,768]{2,1,0:T(8,128)(2,1)}), bf16[32,40,768]{2,1,0:T(8,128)(2,1)S(1)}, u32[]{:S(2)}, u32[]{:S(2)}) %all-to-all-start.5) | async-done | bytes 1966112 | tf_op jit(solution)/shard_map/all_to_all | solution.py:572
  160.9 46.2 %attend.2 = (bf16[1024,768]{1,0:T(8,128)(2,1)}, bf16[1024,768]{1,0:T(8,128)(2,1)}, bf16[1024,768]{1,0:T(8,128)(2,1)}, bf16[1024,768]{1,0:T(8,128)(2,1)}, f32[6,2,1024]{2,1,0:T(2,128)}) custom-call(f32[1024,768]{1,0:T(8,128)} %fusion.124.q_ref, f32[1024,1536]{1,0:T(8,128)} %fusion.78.k_ref.v_ref, f32[1024,1536]{1,0:T(8,128)} %fusion.78.k_ref.v_ref, ...), custom_call_target="tpu_custom_call" | custom-call | flops 1000 | bytes 1000 | tf_op jit(solution)/shard_map/attend/pallas_call | solution.py:165
  263.9 15.2 attend.3
  300.5 30.8 %collective-permute-done = bf16[1000,768]{1,0:T(8,128)(2,1)} collective-permute-done((bf16[1000,768]{1,0:T(8,128)(2,1)S(1)}, bf16[1000,768]{1,0:T(8,128)(2,1)}, u32[]{:S(2)}, u32[]{:S(2)}) %collective-permute-start) | collective-permute-done | bytes 1536032 | tf_op jit(solution)/shard_map/ppermute | solution.py:373
  349.1 19.5 collective-permute-done.2
  418.5 22.1 %fusion.281 = (f32[2048]{0:T(1024)S(1)}, f32[2048,4000]{0,1:T(8,128)}) fusion(bf16[2048,768]{1,0:T(8,128)(2,1)} %all-gather.11.cloned.1.call-done, bf16[4000,768]{1,0:T(8,128)(2,1)} %bitcast.475), kind=kOutput, calls=%fused_computation.538 | convolution fusion | flops 12591101952 | bytes 42065920 | tf_op jit(solution)/shard_map/dot_general | solution.py:53
  440.6 18.3 exponential_reduce_fusion
  480.6 20.7 %fusion.282 = f32[2048,768]{1,0:T(8,128)} fusion(bf16[2048,4000]{0,1:T(8,128)(2,1)} %fusion.28, bf16[4000,768]{1,0:T(8,128)(2,1)} %bitcast.476), kind=kOutput, calls=%fused_computation.539 | convolution fusion | flops 12582912000 | bytes 28819456 | tf_op jit(solution)/shard_map/dot_general | solution.py:53
  501.5 19.6 fusion.283
  521.1 39.5 %reduce-scatter.3.cloned.1.call-done = f32[256,768]{1,0:T(8,128)} async-done(((f32[2048,768]{1,0:T(8,128)}), f32[256,768]{1,0:T(8,128)}) %reduce-scatter.3.cloned.1.call-update) | async-done | bytes 786448 | tf_op jit(solution)/shard_map/reduce_scatter | solution.py:666
  577.9 15.8 attend_back.2
  647.7 13.0 fusion.31
  677.1 15.4 bitcast_add_fusion
  727.0 14.3 multiply_reduce_fusion.2
  814.3 47.1 %attend_back.3 = (bf16[1024,768]{1,0:T(8,128)(2,1)}, bf16[1024,768]{1,0:T(8,128)(2,1)}, bf16[1024,768]{1,0:T(8,128)(2,1)}) custom-call(bf16[1024,768]{1,0:T(8,128)(2,1)} %get-tuple-element.478.qs_ref, bf16[1024,768]{1,0:T(8,128)(2,1)} %get-tuple-element.479.k_ref, bf16[1024,768]{1,0:T(8,128)(2,1)} %get-tuple-element.480.v_ref, ...), custom_call_target="tpu_custom_call" | custom-call | flops 1000 | bytes 1000 | tf_op jit(solution)/shard_map/attend_back/pallas_call | solution.py:182
  924.5 18.7 collective-permute-done.14
  946.6 37.5 %collective-permute-done.15 = f32[4,2,144,768]{3,2,1,0:T(8,128)} collective-permute-done((f32[4,2,144,768]{3,2,1,0:T(8,128)S(1)}, f32[4,2,144,768]{3,2,1,0:T(8,128)}, u32[]{:S(2)}, u32[]{:S(2)}) %collective-permute-start.15) | collective-permute-done | bytes 3538976 | tf_op jit(solution)/shard_map/ppermute | solution.py:373
  985.0 37.1 %collective-permute-done.13 = f32[4,144,768]{2,1,0:T(8,128)} collective-permute-done((f32[4,144,768]{2,1,0:T(8,128)}, f32[4,144,768]{2,1,0:T(8,128)}, u32[]{:S(2)}, u32[]{:S(2)}) %collective-permute-start.13) | collective-permute-done | bytes 1769504 | tf_op jit(solution)/shard_map/ppermute | solution.py:373
  1102.0 30.9 %collective-permute-done.23 = f32[4,144,768]{2,1,0:T(8,128)} collective-permute-done((f32[4,144,768]{2,1,0:T(8,128)}, f32[4,144,768]{2,1,0:T(8,128)}, u32[]{:S(2)}, u32[]{:S(2)}) %collective-permute-start.23) | collective-permute-done | bytes 1769504 | tf_op jit(solution)/shard_map/ppermute | solution.py:373
  1207.3 17.0 all-to-all-start.6
  1239.1 72.6 %collective-permute-done.34 = f32[288,768]{1,0:T(8,128)S(1)} collective-permute-done((f32[288,768]{1,0:T(8,128)S(1)}, f32[288,768]{1,0:T(8,128)S(1)}, u32[]{:S(2)}, u32[]{:S(2)}) %collective-permute-start.34) | collective-permute-done | bytes 884768 | tf_op jit(solution)/shard_map/ppermute | solution.py:373
  1313.2 17.2 collective-permute-done.36
  1338.8 21.5 %collective-permute-start.45 = (f32[288,768]{1,0:T(8,128)S(1)}, f32[288,768]{1,0:T(8,128)}, u32[]{:S(2)}, u32[]{:S(2)}) collective-permute-start(f32[288,768]{1,0:T(8,128)S(1)} %get-tuple-element.588), channel_id=1, source_target_pairs={{10,2},{11,3},{14,6},{15,7},{18,10},{19,11},{22,14},{23,15},{26,18... | collective-permute-start | bytes 2654216 | tf_op jit(solution)/shard_map/ppermute | solution.py:373
  1373.7 22.1 %collective-permute-start.50 = (f32[288,768]{1,0:T(8,128)}, f32[288,768]{1,0:T(8,128)}, u32[]{:S(2)}, u32[]{:S(2)}) collective-permute-start(f32[288,768]{1,0:T(8,128)} %fusion.192), channel_id=1, source_target_pairs={{0,16},{1,20},{3,28},{5,21},{8,17},{9,22},{10,26},{11,29},{13,24},... | collective-permute-start | bytes 2654216 | tf_op jit(solution)/shard_map/ppermute | solution.py:373
  1417.4 57.4 %collective-permute-start.54 = (f32[288,768]{1,0:T(8,128)}, f32[288,768]{1,0:T(8,128)S(1)}, u32[]{:S(2)}, u32[]{:S(2)}) collective-permute-start(f32[288,768]{1,0:T(8,128)} %fusion.145), channel_id=1, source_target_pairs={{0,0},{1,4},{3,12},{5,5},{8,1},{9,6},{10,10},{11,13},{13,8},{16,2}... | collective-permute-start | bytes 2654216 | tf_op jit(solution)/shard_map/ppermute | solution.py:373
  1492.3 34.7 %collective-permute-start.58 = (f32[384,768]{1,0:T(8,128)S(1)}, f32[384,768]{1,0:T(8,128)S(1)}, u32[]{:S(2)}, u32[]{:S(2)}) collective-permute-start(f32[384,768]{1,0:T(8,128)S(1)} %dynamic-slice_bitcast_fusion.12), channel_id=1, source_target_pairs={{0,1},{1,0},{2,3},{3,2},{4,5},{5,4},{6,7},{7,6},{8,9},{9,8},{10,11... | collective-permute-start | bytes 3538952 | tf_op jit(solution)/shard_map/ppermute | solution.py:373
  1546.1 13.2 collective-permute-done.59
  1568.9 38.9 %all-gather.3 = f32[256,768]{1,0:T(8,128)S(1)} all-gather(f32[8,768]{1,0:T(8,128)S(1)} %concatenate.116), channel_id=5, replica_groups=mesh['z'=4,'x'=2,'y'=2,'c'=2] {'z','x','y','c'}, dimensions={0}, use_global_device_ids=true | all-gather | bytes 811008 | tf_op jit(solution)/shard_map/all_gather | solution.py:741
  1627.5 82.9 %orthogonal_rows.1 = f32[192,768]{1,0:T(8,128)} custom-call(f32[768,768]{1,0:T(8,128)S(1)} %fusion.288.gram_ref, f32[192,768]{1,0:T(8,128)S(1)} %constant_dynamic-slice_fusion.rows_ref), custom_call_target="tpu_custom_call" | custom-call | flops 1000 | bytes 1000 | tf_op jit(solution)/shard_map/orthogonal_rows/pallas_call | solution.py:253
  1769.2 63.4 %all-gather.13.cloned.1.call-done = f32[6144,768]{1,0:T(8,128)} async-done(((f32[192,768]{1,0:T(8,128)}), f32[6144,768]{1,0:T(8,128)}) %all-gather.13.cloned.1.call-update) | async-done | bytes 18874384 | tf_op jit(solution)/shard_map/all_gather | solution.py:765
  1832.7 126.2 %all-gather.15.cloned.1.call-done = f32[6144,768]{1,0:T(8,128)} async-done(((f32[192,768]{1,0:T(8,128)}), f32[6144,768]{1,0:T(8,128)}) %all-gather.15.cloned.1.call-update) | async-done | bytes 18874384 | tf_op jit(solution)/shard_map/all_gather | solution.py:762
  1958.9 13.7 copy.168
  (678 shorter events, 850.2 us)
Async XLA Ops:
  7.2 141.5 %all-gather.17.cloned.1.call-start = ((), (), s32[]{:S(2)}) async-start(), calls=%async_computation.14 | async-start | bytes 14598144 | tf_op jit(solution)/shard_map/all_gather | solution.py:555
  9.8 244.0 %all-gather.19.cloned.1.call-start = ((), (), s32[]{:S(2)}) async-start(), calls=%async_computation.15 | async-start | bytes 14598144 | tf_op jit(solution)/shard_map/all_gather | solution.py:637
  38.3 82.7 %all-to-all-start.5 = ((bf16[32,40,768]{2,1,0:T(8,128)(2,1)}), bf16[32,40,768]{2,1,0:T(8,128)(2,1)S(1)}, u32[]{:S(2)}, u32[]{:S(2)}) async-start(bf16[32,40,768]{2,1,0:T(8,128)(2,1)} %bitcast.482), calls=%async_computation.5 | async-start | bytes 3932160 | tf_op jit(solution)/shard_map/all_to_all | solution.py:572
  41.9 376.6 %all-gather.11.cloned.1.call-start = ((), (), s32[]{:S(2)}) async-start(), calls=%async_computation.9 | async-start | bytes 3538944 | tf_op jit(solution)/shard_map/all_gather | solution.py:644
  292.8 267.9 %reduce-scatter.3.cloned.1.call-start = ((), (), s32[]{:S(2)}) async-start(), calls=%async_computation.10 | async-start | bytes 7077888 | tf_op jit(solution)/shard_map/reduce_scatter | solution.py:666
  501.4 360.1 %reduce-scatter.5.cloned.1.call-start = ((), (), s32[]{:S(2)}) async-start(), calls=%async_computation.11 | async-start | bytes 15360000 | tf_op jit(solution)/shard_map/reduce_scatter | solution.py:669
  772.7 88.8 %collective-permute-start.9 = (f32[2,4,144,768]{3,2,1,0:T(8,128)}, f32[2,4,144,768]{3,2,1,0:T(8,128)}, u32[]{:S(2)}, u32[]{:S(2)}) collective-permute-start(f32[2,4,144,768]{3,2,1,0:T(8,128)} %dynamic-slice_bitcast_fusion.3), channel_id=1, source_target_pairs={{0,4},{1,5},{2,6},{3,7},{4,0},{5,1},{6,2},{7,3},{8,12},{9,13},{10,... | collective-permute-start | bytes 10616840 | tf_op jit(solution)/shard_map/ppermute | solution.py:373
  774.6 86.9 %collective-permute-start.10 = (f32[4,2,144,768]{3,2,1,0:T(8,128)}, f32[4,2,144,768]{3,2,1,0:T(8,128)}, u32[]{:S(2)}, u32[]{:S(2)}) collective-permute-start(f32[4,2,144,768]{3,2,1,0:T(8,128)} %dynamic-slice_bitcast_fusion.2), channel_id=1, source_target_pairs={{0,2},{1,3},{2,0},{3,1},{4,6},{5,7},{6,4},{7,5},{8,10},{9,11},{10,... | collective-permute-start | bytes 10616840 | tf_op jit(solution)/shard_map/ppermute | solution.py:373
  899.3 122.8 %collective-permute-start.11 = (f32[4,2,288,768]{3,2,1,0:T(8,128)}, f32[4,2,288,768]{3,2,1,0:T(8,128)}, u32[]{:S(2)}, u32[]{:S(2)}) collective-permute-start(f32[4,2,288,768]{3,2,1,0:T(8,128)} %bitcast.65), channel_id=1, source_target_pairs={{1,0},{3,2},{5,4},{7,6},{9,8},{11,10},{13,12},{15,14},{17,16},{19,... | collective-permute-start | bytes 21233672 | tf_op jit(solution)/shard_map/ppermute | solution.py:373
  906.3 77.7 %collective-permute-start.15 = (f32[4,2,144,768]{3,2,1,0:T(8,128)S(1)}, f32[4,2,144,768]{3,2,1,0:T(8,128)}, u32[]{:S(2)}, u32[]{:S(2)}) collective-permute-start(f32[4,2,144,768]{3,2,1,0:T(8,128)S(1)} %copy-done.48), channel_id=1, source_target_pairs={{0,2},{1,3},{4,6},{5,7},{8,10},{9,11},{12,14},{13,15},{16,18},{17,... | collective-permute-start | bytes 10616840 | tf_op jit(solution)/shard_map/ppermute | solution.py:373
  911.5 72.6 %collective-permute-start.17 = (f32[4,2,144,768]{3,2,1,0:T(8,128)}, f32[4,2,144,768]{3,2,1,0:T(8,128)}, u32[]{:S(2)}, u32[]{:S(2)}) collective-permute-start(f32[4,2,144,768]{3,2,1,0:T(8,128)} %get-tuple-element.531), channel_id=1, source_target_pairs={{3,1},{7,5},{11,9},{15,13},{19,17},{23,21},{27,25},{31,29}} | collective-permute-start | bytes 10616840 | tf_op jit(solution)/shard_map/ppermute | solution.py:373
  943.2 41.9 %collective-permute-start.12 = (f32[4,144,768]{2,1,0:T(8,128)}, f32[4,144,768]{2,1,0:T(8,128)}, u32[]{:S(2)}, u32[]{:S(2)}) collective-permute-start(f32[4,144,768]{2,1,0:T(8,128)} %dynamic-slice_bitcast_fusion.9), channel_id=1, source_target_pairs={{0,4},{1,5},{2,6},{3,7},{4,0},{5,1},{6,2},{7,3},{8,12},{9,13},{10,... | collective-permute-start | bytes 5308424 | tf_op jit(solution)/shard_map/ppermute | solution.py:373
  945.1 77.0 %collective-permute-start.13 = (f32[4,144,768]{2,1,0:T(8,128)}, f32[4,144,768]{2,1,0:T(8,128)}, u32[]{:S(2)}, u32[]{:S(2)}) collective-permute-start(f32[4,144,768]{2,1,0:T(8,128)} %dynamic-slice_bitcast_fusion.8), channel_id=1, source_target_pairs={{0,2},{1,3},{2,0},{3,1},{4,6},{5,7},{6,4},{7,5},{8,10},{9,11},{10,... | collective-permute-start | bytes 5308424 | tf_op jit(solution)/shard_map/ppermute | solution.py:373
  1058.6 41.2 %collective-permute-start.18 = (f32[4,144,768]{2,1,0:T(8,128)S(1)}, f32[4,144,768]{2,1,0:T(8,128)}, u32[]{:S(2)}, u32[]{:S(2)}) collective-permute-start(f32[4,144,768]{2,1,0:T(8,128)S(1)} %dynamic-slice_bitcast_fusion.7), channel_id=1, source_target_pairs={{0,4},{2,6},{4,0},{6,2},{8,12},{10,14},{12,8},{14,10},{16,20},{18,... | collective-permute-start | bytes 5308424 | tf_op jit(solution)/shard_map/ppermute | solution.py:373
  1067.2 65.7 %collective-permute-start.19 = (f32[4,2,144,768]{3,2,1,0:T(8,128)}, f32[4,2,144,768]{3,2,1,0:T(8,128)}, u32[]{:S(2)}, u32[]{:S(2)}) collective-permute-start(f32[4,2,144,768]{3,2,1,0:T(8,128)} %get-tuple-element.540), channel_id=1, source_target_pairs={{2,0},{6,4},{10,8},{14,12},{18,16},{22,20},{26,24},{30,28}} | collective-permute-start | bytes 10616840 | tf_op jit(solution)/shard_map/ppermute | solution.py:373
  1091.5 41.5 %collective-permute-start.23 = (f32[4,144,768]{2,1,0:T(8,128)}, f32[4,144,768]{2,1,0:T(8,128)}, u32[]{:S(2)}, u32[]{:S(2)}) collective-permute-start(f32[4,144,768]{2,1,0:T(8,128)} %bitcast_add_fusion.11), channel_id=1, source_target_pairs={{0,2},{1,3},{4,6},{5,7},{8,10},{9,11},{12,14},{13,15},{16,18},{17,... | collective-permute-start | bytes 5308424 | tf_op jit(solution)/shard_map/ppermute | solution.py:373
  1207.3 269.0 %all-to-all-start.6 = ((f32[32,40,768]{2,1,0:T(8,128)}), f32[32,40,768]{2,1,0:T(8,128)}, u32[]{:S(2)}, u32[]{:S(2)}) async-start(f32[32,40,768]{2,1,0:T(8,128)} %bitcast.478), calls=%async_computation.8 | async-start | bytes 7864320 | tf_op jit(solution)/shard_map/all_to_all | solution.py:579
  1224.3 608.3 %all-gather.13.cloned.1.call-start = ((), (), s32[]{:S(2)}) async-start(), calls=%async_computation.12 | async-start | bytes 19464192 | tf_op jit(solution)/shard_map/all_gather | solution.py:765
  1230.2 81.5 %collective-permute-start.34 = (f32[288,768]{1,0:T(8,128)S(1)}, f32[288,768]{1,0:T(8,128)S(1)}, u32[]{:S(2)}, u32[]{:S(2)}) collective-permute-start(f32[288,768]{1,0:T(8,128)S(1)} %get-tuple-element.571), channel_id=1, source_target_pairs={{0,8},{4,12}} | collective-permute-start | bytes 2654216 | tf_op jit(solution)/shard_map/ppermute | solution.py:373
  1234.1 78.3 %collective-permute-start.35 = (f32[288,768]{1,0:T(8,128)S(1)}, f32[288,768]{1,0:T(8,128)S(1)}, u32[]{:S(2)}, u32[]{:S(2)}) collective-permute-start(f32[288,768]{1,0:T(8,128)S(1)} %get-tuple-element.572), channel_id=1, source_target_pairs={{24,16},{28,20}} | collective-permute-start | bytes 2654216 | tf_op jit(solution)/shard_map/ppermute | solution.py:373
  1234.9 95.5 %collective-permute-start.36 = (f32[288,768]{1,0:T(8,128)S(1)}, f32[288,768]{1,0:T(8,128)}, u32[]{:S(2)}, u32[]{:S(2)}) collective-permute-start(f32[288,768]{1,0:T(8,128)S(1)} %get-tuple-element.573), channel_id=1, source_target_pairs={{0,8},{1,9},{2,10},{3,11},{4,12},{5,13},{6,14},{7,15},{8,16},{9,17... | collective-permute-start | bytes 2654216 | tf_op jit(solution)/shard_map/ppermute | solution.py:373
  1237.1 94.0 %collective-permute-start.37 = (f32[288,768]{1,0:T(8,128)S(1)}, f32[288,768]{1,0:T(8,128)}, u32[]{:S(2)}, u32[]{:S(2)}) collective-permute-start(f32[288,768]{1,0:T(8,128)S(1)} %get-tuple-element.574), channel_id=1, source_target_pairs={{8,0},{9,1},{10,2},{11,3},{12,4},{13,5},{14,6},{15,7},{16,8},{17,9... | collective-permute-start | bytes 2654216 | tf_op jit(solution)/shard_map/ppermute | solution.py:373
  1238.4 92.7 %collective-permute-start.38 = (f32[288,768]{1,0:T(8,128)S(1)}, f32[288,768]{1,0:T(8,128)S(1)}, u32[]{:S(2)}, u32[]{:S(2)}) collective-permute-start(f32[288,768]{1,0:T(8,128)S(1)} %copy-done.79), channel_id=1, source_target_pairs={{2,10},{3,11},{6,14},{7,15},{10,18},{11,19},{14,22},{15,23}} | collective-permute-start | bytes 2654216 | tf_op jit(solution)/shard_map/ppermute | solution.py:373
  1364.9 43.7 %collective-permute-start.48 = (f32[288,768]{1,0:T(8,128)}, f32[288,768]{1,0:T(8,128)}, u32[]{:S(2)}, u32[]{:S(2)}) collective-permute-start(f32[288,768]{1,0:T(8,128)} %get-tuple-element.597), channel_id=1, source_target_pairs={{0,8},{4,12},{8,16},{12,20},{16,24},{20,28}} | collective-permute-start | bytes 2654216 | tf_op jit(solution)/shard_map/ppermute | solution.py:373
  1373.7 41.7 %collective-permute-start.50 = (f32[288,768]{1,0:T(8,128)}, f32[288,768]{1,0:T(8,128)}, u32[]{:S(2)}, u32[]{:S(2)}) collective-permute-start(f32[288,768]{1,0:T(8,128)} %fusion.192), channel_id=1, source_target_pairs={{0,16},{1,20},{3,28},{5,21},{8,17},{9,22},{10,26},{11,29},{13,24},... | collective-permute-start | bytes 2654216 | tf_op jit(solution)/shard_map/ppermute | solution.py:373
  1408.6 67.7 %collective-permute-start.53 = (f32[288,768]{1,0:T(8,128)}, f32[288,768]{1,0:T(8,128)}, u32[]{:S(2)}, u32[]{:S(2)}) collective-permute-start(f32[288,768]{1,0:T(8,128)} %fusion.192), channel_id=1, source_target_pairs={{6,25},{21,24},{22,26}} | collective-permute-start | bytes 2654216 | tf_op jit(solution)/shard_map/ppermute | solution.py:373
  1414.6 61.7 %collective-permute-start.57 = (f32[288,768]{1,0:T(8,128)}, f32[288,768]{1,0:T(8,128)S(1)}, u32[]{:S(2)}, u32[]{:S(2)}) collective-permute-start(f32[288,768]{1,0:T(8,128)} %fusion.145), channel_id=1, source_target_pairs={{6,9},{21,8},{22,10}} | collective-permute-start | bytes 2654216 | tf_op jit(solution)/shard_map/ppermute | solution.py:373
  1415.4 62.3 %collective-permute-start.56 = (f32[288,768]{1,0:T(8,128)}, f32[288,768]{1,0:T(8,128)S(1)}, u32[]{:S(2)}, u32[]{:S(2)}) collective-permute-start(f32[288,768]{1,0:T(8,128)} %fusion.145), channel_id=1, source_target_pairs={{2,9},{3,11},{17,8},{18,10}} | collective-permute-start | bytes 2654216 | tf_op jit(solution)/shard_map/ppermute | solution.py:373
  1416.1 62.9 %collective-permute-start.55 = (f32[288,768]{1,0:T(8,128)}, f32[288,768]{1,0:T(8,128)S(1)}, u32[]{:S(2)}, u32[]{:S(2)}) collective-permute-start(f32[288,768]{1,0:T(8,128)} %fusion.145), channel_id=1, source_target_pairs={{4,0},{7,12},{9,8},{12,1},{14,10},{15,13},{20,2},{23,14},{28,3},{2... | collective-permute-start | bytes 2654216 | tf_op jit(solution)/shard_map/ppermute | solution.py:373
  1417.4 62.9 %collective-permute-start.54 = (f32[288,768]{1,0:T(8,128)}, f32[288,768]{1,0:T(8,128)S(1)}, u32[]{:S(2)}, u32[]{:S(2)}) collective-permute-start(f32[288,768]{1,0:T(8,128)} %fusion.145), channel_id=1, source_target_pairs={{0,0},{1,4},{3,12},{5,5},{8,1},{9,6},{10,10},{11,13},{13,8},{16,2}... | collective-permute-start | bytes 2654216 | tf_op jit(solution)/shard_map/ppermute | solution.py:373
  1562.0 49.7 %collective-permute-start.60 = (f32[384,768]{1,0:T(8,128)}, f32[384,768]{1,0:T(8,128)}, u32[]{:S(2)}, u32[]{:S(2)}) collective-permute-start(f32[384,768]{1,0:T(8,128)} %add.817), channel_id=1, source_target_pairs={{0,1},{1,0},{2,3},{3,2},{4,5},{5,4},{6,7},{7,6},{8,9},{9,8},{10,11... | collective-permute-start | bytes 3538952 | tf_op jit(solution)/shard_map/ppermute | solution.py:373
  1710.4 248.5 %all-gather.15.cloned.1.call-start = ((), (), s32[]{:S(2)}) async-start(), calls=%async_computation.13 | async-start | bytes 19464192 | tf_op jit(solution)/shard_map/all_gather | solution.py:762
  (200 other events, 4131.3 us)
Sparse Core Ops, SparseCore 0:
  11.6 137.0 all-gather.16
  152.2 101.4 all-gather.18
  292.9 30.4 all-gather.10
  501.5 59.1 reduce-scatter.2
  645.9 207.5 reduce-scatter.4
  1710.5 122.0 all-gather.12
  1836.0 122.8 all-gather.14

commit v2 on v1

--- a/solution.py
+++ b/solution.py
@@ -1,3 +1,5 @@
+import functools
+
 import jax
 import jax.numpy as jnp
 import numpy as np
@@ -46,7 +48,7 @@
 DATA = ("z", "x", "y", "c")
 DP = ("z", "x")
 FS = ("y", "c")
-HEAD_GROUP = ("x", "y", "c")
+HEAD_GROUP = ("z", "y", "c")
 
 
 def dot(a, b, dims, precision=None):
@@ -230,34 +232,33 @@
     return jnp.concatenate(right, axis=0) * lax.rsqrt(pivots)
 
 
-def orthogonal_kernel(gram_ref, rows_ref, out_ref, rest):
-    rest[...] = gram_ref[...]
+def orthogonal_kernel(steps, gram_ref, rows_ref, out_ref, rest_ref):
+    rest_ref[...] = gram_ref[...]
     out_ref[...] = rows_ref[...]
-    lane = lax.broadcasted_iota(jnp.int32, (1, D), 1)
+    lane = lax.broadcasted_iota(jnp.int32, (1, gram_ref.shape[0]), 1)
 
     def body(b, _):
         start = pl.multiple_of(b * STEPS, STEPS)
         here = pl.ds(start, STEPS)
-        inverse = inverse_factor(rest[here, here])
-        upper = jnp.where(lane >= start + STEPS, fm(inverse, rest[here, :], 1, 0), 0.0)
+        inverse = inverse_factor(rest_ref[here, here])
+        upper = jnp.where(lane >= start + STEPS, fm(inverse, rest_ref[here, :], 1, 0), 0.0)
         done = fm(out_ref[:, here], inverse, 1, 1)
         out_ref[...] -= fm(done, upper, 1, 0)
         out_ref[:, here] = done
-        rest[...] -= fm(upper, upper, 0, 0)
+        rest_ref[...] -= fm(upper, upper, 0, 0)
         return 0
 
-    lax.fori_loop(0, D // STEPS, body, 0)
-
-
-def orthogonal_rows(gram, rows):
+    lax.fori_loop(0, steps, body, 0)
+
+
+def orthogonal_rows(gram, rows, steps):
     return pl.pallas_call(
-        orthogonal_kernel,
-        out_shape=jax.ShapeDtypeStruct(rows.shape, f32),
+        functools.partial(orthogonal_kernel, steps),
+        out_shape=[jax.ShapeDtypeStruct(rows.shape, f32), jax.ShapeDtypeStruct(gram.shape, f32)],
         in_specs=[pl.BlockSpec(memory_space=pltpu.VMEM)] * 2,
-        out_specs=pl.BlockSpec(memory_space=pltpu.VMEM),
-        scratch_shapes=[pltpu.VMEM((D, D), f32)],
+        out_specs=[pl.BlockSpec(memory_space=pltpu.VMEM)] * 2,
         compiler_params=pltpu.CompilerParams(vmem_limit_bytes=40 * 2**20),
-        cost_estimate=LIGHT,
+        cost_estimate=pl.CostEstimate(flops=10**11, bytes_accessed=8 * D * D, transcendentals=0),
         name="orthogonal_rows",
     )(gram, rows)
 
@@ -301,7 +302,7 @@
     return result, saved
 
 
-def ffn_back(grad_out, saved, weights, gains, between):
+def ffn_back(grad_out, saved, weights, gains, cut, between):
     _, _, w_gu, w_down = parts_of(weights)
     _, _, _, _, attended, middle, normed_ffn, gate_up, activated = saved
     grad_low = grad_out.astype(bf16)
@@ -310,7 +311,7 @@
     _, pull_act = jax.vjp(silu_up, gate_up[:, :FF], gate_up[:, FF:])
     grad_gate_up = jnp.concatenate(pull_act(grad_act), axis=1).astype(bf16)
     grad_gate_up, grad_down = between((grad_gate_up, grad_down))
-    grad_gu = tn(grad_gate_up, normed_ffn)
+    grad_gu = [tn(grad_gate_up[:, :cut], normed_ffn), tn(grad_gate_up[:, cut:], normed_ffn)]
     _, pull_ffn = jax.vjp(rms_scale, middle, gains[1])
     grad_middle, grad_gain = pull_ffn(nn(grad_gate_up, w_gu))
     grad_middle = grad_out + grad_middle
@@ -340,12 +341,6 @@
     return grad_middle + grad_residual, grad_qkv, grad_gain
 
 
-def renew_rows(statistic, basis, start, rows):
-    product = nn(statistic, basis, highest)
-    gram = tn(product, product, highest)
-    return orthogonal_rows(gram, lax.dynamic_slice_in_dim(product, start, rows))
-
-
 def make_shards(sizes):
     n_z, n_x, n_y, n_c = (sizes[a] for a in ("z", "x", "y", "c"))
     n_dp, n_fs = n_z * n_x, n_y * n_c
@@ -372,18 +367,6 @@
                 pairs.append((np.ravel_multi_index(source, shape), np.ravel_multi_index(dest, shape)))
         return lax.ppermute(value, DATA, [(int(s), int(d)) for s, d in pairs])
 
-    def line_gather(own):
-        if not paired:
-            return lax.all_gather(own, "z", axis=0, tiled=True)
-        at = lax.axis_index("z")
-        places = jnp.zeros((2 * n_z - 1,) + own.shape, own.dtype).at[n_z - 1].set(own)
-        up, down = own, own
-        for k in range(1, n_z):
-            up = moved(up, lambda z, x, y, c: (z + 1, x, y, c) if z + 1 < n_z else None)
-            down = moved(down, lambda z, x, y, c: (z - 1, x, y, c) if z > 0 else None)
-            places = places.at[n_z - 1 - k].set(up).at[n_z - 1 + k].set(down)
-        return lax.dynamic_slice_in_dim(places, n_z - 1 - at, n_z, axis=0).reshape(-1, D)
-
     def take(value, axis, at):
         return lax.dynamic_index_in_dim(value, at, axis, keepdims=False)
 
@@ -399,55 +382,25 @@
             )
         return value[at] + up + down
 
-    def two_ways(value, cross_y, inside):
-        half = value.shape[-2] // 2
-        first, second = value[..., :half, :], value[..., half:, :]
-        x = lax.axis_index("x")
-        x_at = -3
-        sent_x, sent_y = yield (
-            (take(first, x_at, 1 - x), lambda z, x, y, c: (z, 1 - x, y, c) if inside(None, c) else None),
-            cross_y(second),
-        )
-        first = take(first, x_at, x) + sent_x
-        second = cross_y(second, sent_y)
-        sent_x, sent_y = yield (
-            (take(second, x_at, 1 - x), lambda z, x, y, c: (z, 1 - x, y, c) if inside(y, c) else None),
-            cross_y(first),
-        )
-        first = cross_y(first, sent_y)
-        second = take(second, x_at, x) + sent_x
-        return (yield from z_line(jnp.concatenate([first, second], axis=-2), inside))
-
     def sum_all(value):
-        c, y = lax.axis_index("c"), lax.axis_index("y")
+        c, y, x = lax.axis_index("c"), lax.axis_index("y"), lax.axis_index("x")
+        rows = value.shape[-2] // 2
+
+        def by_x(z, x, y, c):
+            return z, 1 - x, y, c
+
+        def by_y(z, x, y, c):
+            return z, x, 1 - y, c
+
+        kept = take(value, 1, c)
         (sent,) = yield ((take(value, 1, 1 - c), lambda z, x, y, c: (z, x, y, 1 - c)),)
-        value = take(value, 1, c) + sent
-
-        def cross_y(part, sent=None):
-            if sent is None:
-                return take(part, 0, 1 - y), lambda z, x, y, c: (z, x, 1 - y, c)
-            return take(part, 0, y) + sent
-
-        return (yield from two_ways(value, cross_y, lambda y, c: True))
-
-    def sum_at(value, y_at, c_at=None):
-        c = lax.axis_index("c")
-        if c_at is None:
-            request = value[1 - c], lambda z, x, y, c: (z, x, y, 1 - c)
-        else:
-            request = value, lambda z, x, y, c: (z, x, y, c_at) if c != c_at else None
-        (sent,) = yield (request,)
-        value = (value[c] if c_at is None else value) + sent
-
-        def inside(y, c):
-            return (y is None or y == y_at) and (c_at is None or c == c_at)
-
-        def cross_y(part, sent=None):
-            if sent is None:
-                return part, lambda z, x, y, c: (z, x, y_at, c) if y != y_at and inside(None, c) else None
-            return part + sent
-
-        return (yield from two_ways(value, cross_y, inside))
+        first = kept[..., :rows, :] + sent[..., :rows, :]
+        second = kept[..., rows:, :] + sent[..., rows:, :]
+        sent_x, sent_y = yield ((take(first, 2, 1 - x), by_x), (take(second, 0, 1 - y), by_y))
+        first, second = take(first, 2, x) + sent_x, take(second, 0, y) + sent_y
+        sent_y, sent_x = yield ((take(first, 0, 1 - y), by_y), (take(second, 1, 1 - x), by_x))
+        first, second = take(first, 0, y) + sent_y, take(second, 1, x) + sent_x
+        return (yield from z_line(jnp.concatenate([first, second], axis=-2), lambda y, c: True))
 
     class Lane:
         def __init__(self, steps):
@@ -475,44 +428,24 @@
             lane.land(each)
         return start(value, *lanes)
 
-    def stat_routes():
-        rounds, taken = [], []
-        for kind in range(KINDS):
-            blocks = range(BOUNDS[kind] // cols, -(-BOUNDS[kind + 1] // cols))
-            for share, part in enumerate(np.array_split(np.array(blocks), sharing)):
-                for block in part:
-                    r = 0
-                    while r < len(rounds) and (block in taken[r] or (kind, share) in rounds[r].values()):
-                        r += 1
-                    if r == len(rounds):
-                        rounds.append({})
-                        taken.append(set())
-                    rounds[r][int(block)] = (kind, share)
-                    taken[r].add(block)
-        masks = np.zeros((KINDS, sharing, len(rounds), cols), np.float32)
-        for r, each in enumerate(rounds):
-            for block, (kind, share) in each.items():
-                masks[kind, share, r] = kind_of[block * cols : (block + 1) * cols] == kind
-        return rounds, masks
-
-    def gather_stat(own, layer_at):
-        rounds, _ = stat_routes()
-        received = []
-        for each in rounds:
-
-            def target(z, x, y, c, each=each):
-                found = each.get((y * n_c + c) * n_dp + z * n_x + x)
-                if found is None:
-                    return None
-                kind, share = found
-                dp = layer_at * KINDS + kind
-                return dp // n_x, dp % n_x, share // n_c, share % n_c
-
-            received.append(moved(own, target))
-        return received
-
-    def share_stat(pieces, mask):
-        columns = jnp.concatenate([piece * mask[r][:, None] for r, piece in enumerate(pieces)], axis=0)
+    half = cols // 2
+    has = [[(kind_of.reshape(n_fs, n_dp, cols) == kind)[f].any(axis=1) for f in range(n_fs)] for kind in range(KINDS)]
+    merges = [n_fs == 4 and not any((has[k][y] & has[k][2 + y]).any() for y in range(2)) for k in range(KINDS)]
+    work_axes = ("y", "z", "x", "c")
+
+    def to_work(own):
+        y, c = lax.axis_index("y"), lax.axis_index("c")
+        pieces = own.reshape(1, 2, half, D) * (jnp.arange(2)[:, None, None, None] == c)
+        got = lax.all_to_all(pieces.reshape(-1, D), FS, 0, 0, tiled=True).reshape(2, 2, half, D)
+        return take(got, 1, y).reshape(-1, D)
+
+    def from_work(work):
+        y, c = lax.axis_index("y"), lax.axis_index("c")
+        pieces = work.reshape(2, 1, half, D) * (jnp.arange(2)[None, :, None, None] == y)
+        got = lax.all_to_all(pieces.reshape(-1, D), FS, 0, 0, tiled=True).reshape(2, 2, half, D)
+        return take(got, 0, c).reshape(-1, D)
+
+    def share_stat(columns):
         part = tn(columns, columns, highest)
         c = lax.axis_index("c")
         halves = part.reshape(2, D // 2, D)
@@ -632,29 +565,37 @@
         slots = (pick, picked(doc)[None, :], pair_tables(picked(position)))
 
         group_codes = lax.all_gather(jnp.stack([targets, code]), HEAD_GROUP, axis=1, tiled=True)
+        residual, group_codes = lax.optimization_barrier((residual, group_codes))
         group_targets, group_codes = group_codes[0], group_codes[1]
 
         mats_1 = lax.all_gather(work_mats[1], OWNERS, axis=0, tiled=True)
-        head = line_gather(work_tables[1])
-
         residual, saved_0 = layer_forward(residual, None, mats_0, norm_gains[0:2], docs, tables)
+        if paired:
+            x = lax.axis_index("x")
+            other = moved(work_tables[1], lambda z, x, y, c: (z, 1 - x, y, c))
+            residual, other = lax.optimization_barrier((residual, other))
+            head = jnp.concatenate([jnp.where(x == 0, work_tables[1], other), jnp.where(x == 0, other, work_tables[1])], 0)
+        else:
+            head = lax.all_gather(work_tables[1], "x", axis=0, tiled=True)
         final, saved_1 = layer_forward(residual, slots, mats_1, norm_gains[2:4], docs, tables)
 
         chosen_full, pull_final = jax.vjp(rms_scale, final, norm_gains[2 * LAYERS])
         states = lax.all_gather(chosen_full.astype(bf16), HEAD_GROUP, axis=0, tiled=True)
         logits = nt(states, head)
-        base_shard = lax.axis_index(FS) * n_dp + lax.axis_index("x")
-        vocab_ids = (
-            (base_shard + jnp.arange(n_z, dtype=jnp.int32) * n_x)[:, None] * per + row_ids[None, :]
-        ).reshape(-1)
+        base_shard = lax.axis_index(FS) * n_dp + lax.axis_index("z") * n_x
+        vocab_ids = base_shard * per + jnp.arange(n_x * per, dtype=jnp.int32)
         onehot = vocab_ids[None, :] == group_targets[:, None]
         top = jnp.max(logits, axis=1)
         total = jnp.sum(jnp.exp(logits - top[:, None]), axis=1)
         hit_logit = jnp.sum(jnp.where(onehot, logits, 0.0), axis=1)
-        each = lax.all_gather(jnp.stack([top, total, hit_logit]), HEAD_GROUP, axis=0)
-        top_all = jnp.max(each[:, 0], axis=0)
-        log_total = top_all + jnp.log(jnp.sum(each[:, 1] * jnp.exp(each[:, 0] - top_all), axis=0))
-        target_logit = jnp.sum(each[:, 2], axis=0)
+        parts = jnp.stack([top, total, hit_logit])
+        for axes in (FS, "z"):
+            each = lax.all_gather(parts, axes, axis=0)
+            top = jnp.max(each[:, 0], axis=0)
+            parts = jnp.stack(
+                [top, jnp.sum(each[:, 1] * jnp.exp(each[:, 0] - top), axis=0), jnp.sum(each[:, 2], axis=0)]
+            )
+        log_total, target_logit = parts[0] + jnp.log(parts[1]), parts[2]
         weight = jnp.where(group_codes > 0, BINS / jnp.maximum(group_codes, 1).astype(f32), 0.0)
         own_start = lax.axis_index(HEAD_GROUP) * SLOTS
         loss_part = jnp.sum(
@@ -666,67 +607,65 @@
         grad_states = lax.psum_scatter(nn(grad_logits, head), HEAD_GROUP, scatter_dimension=0, tiled=True)
         head_part = tn(grad_logits, states)
         grad_states, head_part = lax.optimization_barrier((grad_states, head_part))
-        grad_head = lax.psum_scatter(head_part, "z", scatter_dimension=0, tiled=True)
+        if paired:
+            head_part = head_part.reshape(n_x, per, D)
+            head_sent = moved(take(head_part, 0, 1 - x), lambda z, x, y, c: (z, 1 - x, y, c))
+        else:
+            grad_head = lax.psum_scatter(head_part, "x", scatter_dimension=0, tiled=True)
         grad_final, grad_final_gain = pull_final(grad_states)
+
+        cut = WIDE // 2 - 4 * D
 
         def same(value):
             return value
 
         middle_1, branch, out_1, gu_1, down_1, gain_f1 = ffn_back(
-            grad_final, saved_1, mats_1, norm_gains[2:4], same
+            grad_final, saved_1, mats_1, norm_gains[2:4], cut, same
         )
         grad_1, qkv_1, gain_a1 = attention_back(
             middle_1, branch, saved_1, slots, mats_1, norm_gains[2:4], docs, tables, same, same
         )
-        all_1 = jnp.concatenate([qkv_1, out_1, gu_1, down_1], axis=0)
+        all_1 = jnp.concatenate([qkv_1, out_1, *gu_1, down_1], axis=0)
         if paired:
             blocks = (n_z, n_x, cols, D)
-            kept_head = [grad_head]
-
-            def land_head(value):
-                value, kept_head[0] = lax.optimization_barrier((value, kept_head[0]))
-                return tick(value, lane_1)
-
             lane_1 = Lane(sum_all(all_1.reshape((n_y, n_c) + blocks)))
+            grad_1, head_sent = lax.optimization_barrier((grad_1, head_sent))
+            grad_head = take(head_part, 0, x) + head_sent
             grad_1 = start(grad_1, lane_1)
             middle_0, branch, out_0, gu_0, down_0, gain_f0 = ffn_back(
-                grad_1, saved_0, mats_0, norm_gains[0:2], lambda v: tick(v, lane_1)
+                grad_1, saved_0, mats_0, norm_gains[0:2], cut, lambda v: tick(v, lane_1)
             )
-            cut = span - D
-            early_2 = Lane(sum_at(jnp.concatenate([out_0, gu_0[:cut]], axis=0).reshape(blocks), 0, 1))
-            early_1 = Lane(sum_at(jnp.concatenate([gu_0[cut:], down_0], axis=0).reshape((n_c,) + blocks), 1))
-            middle_0, branch = start((middle_0, branch), early_1, early_2)
+            early = jnp.concatenate([gu_0[1], down_0], axis=0)
+            middle_0, branch, early = lax.optimization_barrier((middle_0, branch, early))
+            early = lax.psum_scatter(early, work_axes, scatter_dimension=0, tiled=True)
             grad_0, qkv_0, gain_a0 = attention_back(
                 middle_0, branch, saved_0, None, mats_0, norm_gains[0:2], docs, tables,
-                lambda v: tick(v, early_1, early_2), land_head,
+                same, lambda v: tick(v, lane_1),
             )
-            late = Lane(sum_at(qkv_0.reshape(blocks), 0, 0))
+            late = jnp.concatenate([qkv_0, out_0, gu_0[0]], axis=0)
+            grad_0, late, early = lax.optimization_barrier((grad_0, late, early))
+            late = lax.psum_scatter(late, work_axes, scatter_dimension=0, tiled=True)
             sent = embed_send(hit_0, grad_0)
-            grad_0, sent = start((grad_0, sent), late)
+            sent = tick(sent, lane_1)
             embed_got = exchange(sent)
-            lanes = (late, lane_1, early_1, early_2)
-            tick(grad_0, *lanes)
+            tick((), lane_1)
+            embed_got = tick(embed_got, lane_1)
             while not lane_1.done:
-                tick(grad_0, *lanes)
+                tick((), lane_1)
             own_1 = lane_1.result
-            pieces_1 = gather_stat(own_1, 1)
-            tick(grad_0, *lanes)
-            embed_got, pieces_1 = lax.optimization_barrier((embed_got, pieces_1))
-            while not all(lane.done for lane in lanes):
-                tick(grad_0, *lanes)
-            y, c = lax.axis_index("y"), lax.axis_index("c")
-            own_0 = jnp.where(y == 1, early_1.result, jnp.where(c == 1, early_2.result, late.result))
-            grad_head = kept_head[0]
-            pieces_0 = gather_stat(own_0, 0)
+            work_1 = to_work(own_1)
+            work_1, late = lax.optimization_barrier((work_1, late))
+            work_0 = jnp.concatenate([late, early], axis=0)
+            own_0 = from_work(work_0)
         else:
             own_1 = lax.psum_scatter(all_1, OWNERS, scatter_dimension=0, tiled=True)
             middle_0, branch, out_0, gu_0, down_0, gain_f0 = ffn_back(
-                grad_1, saved_0, mats_0, norm_gains[0:2], same
+                grad_1, saved_0, mats_0, norm_gains[0:2], cut, same
             )
             grad_0, qkv_0, gain_a0 = attention_back(
                 middle_0, branch, saved_0, None, mats_0, norm_gains[0:2], docs, tables, same, same
             )
-            all_0 = jnp.concatenate([qkv_0, out_0, gu_0, down_0], axis=0)
+            all_0 = jnp.concatenate([qkv_0, out_0, *gu_0, down_0], axis=0)
             own_0 = lax.psum_scatter(all_0, OWNERS, scatter_dimension=0, tiled=True)
             embed_got, stat_1 = exchange(embed_send(hit_0, grad_0)), stat_scatter(own_1)
             stat_0 = stat_scatter(own_0)
@@ -738,7 +677,8 @@
         square = jnp.sum(own_mats * own_mats) + jnp.sum(grad_embed * grad_embed) + jnp.sum(grad_head * grad_head)
         scalars = jnp.stack([square, loss_part, count.astype(f32)])
         small = jnp.concatenate([gain_part, jnp.broadcast_to(scalars[:, None], (3, D))], axis=0)
-        small = jnp.sum(lax.all_gather(small, DATA, axis=0), axis=0)
+        small = jnp.sum(lax.all_gather(small, ("x", "y", "c"), axis=0), axis=0)
+        small = jnp.sum(lax.all_gather(small, "z", axis=0), axis=0)
         gain_sum = small[: 2 * LAYERS + 1]
         square_sum, loss_sum, mask_count = (small[2 * LAYERS + 1 + i, 0] for i in range(3))
         clip_norm = jnp.sqrt(square_sum + jnp.sum(gain_sum * gain_sum)) / mask_count
@@ -751,18 +691,39 @@
         basis_start = (linear % sharing) * basis_rows
         flat_stats = soap_stats.reshape(n_mats, D, D)
         if paired:
-            mask = jnp.asarray(stat_routes()[1])[own_mat % KINDS, at_fs]
-            own_sum = share_stat([a + b for a, b in zip(pieces_0, pieces_1)], mask)
+            y, c = lax.axis_index("y"), lax.axis_index("c")
+            starts = ((jnp.arange(2) * 2 + y) * n_dp + at_dp) * cols + c * half
+            work_cols = (starts[:, None] + jnp.arange(half)[None, :]).reshape(-1)
+            work_kinds = sum((work_cols >= b).astype(jnp.int32) for b in BOUNDS[1:-1])
+            to_owner = []
+            for work in (work_0, work_1):
+                for kind in range(KINDS):
+                    mine = jnp.where((work_kinds == kind)[:, None], work, 0.0)
+                    to_owner.append(mine[:half] + mine[half:] if merges[kind] else mine)
+            most_rows = max(piece.shape[0] for piece in to_owner)
+            to_owner = [jnp.pad(piece, ((0, most_rows - piece.shape[0]), (0, 0))) for piece in to_owner]
+            columns = lax.all_to_all(jnp.stack(to_owner), DP, 0, 0, tiled=True)
+            own_sum = share_stat(columns.reshape(-1, D))
         else:
             own_sum = jnp.concatenate(
                 [lax.all_gather(part, DATA, axis=0, tiled=True) for part in (stat_0, stat_1)], axis=0
             ).reshape(n_mats, D, D)[own_mat]
+        sum_part = lax.dynamic_slice_in_dim(own_sum, basis_start, basis_rows)
+        stat_sums = lax.all_gather(sum_part, DATA, axis=0, tiled=True).reshape(n_mats, D, D)
         own_stat = stat_decay * flat_stats[own_mat] + stat_scale * own_sum
-        stats_part = lax.dynamic_slice_in_dim(own_stat, basis_start, basis_rows)
-        new_stats = lax.all_gather(stats_part, DATA, axis=0, tiled=True).reshape(soap_stats.shape)
         own_basis = soap_bases.reshape(n_mats, D, D)[own_mat]
-        new_rows = renew_rows(own_stat, own_basis, basis_start, basis_rows)
-        new_bases = lax.all_gather(new_rows, DATA, axis=0, tiled=True).reshape(soap_bases.shape)
+        product = nn(own_stat, own_basis, highest)
+        gram = tn(product, product, highest)
+        rows = lax.dynamic_slice_in_dim(product, basis_start, basis_rows)
+        rows, gram, stat_sums = lax.optimization_barrier((rows, gram, stat_sums))
+        first, rest = orthogonal_rows(gram, rows, D // (2 * STEPS))
+        first, rows, gram = lax.optimization_barrier((first[:, : D // 2], first[:, D // 2 :], rest[D // 2 :, D // 2 :]))
+        first = lax.all_gather(first, DATA, axis=0, tiled=True)
+        second, _ = orthogonal_rows(gram, rows, D // (2 * STEPS))
+        first, second = lax.optimization_barrier((first, second))
+        second = lax.all_gather(second, DATA, axis=0, tiled=True)
+        new_stats = (stat_decay * flat_stats + stat_scale * stat_sums).reshape(soap_stats.shape)
+        new_bases = jnp.concatenate([first, second], axis=1).reshape(soap_bases.shape)
 
         clipped = own_mats * factor
         basis_lo = jnp.take(soap_bases, lo, axis=1)

time: 2000 us -> 1710 us (0.85)
  starting transfers between devices: 325 us -> 55.9 us
  blocking collectives: 57.2 us -> 186 us
  local copies, waits for them, and re-layouts: 173 us -> 73.9 us
  other arithmetic: 226 us -> 193 us
    ppermute x61 -> x16, starting transfers between devices: 297 us -> 33 us  [moved(): return lax.ppermute(value, DATA, [(int(s), int(d)) for s, d in pairs])]
    all_gather x2 -> x3, waiting for transfers between devices: 190 us -> 83.4 us  [the longest x1 43.3 us: shards(): first = lax.all_gather(first, DATA, axis=0, tiled=True)]
    all_to_all x0 -> x1, blocking collectives: none -> 83 us  [shards(): columns = lax.all_to_all(jnp.stack(to_owner), DP, 0, 0, tiled=True)]
    reduce_scatter x1, waiting for transfers between devices: 39.5 us -> 114 us  [shards(): lax.psum_scatter(nn(grad_logits, head), HEAD_GROUP, scatter_dimension=0,...]
    all_to_all x1, waiting for transfers between devices: 68.8 us -> 0.01 us  [fetch(): got = lax.all_to_all(sent, OWNERS, 0, 0, tiled=True)]
    all_gather x1, waiting for transfers between devices: 0.01 us -> 53.6 us  [shards(): lax.all_gather(chosen_full.astype(bf16), HEAD_GROUP, axis=0, tiled=True)]
    all_gather x1, blocking collectives: 8.87 us -> 60.1 us  [shards(): lax.all_gather(jnp.stack([targets, code]), HEAD_GROUP, axis=1, tiled=True)]
    unnamed x321 -> x260, local copies, waits for them, and re-layouts: 77.2 us -> 28.5 us
  transfers between devices with their start and end apart: 71 -> 30, of which waited for: 25 -> 22; matrix products, arithmetic and copies ran while one was open for 18% -> 21% of each run, Pallas kernels for 5% -> 9%
where the time goes in v2:
time: 1710 us
  waiting for transfers between devices  648 us (38%)
  matrix products  316 us (18%)
  Pallas kernels  203 us (12%)
  other arithmetic  193 us (11%)
  blocking collectives  186 us (11%)
  local copies, waits for them, and re-layouts  73.9 us (4%)
  starting transfers between devices  55.9 us (3%)
  between operations  30.1 us (2%)
    dot_general x50, matrix products, dot(): lax.dot_general(a, b, (dims, ((), ())), precision=precision, preferred_el...  282 us
    ppermute x16, waiting for transfers between devices, moved(): return lax.ppermute(value, DATA, [(int(s), int(d)) for s, d in pairs])  279 us
    reduce_scatter x1, waiting for transfers between devices, shards(): lax.psum_scatter(nn(grad_logits, head), HEAD_GROUP, scatter_dimension=0,...  114 us
    all_to_all x1, blocking collectives, shards(): columns = lax.all_to_all(jnp.stack(to_owner), DP, 0, 0, tiled=True)  83 us
    pallas_call x2, Pallas kernels, orthogonal_rows(): pl.pallas_call(functools.partial(orthogonal_kernel, steps), out_shape=[ja...  78.9 us
    pallas_call x2, Pallas kernels, attend_back(): pl.pallas_call(attend_back_kernel, grid=(PAIRS,), in_specs=[column(n_q),...  63.2 us
    pallas_call x2, Pallas kernels, attend(): pl.pallas_call(attend_kernel, grid=(PAIRS,), in_specs=[column(n_q), colum...  61.3 us
    all_gather x1, blocking collectives, shards(): lax.all_gather(jnp.stack([targets, code]), HEAD_GROUP, axis=1, tiled=True)  60.1 us
  transfers between devices with their start and end apart: 30, of which 22 were waited for; matrix products, arithmetic and copies ran while one was open for 21% of the time, Pallas kernels for 9%

profile of v2, /device:TPU:0, one launch (start us, length us, event | category | flops | bytes accessed | tf_op | source)
XLA Modules:
  0.0 1705.5 jit_solution(4394293260124285276)
XLA Ops:
  48.2 60.1 %all_gather.45 = s32[2,4096]{1,0:T(2,128)} all-gather(s32[2,256]{1,0:T(2,128)S(1)} %pad_add_fusion), channel_id=1, replica_groups=mesh['z'=4,'x'=2,'y'=2,'c'=2] {'z','y','c'}, dimensions={1}, use_global_device_ids=true | all-gather | bytes 34816 | tf_op jit(solution)/shard_map/all_gather | solution.py:567
  130.5 24.4 %all-gather.23.cloned.1.call-done = bf16[1,9216,768]{2,1,0:T(8,128)(2,1)} async-done(((bf16[1,288,768]{2,1,0:T(8,128)(2,1)}), bf16[1,9216,768]{2,1,0:T(8,128)(2,1)}) %all-gather.23.cloned.1.call-update) | async-done | bytes 14155792 | tf_op jit(solution)/shard_map/all_gather | solution.py:488
  167.2 46.1 %attend.2 = (bf16[1024,768]{1,0:T(8,128)(2,1)}, bf16[1024,768]{1,0:T(8,128)(2,1)}, bf16[1024,768]{1,0:T(8,128)(2,1)}, bf16[1024,768]{1,0:T(8,128)(2,1)}, f32[6,2,1024]{2,1,0:T(2,128)}) custom-call(f32[1024,768]{1,0:T(8,128)} %fusion.129.q_ref, f32[1024,1536]{1,0:T(8,128)} %fusion.73.k_ref.v_ref, f32[1024,1536]{1,0:T(8,128)} %fusion.73.k_ref.v_ref, ...), custom_call_target="tpu_custom_call" | custom-call | flops 1000 | bytes 1000 | tf_op jit(solution)/shard_map/attend/pallas_call | solution.py:167
  244.6 15.2 all-gather.25.cloned.1.call-done
  270.1 15.2 attend.3
  307.7 53.6 %all-gather.15.cloned.1.call-done = bf16[4096,768]{1,0:T(8,128)(2,1)} async-done(((bf16[256,768]{1,0:T(8,128)(2,1)}), bf16[4096,768]{1,0:T(8,128)(2,1)}) %all-gather.15.cloned.1.call-update) | async-done | bytes 6291472 | tf_op jit(solution)/shard_map/all_gather | solution.py:583
  361.3 21.9 %fusion.240 = (f32[4096]{0:T(1024)S(1)}, f32[4096,2000]{0,1:T(8,128)}) fusion(bf16[4096,768]{1,0:T(8,128)(2,1)} %all-gather.15.cloned.1.call-done, bf16[1000,768]{1,0:T(8,128)(2,1)} %get-tuple-element.597, bf16[1000,768]{1,0:T(8,128)(2,1)} %get-tuple-element.596), kind=kOutput, calls=%fused_computation.470 | convolution fusion | flops 12597243904 | bytes 42147840 | tf_op jit(solution)/shard_map/dot_general | solution.py:55
  383.1 18.0 %exponential_reduce_fusion = (f32[4096]{0:T(1024)S(1)}, f32[4096]{0:T(1024)S(1)}) fusion(f32[4096,2000]{0,1:T(8,128)} %get-tuple-element.656, f32[4096]{0:T(1024)S(1)} %get-tuple-element.655, s32[4096]{0:T(1024)S(1)} %bitcast.441, s32[2000]{0:T(1024)S(1)} %copy-done.69), kind=kLoop, calls=%fused_computation.35 | loop fusion | flops 40951808 | bytes 32841536 | tf_op jit(solution)/shard_map/reduce_sum | solution.py:589
  407.5 13.9 all-gather.7
  434.3 18.9 %fusion.103 = f32[4096,768]{1,0:T(8,128)} fusion(bf16[4096,2000]{0,1:T(8,128)(2,1)} %fusion.28, bf16[1000,768]{1,0:T(8,128)(2,1)S(1)} %copy-done.53, bf16[1000,768]{1,0:T(8,128)(2,1)S(1)} %copy-done.52), kind=kOutput, calls=%fused_computation.198 | convolution fusion | flops 12589056000 | bytes 32038912 | tf_op jit(solution)/shard_map/dot_general | solution.py:55
  453.3 19.6 %fusion.241 = f32[2000,768]{1,0:T(8,128)} fusion(bf16[4096,2000]{0,1:T(8,128)(2,1)} %fusion.28, bf16[4096,768]{1,0:T(8,128)(2,1)} %all-gather.15.cloned.1.call-done), kind=kOutput, calls=%fused_computation.471 | convolution fusion | flops 12582912000 | bytes 28819456 | tf_op jit(solution)/shard_map/dot_general | solution.py:55
  472.9 113.9 %reduce-scatter.4.cloned.1.call-done = f32[256,768]{1,0:T(8,128)} async-done(((f32[4096,768]{1,0:T(8,128)}), f32[256,768]{1,0:T(8,128)}) %reduce-scatter.4.cloned.1.call-update) | async-done | bytes 786448 | tf_op jit(solution)/shard_map/reduce_scatter | solution.py:607
  607.3 15.5 attend_back.2
  659.0 18.7 %dynamic-slice_bitcast_fusion = (f32[2,4,2,288,768]{4,3,2,1,0:T(8,128)}, f32[2,4,2,288,768]{4,3,2,1,0:T(8,128)}) fusion(f32[2,2,4,2,288,768]{5,4,3,2,1,0:T(8,128)} %bitcast.407, s32[]{:T(128)S(6)} %select_n.345, s32[]{:T(128)S(6)} %select_n.344), kind=kLoop, calls=%fused_computation.39 | loop fusion | bytes 56623112 | tf_op jit(solution)/shard_map/jit(dynamic_index_in_dim)/squeeze | solution.py:371
  767.1 47.6 %attend_back.3 = (bf16[1024,768]{1,0:T(8,128)(2,1)}, bf16[1024,768]{1,0:T(8,128)(2,1)}, bf16[1024,768]{1,0:T(8,128)(2,1)}) custom-call(bf16[1024,768]{1,0:T(8,128)(2,1)} %get-tuple-element.343.qs_ref, bf16[1024,768]{1,0:T(8,128)(2,1)} %get-tuple-element.344.k_ref, bf16[1024,768]{1,0:T(8,128)(2,1)} %get-tuple-element.345.v_ref, ...), custom_call_target="tpu_custom_call" | custom-call | flops 1000 | bytes 1000 | tf_op jit(solution)/shard_map/attend_back/pallas_call | solution.py:184
  814.8 37.9 %collective-permute-done.3 = f32[2,4,144,768]{3,2,1,0:T(8,128)} collective-permute-done((f32[2,4,144,768]{3,2,1,0:T(8,128)}, f32[2,4,144,768]{3,2,1,0:T(8,128)}, u32[]{:S(2)}, u32[]{:S(2)}) %collective-permute-start.3) | collective-permute-done | bytes 3538976 | tf_op jit(solution)/shard_map/ppermute | solution.py:368
  894.5 33.9 %reduce-scatter.6.cloned.1.call-done = f32[144,768]{1,0:T(8,128)} async-done(((f32[4608,768]{1,0:T(8,128)}), f32[144,768]{1,0:T(8,128)}) %reduce-scatter.6.cloned.1.call-update) | async-done | bytes 442384 | tf_op jit(solution)/shard_map/reduce_scatter | solution.py:640
  937.9 30.0 %collective-permute-done.5 = f32[4,144,768]{2,1,0:T(8,128)} collective-permute-done((f32[4,144,768]{2,1,0:T(8,128)}, f32[4,144,768]{2,1,0:T(8,128)}, u32[]{:S(2)}, u32[]{:S(2)}) %collective-permute-start.5) | collective-permute-done | bytes 1769504 | tf_op jit(solution)/shard_map/ppermute | solution.py:368
  983.7 117.7 %collective-permute-done.7 = f32[288,768]{1,0:T(8,128)} collective-permute-done((f32[288,768]{1,0:T(8,128)}, f32[288,768]{1,0:T(8,128)}, u32[]{:S(2)}, u32[]{:S(2)}) %collective-permute-start.7) | collective-permute-done | bytes 884768 | tf_op jit(solution)/shard_map/ppermute | solution.py:368
  1111.2 33.0 %collective-permute-done.9 = f32[288,768]{1,0:T(8,128)} collective-permute-done((f32[288,768]{1,0:T(8,128)}, f32[288,768]{1,0:T(8,128)}, u32[]{:S(2)}, u32[]{:S(2)}) %collective-permute-start.9) | collective-permute-done | bytes 884768 | tf_op jit(solution)/shard_map/ppermute | solution.py:368
  1158.6 23.8 %collective-permute-done.11 = f32[288,768]{1,0:T(8,128)} collective-permute-done((f32[288,768]{1,0:T(8,128)}, f32[288,768]{1,0:T(8,128)}, u32[]{:S(2)}, u32[]{:S(2)}) %collective-permute-start.11) | collective-permute-done | bytes 884768 | tf_op jit(solution)/shard_map/ppermute | solution.py:368
  1193.0 21.7 %all-to-all-done.7 = f32[4,144,768]{2,1,0:T(8,128)S(1)} async-done(((f32[4,144,768]{2,1,0:T(8,128)}), f32[4,144,768]{2,1,0:T(8,128)S(1)}, u32[]{:S(2)}, u32[]{:S(2)}) %all-to-all-start.7) | async-done | bytes 1769504 | tf_op jit(solution)/shard_map/all_to_all | solution.py:439
  1217.2 83.0 %all_to_all.121 = f32[8,144,768]{2,1,0:T(8,128)S(1)} all-to-all(f32[8,144,768]{2,1,0:T(8,128)S(1)} %fusion.168), channel_id=1, replica_groups=mesh['z'=4,'x'=2,'y'=2,'c'=2] {'z','x'}, dimensions={0} | all-to-all | bytes 7077888 | tf_op jit(solution)/shard_map/all_to_all | solution.py:705
  1318.7 27.4 %collective-permute-done.14 = f32[384,768]{1,0:T(8,128)S(1)} collective-permute-done((f32[384,768]{1,0:T(8,128)S(1)}, f32[384,768]{1,0:T(8,128)S(1)}, u32[]{:S(2)}, u32[]{:S(2)}) %collective-permute-start.14) | collective-permute-done | bytes 1179680 | tf_op jit(solution)/shard_map/ppermute | solution.py:368
  1380.0 18.8 %all-to-all-done.8 = f32[4,144,768]{2,1,0:T(8,128)} async-done(((f32[4,144,768]{2,1,0:T(8,128)}), f32[4,144,768]{2,1,0:T(8,128)}, u32[]{:S(2)}, u32[]{:S(2)}) %all-to-all-start.8) | async-done | bytes 1769504 | tf_op jit(solution)/shard_map/all_to_all | solution.py:445
  1413.3 14.4 all-gather.5
  1447.3 28.1 %all-gather.17.cloned.1.call-done = f32[6144,768]{1,0:T(8,128)} async-done(((f32[192,768]{1,0:T(8,128)}), f32[6144,768]{1,0:T(8,128)}) %all-gather.17.cloned.1.call-update) | async-done | bytes 18874384 | tf_op jit(solution)/shard_map/all_gather | solution.py:712
  1475.3 41.6 %orthogonal_rows.2 = (f32[192,768]{1,0:T(8,128)S(1)}, f32[768,768]{1,0:T(8,128)S(1)}) custom-call(f32[768,768]{1,0:T(8,128)S(1)} %fusion.243.gram_ref, f32[192,768]{1,0:T(8,128)S(1)} %constant_dynamic-slice_fusion.rows_ref), custom_call_target="tpu_custom_call" | custom-call | flops 99999997952 | bytes 4718592 | tf_op jit(solution)/shard_map/orthogonal_rows/pallas_call | solution.py:255
  1517.9 37.3 %orthogonal_rows.3 = (f32[192,384]{1,0:T(8,128)}, f32[384,384]{1,0:T(8,128)}) custom-call(f32[384,384]{1,0:T(8,128)S(1)} %slice.352.gram_ref, f32[192,384]{1,0:T(8,128)S(1)} %get-tuple-element.418.rows_ref), custom_call_target="tpu_custom_call" | custom-call | flops 99999997952 | bytes 4718592 | tf_op jit(solution)/shard_map/orthogonal_rows/pallas_call | solution.py:255
  1555.2 43.3 %all-gather.19.cloned.1.call-done = f32[6144,384]{1,0:T(8,128)} async-done(((f32[192,384]{1,0:T(8,128)}), f32[6144,384]{1,0:T(8,128)}) %all-gather.19.cloned.1.call-update) | async-done | bytes 9437200 | tf_op jit(solution)/shard_map/all_gather | solution.py:721
  1651.5 19.1 %multiply_add_fusion = f32[8,768,768]{2,1,0:T(8,128)} fusion(f32[8,768,768]{2,1,0:T(8,128)} %bitcast.420, f32[]{:T(128)S(6)} %mul.826, f32[2,4,768,768]{3,2,1,0:T(8,128)} %param.31), kind=kLoop, calls=%fused_computation.37 | loop fusion | flops 14155776 | bytes 56623108 | tf_op jit(solution)/shard_map/add | solution.py:725
  1682.7 14.7 pad_maximum_fusion
  (523 shorter events, 547.3 us)
Async XLA Ops:
  7.2 147.7 %all-gather.23.cloned.1.call-start = ((), (), s32[]{:S(2)}) async-start(), calls=%async_computation.20 | async-start | bytes 14598144 | tf_op jit(solution)/shard_map/all_gather | solution.py:488
  9.8 250.1 %all-gather.25.cloned.1.call-start = ((), (), s32[]{:S(2)}) async-start(), calls=%async_computation.21 | async-start | bytes 14598144 | tf_op jit(solution)/shard_map/all_gather | solution.py:571
  13.0 274.1 %copy-start.65 = (s32[1,1024]{1,0:T(1,128)}, s32[1,1024]{1,0:T(1,128)S(1)}, u32[]{:S(2)}) copy-start(s32[1,1024]{1,0:T(1,128)S(1)} %get-tuple-element.634) | copy-start | bytes 12292
  18.1 14.4 all-to-all-start.4
  37.7 79.3 %all-to-all-start.5 = ((bf16[32,40,768]{2,1,0:T(8,128)(2,1)}), bf16[32,40,768]{2,1,0:T(8,128)(2,1)S(1)}, u32[]{:S(2)}, u32[]{:S(2)}) async-start(bf16[32,40,768]{2,1,0:T(8,128)(2,1)} %bitcast.437), calls=%async_computation.5 | async-start | bytes 3932160 | tf_op jit(solution)/shard_map/all_to_all | solution.py:505
  41.2 320.1 %all-gather.15.cloned.1.call-start = ((), (), s32[]{:S(2)}) async-start(), calls=%async_computation.13 | async-start | bytes 6684672 | tf_op jit(solution)/shard_map/all_gather | solution.py:583
  43.8 197.8 %collective-permute-start = (bf16[1000,768]{1,0:T(8,128)(2,1)}, bf16[1000,768]{1,0:T(8,128)(2,1)}, u32[]{:S(2)}, u32[]{:S(2)}) collective-permute-start(bf16[1000,768]{1,0:T(8,128)(2,1)} %slice_bitcast_fusion.18), channel_id=1, source_target_pairs={{0,4},{1,5},{2,6},{3,7},{4,0},{5,1},{6,2},{7,3},{8,12},{9,13},{10,... | collective-permute-start | bytes 4608008 | tf_op jit(solution)/shard_map/ppermute | solution.py:368
  110.6 189.3 %copy-start.80 = (f32[768]{0:T(1024)}, f32[768]{0:T(1024)S(1)}, u32[]{:S(2)}) copy-start(f32[768]{0:T(1024)S(1)} %get-tuple-element.530) | copy-start | bytes 9220
  301.1 285.7 %reduce-scatter.4.cloned.1.call-start = ((), (), s32[]{:S(2)}) async-start(), calls=%async_computation.14 | async-start | bytes 13369344 | tf_op jit(solution)/shard_map/reduce_scatter | solution.py:607
  453.2 475.2 %reduce-scatter.6.cloned.1.call-start = ((), (), s32[]{:S(2)}) async-start(), calls=%async_computation.15 | async-start | bytes 14598144 | tf_op jit(solution)/shard_map/reduce_scatter | solution.py:640
  603.1 74.6 %collective-permute-start.1 = (f32[1000,768]{1,0:T(8,128)}, f32[1000,768]{1,0:T(8,128)}, u32[]{:S(2)}, u32[]{:S(2)}) collective-permute-start(f32[1000,768]{1,0:T(8,128)} %dynamic-slice_bitcast_fusion.4), channel_id=1, source_target_pairs={{0,4},{1,5},{2,6},{3,7},{4,0},{5,1},{6,2},{7,3},{8,12},{9,13},{10,... | collective-permute-start | bytes 9216008 | tf_op jit(solution)/shard_map/ppermute | solution.py:368
  677.7 28.9 %collective-permute-start.2 = (f32[2,4,2,288,768]{4,3,2,1,0:T(8,128)}, f32[2,4,2,288,768]{4,3,2,1,0:T(8,128)}, u32[]{:S(2)}, u32[]{:S(2)}) collective-permute-start(f32[2,4,2,288,768]{4,3,2,1,0:T(8,128)} %get-tuple-element.362), channel_id=1, source_target_pairs={{0,1},{1,0},{2,3},{3,2},{4,5},{5,4},{6,7},{7,6},{8,9},{9,8},{10,11... | collective-permute-start | bytes 42467336 | tf_op jit(solution)/shard_map/ppermute | solution.py:368
  760.6 454.1 %reduce-scatter.8.cloned.1.call-start = ((), (), s32[]{:S(2)}) async-start(), calls=%async_computation.16 | async-start | bytes 14598144 | tf_op jit(solution)/shard_map/reduce_scatter | solution.py:647
  760.7 91.9 %collective-permute-start.3 = (f32[2,4,144,768]{3,2,1,0:T(8,128)}, f32[2,4,144,768]{3,2,1,0:T(8,128)}, u32[]{:S(2)}, u32[]{:S(2)}) collective-permute-start(f32[2,4,144,768]{3,2,1,0:T(8,128)} %dynamic-slice_bitcast_fusion.3), channel_id=1, source_target_pairs={{0,4},{1,5},{2,6},{3,7},{4,0},{5,1},{6,2},{7,3},{8,12},{9,13},{10,... | collective-permute-start | bytes 10616840 | tf_op jit(solution)/shard_map/ppermute | solution.py:368
  761.3 91.6 %collective-permute-start.4 = (f32[4,2,144,768]{3,2,1,0:T(8,128)}, f32[4,2,144,768]{3,2,1,0:T(8,128)}, u32[]{:S(2)}, u32[]{:S(2)}) collective-permute-start(f32[4,2,144,768]{3,2,1,0:T(8,128)} %dynamic-slice_bitcast_fusion.2), channel_id=1, source_target_pairs={{0,2},{1,3},{2,0},{3,1},{4,6},{5,7},{6,4},{7,5},{8,10},{9,11},{10,... | collective-permute-start | bytes 10616840 | tf_op jit(solution)/shard_map/ppermute | solution.py:368
  928.4 39.4 %collective-permute-start.5 = (f32[4,144,768]{2,1,0:T(8,128)}, f32[4,144,768]{2,1,0:T(8,128)}, u32[]{:S(2)}, u32[]{:S(2)}) collective-permute-start(f32[4,144,768]{2,1,0:T(8,128)} %dynamic-slice_bitcast_fusion.6), channel_id=1, source_target_pairs={{0,2},{1,3},{2,0},{3,1},{4,6},{5,7},{6,4},{7,5},{8,10},{9,11},{10,... | collective-permute-start | bytes 5308424 | tf_op jit(solution)/shard_map/ppermute | solution.py:368
  929.8 39.1 %collective-permute-start.6 = (f32[4,144,768]{2,1,0:T(8,128)}, f32[4,144,768]{2,1,0:T(8,128)}, u32[]{:S(2)}, u32[]{:S(2)}) collective-permute-start(f32[4,144,768]{2,1,0:T(8,128)} %dynamic-slice_bitcast_fusion.5), channel_id=1, source_target_pairs={{0,4},{1,5},{2,6},{3,7},{4,0},{5,1},{6,2},{7,3},{8,12},{9,13},{10,... | collective-permute-start | bytes 5308424 | tf_op jit(solution)/shard_map/ppermute | solution.py:368
  974.0 170.2 %all-to-all-start.6 = ((f32[32,40,768]{2,1,0:T(8,128)}), f32[32,40,768]{2,1,0:T(8,128)}, u32[]{:S(2)}, u32[]{:S(2)}) async-start(f32[32,40,768]{2,1,0:T(8,128)} %bitcast.434), calls=%async_computation.8 | async-start | bytes 7864320 | tf_op jit(solution)/shard_map/all_to_all | solution.py:512
  977.5 123.8 %collective-permute-start.7 = (f32[288,768]{1,0:T(8,128)}, f32[288,768]{1,0:T(8,128)}, u32[]{:S(2)}, u32[]{:S(2)}) collective-permute-start(f32[288,768]{1,0:T(8,128)} %get-tuple-element.392), channel_id=1, source_target_pairs={{0,8},{1,9},{2,10},{3,11},{4,12},{5,13},{6,14},{7,15}} | collective-permute-start | bytes 2654216 | tf_op jit(solution)/shard_map/ppermute | solution.py:368
  982.1 119.3 %collective-permute-start.8 = (f32[288,768]{1,0:T(8,128)}, f32[288,768]{1,0:T(8,128)}, u32[]{:S(2)}, u32[]{:S(2)}) collective-permute-start(f32[288,768]{1,0:T(8,128)} %get-tuple-element.393), channel_id=1, source_target_pairs={{24,16},{25,17},{26,18},{27,19},{28,20},{29,21},{30,22},{31,23}} | collective-permute-start | bytes 2654216 | tf_op jit(solution)/shard_map/ppermute | solution.py:368
  1104.2 39.9 %collective-permute-start.9 = (f32[288,768]{1,0:T(8,128)}, f32[288,768]{1,0:T(8,128)}, u32[]{:S(2)}, u32[]{:S(2)}) collective-permute-start(f32[288,768]{1,0:T(8,128)} %get-tuple-element.396), channel_id=1, source_target_pairs={{0,8},{1,9},{2,10},{3,11},{4,12},{5,13},{6,14},{7,15},{8,16},{9,17... | collective-permute-start | bytes 2654216 | tf_op jit(solution)/shard_map/ppermute | solution.py:368
  1109.6 34.5 %collective-permute-start.10 = (f32[288,768]{1,0:T(8,128)}, f32[288,768]{1,0:T(8,128)}, u32[]{:S(2)}, u32[]{:S(2)}) collective-permute-start(f32[288,768]{1,0:T(8,128)} %get-tuple-element.397), channel_id=1, source_target_pairs={{16,8},{17,9},{18,10},{19,11},{20,12},{21,13},{22,14},{23,15},{24,... | collective-permute-start | bytes 2654216 | tf_op jit(solution)/shard_map/ppermute | solution.py:368
  1147.1 35.4 %collective-permute-start.11 = (f32[288,768]{1,0:T(8,128)}, f32[288,768]{1,0:T(8,128)}, u32[]{:S(2)}, u32[]{:S(2)}) collective-permute-start(f32[288,768]{1,0:T(8,128)} %get-tuple-element.401), channel_id=1, source_target_pairs={{0,8},{1,9},{2,10},{3,11},{4,12},{5,13},{6,14},{7,15},{8,16},{9,17... | collective-permute-start | bytes 2654216 | tf_op jit(solution)/shard_map/ppermute | solution.py:368
  1157.2 27.6 %collective-permute-start.12 = (f32[288,768]{1,0:T(8,128)}, f32[288,768]{1,0:T(8,128)}, u32[]{:S(2)}, u32[]{:S(2)}) collective-permute-start(f32[288,768]{1,0:T(8,128)} %get-tuple-element.402), channel_id=1, source_target_pairs={{8,0},{9,1},{10,2},{11,3},{12,4},{13,5},{14,6},{15,7},{16,8},{17,9... | collective-permute-start | bytes 2654216 | tf_op jit(solution)/shard_map/ppermute | solution.py:368
  1188.7 25.9 %all-to-all-start.7 = ((f32[4,144,768]{2,1,0:T(8,128)}), f32[4,144,768]{2,1,0:T(8,128)S(1)}, u32[]{:S(2)}, u32[]{:S(2)}) async-start(f32[4,144,768]{2,1,0:T(8,128)} %bitcast_multiply_fusion.1), calls=%async_computation.9 | async-start | bytes 3538944 | tf_op jit(solution)/shard_map/all_to_all | solution.py:439
  1192.5 282.9 %all-gather.17.cloned.1.call-start = ((), (), s32[]{:S(2)}) async-start(), calls=%async_computation.17 | async-start | bytes 19464192 | tf_op jit(solution)/shard_map/all_gather | solution.py:712
  1315.0 2.9 collective-permute-start.13
  1318.1 28.1 %collective-permute-start.14 = (f32[384,768]{1,0:T(8,128)S(1)}, f32[384,768]{1,0:T(8,128)S(1)}, u32[]{:S(2)}, u32[]{:S(2)}) collective-permute-start(f32[384,768]{1,0:T(8,128)S(1)} %bitcast_add_fusion.5), channel_id=1, source_target_pairs={{0,2},{1,3},{2,0},{3,1},{4,6},{5,7},{6,4},{7,5},{8,10},{9,11},{10,... | collective-permute-start | bytes 3538952 | tf_op jit(solution)/shard_map/ppermute | solution.py:368
  1347.3 3.2 collective-permute-start.15
  1364.1 34.7 %all-to-all-start.8 = ((f32[4,144,768]{2,1,0:T(8,128)}), f32[4,144,768]{2,1,0:T(8,128)}, u32[]{:S(2)}, u32[]{:S(2)}) async-start(f32[4,144,768]{2,1,0:T(8,128)} %bitcast_multiply_fusion), calls=%async_computation.11 | async-start | bytes 3538944 | tf_op jit(solution)/shard_map/all_to_all | solution.py:445
  1368.7 229.8 %all-gather.19.cloned.1.call-start = ((), (), s32[]{:S(2)}) async-start(), calls=%async_computation.18 | async-start | bytes 9732096 | tf_op jit(solution)/shard_map/all_gather | solution.py:721
  1517.8 164.8 %all-gather.21.cloned.1.call-start = ((), (), s32[]{:S(2)}) async-start(), calls=%async_computation.19 | async-start | bytes 9732096 | tf_op jit(solution)/shard_map/all_gather | solution.py:724
  (127 other events, 2650.6 us)
Sparse Core Ops, SparseCore 0:
  11.6 143.2 all-gather.22
  158.5 101.3 all-gather.24
  301.2 59.9 all-gather.14
  453.3 133.3 reduce-scatter.3
  760.8 167.5 reduce-scatter.5
  934.8 239.1 reduce-scatter.7
  1352.9 122.4 all-gather.16
  1517.9 80.5 all-gather.18
  1602.0 80.6 all-gather.20

commit v3 on v2

--- a/solution.py
+++ b/solution.py
@@ -1,5 +1,3 @@
-import functools
-
 import jax
 import jax.numpy as jnp
 import numpy as np
@@ -232,10 +230,10 @@
     return jnp.concatenate(right, axis=0) * lax.rsqrt(pivots)
 
 
-def orthogonal_kernel(steps, gram_ref, rows_ref, out_ref, rest_ref):
+def orthogonal_kernel(gram_ref, rows_ref, out_ref, rest_ref):
     rest_ref[...] = gram_ref[...]
     out_ref[...] = rows_ref[...]
-    lane = lax.broadcasted_iota(jnp.int32, (1, gram_ref.shape[0]), 1)
+    lane = lax.broadcasted_iota(jnp.int32, (1, D), 1)
 
     def body(b, _):
         start = pl.multiple_of(b * STEPS, STEPS)
@@ -248,17 +246,18 @@
         rest_ref[...] -= fm(upper, upper, 0, 0)
         return 0
 
-    lax.fori_loop(0, steps, body, 0)
-
-
-def orthogonal_rows(gram, rows, steps):
+    lax.fori_loop(0, D // STEPS, body, 0)
+
+
+def orthogonal_rows(gram, rows):
     return pl.pallas_call(
-        functools.partial(orthogonal_kernel, steps),
-        out_shape=[jax.ShapeDtypeStruct(rows.shape, f32), jax.ShapeDtypeStruct(gram.shape, f32)],
+        orthogonal_kernel,
+        out_shape=jax.ShapeDtypeStruct(rows.shape, f32),
         in_specs=[pl.BlockSpec(memory_space=pltpu.VMEM)] * 2,
-        out_specs=[pl.BlockSpec(memory_space=pltpu.VMEM)] * 2,
+        out_specs=pl.BlockSpec(memory_space=pltpu.VMEM),
+        scratch_shapes=[pltpu.VMEM((D, D), f32)],
         compiler_params=pltpu.CompilerParams(vmem_limit_bytes=40 * 2**20),
-        cost_estimate=pl.CostEstimate(flops=10**11, bytes_accessed=8 * D * D, transcendentals=0),
+        cost_estimate=pl.CostEstimate(flops=2 * 10**11, bytes_accessed=8 * D * D, transcendentals=0),
         name="orthogonal_rows",
     )(gram, rows)
 
@@ -527,7 +526,7 @@
         residual = fetch(hit_0, rows_0)
         residual = lax.fori_loop(1, rounds, fetch_more, residual)
 
-        at_fs = lax.axis_index(FS)
+        at_fs, at_dp = lax.axis_index(FS), lax.axis_index(DP)
         lo = jnp.asarray(kind_lo, jnp.int32)[at_fs]
         hi = jnp.asarray(kind_hi, jnp.int32)[at_fs]
         col_ids = (at_fs * n_dp + lax.axis_index(DP)) * cols + jnp.arange(cols, dtype=jnp.int32)
@@ -619,78 +618,7 @@
         def same(value):
             return value
 
-        middle_1, branch, out_1, gu_1, down_1, gain_f1 = ffn_back(
-            grad_final, saved_1, mats_1, norm_gains[2:4], cut, same
-        )
-        grad_1, qkv_1, gain_a1 = attention_back(
-            middle_1, branch, saved_1, slots, mats_1, norm_gains[2:4], docs, tables, same, same
-        )
-        all_1 = jnp.concatenate([qkv_1, out_1, *gu_1, down_1], axis=0)
-        if paired:
-            blocks = (n_z, n_x, cols, D)
-            lane_1 = Lane(sum_all(all_1.reshape((n_y, n_c) + blocks)))
-            grad_1, head_sent = lax.optimization_barrier((grad_1, head_sent))
-            grad_head = take(head_part, 0, x) + head_sent
-            grad_1 = start(grad_1, lane_1)
-            middle_0, branch, out_0, gu_0, down_0, gain_f0 = ffn_back(
-                grad_1, saved_0, mats_0, norm_gains[0:2], cut, lambda v: tick(v, lane_1)
-            )
-            early = jnp.concatenate([gu_0[1], down_0], axis=0)
-            middle_0, branch, early = lax.optimization_barrier((middle_0, branch, early))
-            early = lax.psum_scatter(early, work_axes, scatter_dimension=0, tiled=True)
-            grad_0, qkv_0, gain_a0 = attention_back(
-                middle_0, branch, saved_0, None, mats_0, norm_gains[0:2], docs, tables,
-                same, lambda v: tick(v, lane_1),
-            )
-            late = jnp.concatenate([qkv_0, out_0, gu_0[0]], axis=0)
-            grad_0, late, early = lax.optimization_barrier((grad_0, late, early))
-            late = lax.psum_scatter(late, work_axes, scatter_dimension=0, tiled=True)
-            sent = embed_send(hit_0, grad_0)
-            sent = tick(sent, lane_1)
-            embed_got = exchange(sent)
-            tick((), lane_1)
-            embed_got = tick(embed_got, lane_1)
-            while not lane_1.done:
-                tick((), lane_1)
-            own_1 = lane_1.result
-            work_1 = to_work(own_1)
-            work_1, late = lax.optimization_barrier((work_1, late))
-            work_0 = jnp.concatenate([late, early], axis=0)
-            own_0 = from_work(work_0)
-        else:
-            own_1 = lax.psum_scatter(all_1, OWNERS, scatter_dimension=0, tiled=True)
-            middle_0, branch, out_0, gu_0, down_0, gain_f0 = ffn_back(
-                grad_1, saved_0, mats_0, norm_gains[0:2], cut, same
-            )
-            grad_0, qkv_0, gain_a0 = attention_back(
-                middle_0, branch, saved_0, None, mats_0, norm_gains[0:2], docs, tables, same, same
-            )
-            all_0 = jnp.concatenate([qkv_0, out_0, *gu_0, down_0], axis=0)
-            own_0 = lax.psum_scatter(all_0, OWNERS, scatter_dimension=0, tiled=True)
-            embed_got, stat_1 = exchange(embed_send(hit_0, grad_0)), stat_scatter(own_1)
-            stat_0 = stat_scatter(own_0)
-        grad_embed = embed_sum(rows_0, embed_got)
-        grad_embed, _ = lax.fori_loop(1, rounds, give_more, (grad_embed, grad_0))
-
-        gain_part = jnp.stack([gain_a0, gain_f0, gain_a1, gain_f1, grad_final_gain])
-        own_mats = jnp.stack([own_0, own_1])
-        square = jnp.sum(own_mats * own_mats) + jnp.sum(grad_embed * grad_embed) + jnp.sum(grad_head * grad_head)
-        scalars = jnp.stack([square, loss_part, count.astype(f32)])
-        small = jnp.concatenate([gain_part, jnp.broadcast_to(scalars[:, None], (3, D))], axis=0)
-        small = jnp.sum(lax.all_gather(small, ("x", "y", "c"), axis=0), axis=0)
-        small = jnp.sum(lax.all_gather(small, "z", axis=0), axis=0)
-        gain_sum = small[: 2 * LAYERS + 1]
-        square_sum, loss_sum, mask_count = (small[2 * LAYERS + 1 + i, 0] for i in range(3))
-        clip_norm = jnp.sqrt(square_sum + jnp.sum(gain_sum * gain_sum)) / mask_count
-        factor = jnp.minimum(1.0, clip_limit / clip_norm) / mask_count
-
-        at_dp = lax.axis_index(DP)
-        stat_scale = (1.0 - stat_decay) * (factor * factor)
-        own_mat = at_dp * n_mats // n_dp
-        linear = at_dp * n_fs + at_fs
-        basis_start = (linear % sharing) * basis_rows
-        flat_stats = soap_stats.reshape(n_mats, D, D)
-        if paired:
+        def stat_of_owner(work_0, work_1):
             y, c = lax.axis_index("y"), lax.axis_index("c")
             starts = ((jnp.arange(2) * 2 + y) * n_dp + at_dp) * cols + c * half
             work_cols = (starts[:, None] + jnp.arange(half)[None, :]).reshape(-1)
@@ -703,27 +631,97 @@
             most_rows = max(piece.shape[0] for piece in to_owner)
             to_owner = [jnp.pad(piece, ((0, most_rows - piece.shape[0]), (0, 0))) for piece in to_owner]
             columns = lax.all_to_all(jnp.stack(to_owner), DP, 0, 0, tiled=True)
-            own_sum = share_stat(columns.reshape(-1, D))
+            return share_stat(columns.reshape(-1, D))
+
+        own_mat = at_dp * n_mats // n_dp
+        flat_stats = soap_stats.reshape(n_mats, D, D)
+        own_basis = soap_bases.reshape(n_mats, D, D)[own_mat]
+        old_product = nn(flat_stats[own_mat], own_basis, highest)
+
+        def rows_sum(rows):
+            return lax.psum_scatter(rows, work_axes if paired else OWNERS, scatter_dimension=0, tiled=True)
+
+        middle_1, branch, out_1, gu_1, down_1, gain_f1 = ffn_back(
+            grad_final, saved_1, mats_1, norm_gains[2:4], cut, same
+        )
+        grad_1, qkv_1, gain_a1 = attention_back(
+            middle_1, branch, saved_1, slots, mats_1, norm_gains[2:4], docs, tables, same, same
+        )
+        if paired:
+            all_1 = jnp.concatenate([qkv_1, out_1, *gu_1, down_1], axis=0)
+            lane_1 = Lane(sum_all(all_1.reshape(n_y, n_c, n_z, n_x, cols, D)))
+            grad_1, head_sent = lax.optimization_barrier((grad_1, head_sent))
+            grad_head = take(head_part, 0, x) + head_sent
+            grad_1 = start(grad_1, lane_1)
+            middle_0, branch, out_0, gu_0, down_0, gain_f0 = ffn_back(
+                grad_1, saved_0, mats_0, norm_gains[0:2], cut, lambda v: tick(v, lane_1)
+            )
+            early_0 = jnp.concatenate([gu_0[1], down_0], axis=0)
+            middle_0, branch, early_0 = lax.optimization_barrier((middle_0, branch, early_0))
+            early_0 = rows_sum(early_0)
+            grad_0, qkv_0, gain_a0 = attention_back(
+                middle_0, branch, saved_0, None, mats_0, norm_gains[0:2], docs, tables,
+                same, lambda v: tick(v, lane_1),
+            )
+            late_0 = jnp.concatenate([qkv_0, out_0, gu_0[0]], axis=0)
+            grad_0, late_0, early_0 = lax.optimization_barrier((grad_0, late_0, early_0))
+            late_0 = rows_sum(late_0)
+            sent = embed_send(hit_0, grad_0)
+            sent = tick(sent, lane_1)
+            while not lane_1.done:
+                tick((), lane_1)
+            own_1 = lane_1.result
+            work_1 = to_work(own_1)
+            work_1, late_0, sent, old_product = lax.optimization_barrier((work_1, late_0, sent, old_product))
+            embed_got = exchange(sent)
+            work_0 = jnp.concatenate([late_0, early_0], axis=0)
+            own_sum = stat_of_owner(work_0, work_1)
+            own_sum, embed_got = lax.optimization_barrier((own_sum, embed_got))
+            own_0 = from_work(work_0)
         else:
+            own_1 = rows_sum(jnp.concatenate([qkv_1, out_1, *gu_1, down_1], axis=0))
+            middle_0, branch, out_0, gu_0, down_0, gain_f0 = ffn_back(
+                grad_1, saved_0, mats_0, norm_gains[0:2], cut, same
+            )
+            grad_0, qkv_0, gain_a0 = attention_back(
+                middle_0, branch, saved_0, None, mats_0, norm_gains[0:2], docs, tables, same, same
+            )
+            own_0 = rows_sum(jnp.concatenate([qkv_0, out_0, *gu_0, down_0], axis=0))
+            embed_got = exchange(embed_send(hit_0, grad_0))
+            stat_0, stat_1 = stat_scatter(own_0), stat_scatter(own_1)
+        grad_embed = embed_sum(rows_0, embed_got)
+        grad_embed, _ = lax.fori_loop(1, rounds, give_more, (grad_embed, grad_0))
+
+        gain_part = jnp.stack([gain_a0, gain_f0, gain_a1, gain_f1, grad_final_gain])
+        held = jnp.concatenate([work_0, work_1] if paired else [own_0, own_1], axis=0)
+        square = jnp.sum(held * held) + jnp.sum(grad_embed * grad_embed) + jnp.sum(grad_head * grad_head)
+        scalars = jnp.stack([square, loss_part, count.astype(f32)])
+        small = jnp.concatenate([gain_part, jnp.broadcast_to(scalars[:, None], (3, D))], axis=0)
+        small = jnp.sum(lax.all_gather(small, ("x", "y", "c"), axis=0), axis=0)
+        small = jnp.sum(lax.all_gather(small, "z", axis=0), axis=0)
+        gain_sum = small[: 2 * LAYERS + 1]
+        square_sum, loss_sum, mask_count = (small[2 * LAYERS + 1 + i, 0] for i in range(3))
+        clip_norm = jnp.sqrt(square_sum + jnp.sum(gain_sum * gain_sum)) / mask_count
+        factor = jnp.minimum(1.0, clip_limit / clip_norm) / mask_count
+
+        stat_scale = (1.0 - stat_decay) * (factor * factor)
+        linear = at_dp * n_fs + at_fs
+        basis_start = (linear % sharing) * basis_rows
+        if not paired:
             own_sum = jnp.concatenate(
                 [lax.all_gather(part, DATA, axis=0, tiled=True) for part in (stat_0, stat_1)], axis=0
             ).reshape(n_mats, D, D)[own_mat]
         sum_part = lax.dynamic_slice_in_dim(own_sum, basis_start, basis_rows)
         stat_sums = lax.all_gather(sum_part, DATA, axis=0, tiled=True).reshape(n_mats, D, D)
-        own_stat = stat_decay * flat_stats[own_mat] + stat_scale * own_sum
-        own_basis = soap_bases.reshape(n_mats, D, D)[own_mat]
-        product = nn(own_stat, own_basis, highest)
+        product = stat_decay * old_product + stat_scale * nn(own_sum, own_basis, highest)
         gram = tn(product, product, highest)
         rows = lax.dynamic_slice_in_dim(product, basis_start, basis_rows)
-        rows, gram, stat_sums = lax.optimization_barrier((rows, gram, stat_sums))
-        first, rest = orthogonal_rows(gram, rows, D // (2 * STEPS))
-        first, rows, gram = lax.optimization_barrier((first[:, : D // 2], first[:, D // 2 :], rest[D // 2 :, D // 2 :]))
-        first = lax.all_gather(first, DATA, axis=0, tiled=True)
-        second, _ = orthogonal_rows(gram, rows, D // (2 * STEPS))
-        first, second = lax.optimization_barrier((first, second))
-        second = lax.all_gather(second, DATA, axis=0, tiled=True)
+        rows, gram, own_0 = lax.optimization_barrier((rows, gram, own_0))
+        own_mats = jnp.stack([own_0, own_1])
+        new_rows = orthogonal_rows(gram, rows)
+        new_rows, stat_sums = lax.optimization_barrier((new_rows, stat_sums))
+        new_bases = lax.all_gather(new_rows, DATA, axis=0, tiled=True).reshape(soap_bases.shape)
         new_stats = (stat_decay * flat_stats + stat_scale * stat_sums).reshape(soap_stats.shape)
-        new_bases = jnp.concatenate([first, second], axis=1).reshape(soap_bases.shape)
 
         clipped = own_mats * factor
         basis_lo = jnp.take(soap_bases, lo, axis=1)

time: 1710 us -> 1620 us (0.947)
  waiting for transfers between devices: 648 us -> 550 us
    ppermute x16, waiting for transfers between devices: 279 us -> 192 us  [moved(): return lax.ppermute(value, DATA, [(int(s), int(d)) for s, d in pairs])]
    all_gather x1, waiting for transfers between devices: 28.1 us -> 0.02 us  [shards(): lax.all_gather(sum_part, DATA, axis=0, tiled=True).reshape(n_mats, D, D)]
    reduce_scatter x2, waiting for transfers between devices: 33.9 us -> 54 us  [rows_sum(): lax.psum_scatter(rows, work_axes if paired else OWNERS, scatter_dimension...]
    unnamed x260 -> x261, local copies, waits for them, and re-layouts: 28.5 us -> 41.1 us
    dot_general x50 -> x51, matrix products: 282 us -> 290 us  [dot(): lax.dot_general(a, b, (dims, ((), ())), precision=precision, preferred_el...]
    all_gather x2 -> x1, waiting for transfers between devices: 55.4 us -> 49.7 us  [shards(): lax.all_gather(new_rows, DATA, axis=0, tiled=True).reshape(soap_bases.shape)]
    pallas_call x2 -> x1, Pallas kernels: 78.9 us -> 82.9 us  [orthogonal_rows(): pl.pallas_call(orthogonal_kernel, out_shape=jax.ShapeDtypeStruct(rows.sha...]
  transfers between devices with their start and end apart: 30 -> 29, of which waited for: 22 -> 22; matrix products, arithmetic and copies ran while one was open for 21% -> 24% of each run, Pallas kernels for 9% -> 12%
where the time goes in v3:
time: 1620 us
  waiting for transfers between devices  550 us (34%)
  matrix products  324 us (20%)
  Pallas kernels  207 us (13%)
  blocking collectives  184 us (11%)
  other arithmetic  179 us (11%)
  local copies, waits for them, and re-layouts  88 us (5%)
  starting transfers between devices  54.4 us (3%)
  between operations  30.1 us (2%)
    dot_general x51, matrix products, dot(): lax.dot_general(a, b, (dims, ((), ())), precision=precision, preferred_el...  290 us
    ppermute x16, waiting for transfers between devices, moved(): return lax.ppermute(value, DATA, [(int(s), int(d)) for s, d in pairs])  192 us
    reduce_scatter x1, waiting for transfers between devices, shards(): lax.psum_scatter(nn(grad_logits, head), HEAD_GROUP, scatter_dimension=0,...  113 us
    pallas_call x1, Pallas kernels, orthogonal_rows(): pl.pallas_call(orthogonal_kernel, out_shape=jax.ShapeDtypeStruct(rows.sha...  82.9 us
    all_to_all x1, blocking collectives, stat_of_owner(): columns = lax.all_to_all(jnp.stack(to_owner), DP, 0, 0, tiled=True)  81.8 us
    pallas_call x2, Pallas kernels, attend_back(): pl.pallas_call(attend_back_kernel, grid=(PAIRS,), in_specs=[column(n_q),...  63.1 us
    pallas_call x2, Pallas kernels, attend(): pl.pallas_call(attend_kernel, grid=(PAIRS,), in_specs=[column(n_q), colum...  61.2 us
    all_gather x1, blocking collectives, shards(): lax.all_gather(jnp.stack([targets, code]), HEAD_GROUP, axis=1, tiled=True)  60.4 us
  transfers between devices with their start and end apart: 29, of which 22 were waited for; matrix products, arithmetic and copies ran while one was open for 24% of the time, Pallas kernels for 12%

profile of v3, /device:TPU:0, one launch (start us, length us, event | category | flops | bytes accessed | tf_op | source)
XLA Modules:
  0.0 1617.0 jit_solution(14989698417844597126)
XLA Ops:
  48.2 60.4 %all_gather.42 = s32[2,4096]{1,0:T(2,128)} all-gather(s32[2,256]{1,0:T(2,128)S(1)} %pad_add_fusion), channel_id=1, replica_groups=mesh['z'=4,'x'=2,'y'=2,'c'=2] {'z','y','c'}, dimensions={1}, use_global_device_ids=true | all-gather | bytes 34816 | tf_op jit(solution)/shard_map/all_gather | solution.py:566
  130.6 24.3 %all-gather.20.cloned.1.call-done = bf16[1,9216,768]{2,1,0:T(8,128)(2,1)} async-done(((bf16[1,288,768]{2,1,0:T(8,128)(2,1)}), bf16[1,9216,768]{2,1,0:T(8,128)(2,1)}) %all-gather.20.cloned.1.call-update) | async-done | bytes 14155792 | tf_op jit(solution)/shard_map/all_gather | solution.py:487
  167.2 46.1 %attend.2 = (bf16[1024,768]{1,0:T(8,128)(2,1)}, bf16[1024,768]{1,0:T(8,128)(2,1)}, bf16[1024,768]{1,0:T(8,128)(2,1)}, bf16[1024,768]{1,0:T(8,128)(2,1)}, f32[6,2,1024]{2,1,0:T(2,128)}) custom-call(f32[1024,768]{1,0:T(8,128)} %fusion.119.q_ref, f32[1024,1536]{1,0:T(8,128)} %fusion.73.k_ref.v_ref, f32[1024,1536]{1,0:T(8,128)} %fusion.73.k_ref.v_ref, ...), custom_call_target="tpu_custom_call" | custom-call | flops 1000 | bytes 1000 | tf_op jit(solution)/shard_map/attend/pallas_call | solution.py:165
  244.6 15.2 all-gather.22.cloned.1.call-done
  270.0 15.1 attend.3
  307.6 53.6 %all-gather.14.cloned.1.call-done = bf16[4096,768]{1,0:T(8,128)(2,1)} async-done(((bf16[256,768]{1,0:T(8,128)(2,1)}), bf16[4096,768]{1,0:T(8,128)(2,1)}) %all-gather.14.cloned.1.call-update) | async-done | bytes 6291472 | tf_op jit(solution)/shard_map/all_gather | solution.py:582
  361.2 21.9 %fusion.225 = (f32[4096]{0:T(1024)S(1)}, f32[4096,2000]{0,1:T(8,128)}) fusion(bf16[4096,768]{1,0:T(8,128)(2,1)} %all-gather.14.cloned.1.call-done, bf16[1000,768]{1,0:T(8,128)(2,1)} %get-tuple-element.589, bf16[1000,768]{1,0:T(8,128)(2,1)} %get-tuple-element.588), kind=kOutput, calls=%fused_computation.453 | convolution fusion | flops 12597243904 | bytes 42147840 | tf_op jit(solution)/shard_map/dot_general | solution.py:53
  383.0 18.0 %exponential_reduce_fusion = (f32[4096]{0:T(1024)S(1)}, f32[4096]{0:T(1024)S(1)}) fusion(f32[4096,2000]{0,1:T(8,128)} %get-tuple-element.646, f32[4096]{0:T(1024)S(1)} %get-tuple-element.645, s32[4096]{0:T(1024)S(1)} %bitcast.445, s32[2000]{0:T(1024)S(1)} %copy-done.70), kind=kLoop, calls=%fused_computation.35 | loop fusion | flops 40951808 | bytes 32841536 | tf_op jit(solution)/shard_map/reduce_sum | solution.py:588
  407.4 13.9 all-gather.7
  434.0 18.9 %fusion.97 = f32[4096,768]{1,0:T(8,128)} fusion(bf16[4096,2000]{0,1:T(8,128)(2,1)} %fusion.28, bf16[1000,768]{1,0:T(8,128)(2,1)S(1)} %copy-done.55, bf16[1000,768]{1,0:T(8,128)(2,1)S(1)} %copy-done.54), kind=kOutput, calls=%fused_computation.189 | convolution fusion | flops 12589056000 | bytes 32038912 | tf_op jit(solution)/shard_map/dot_general | solution.py:53
  453.0 20.0 %fusion.226 = f32[2000,768]{1,0:T(8,128)} fusion(bf16[4096,2000]{0,1:T(8,128)(2,1)} %fusion.28, bf16[4096,768]{1,0:T(8,128)(2,1)} %all-gather.14.cloned.1.call-done), kind=kOutput, calls=%fused_computation.454 | convolution fusion | flops 12582912000 | bytes 28819456 | tf_op jit(solution)/shard_map/dot_general | solution.py:53
  473.0 113.5 %reduce-scatter.4.cloned.1.call-done = f32[256,768]{1,0:T(8,128)} async-done(((f32[4096,768]{1,0:T(8,128)}), f32[256,768]{1,0:T(8,128)}) %reduce-scatter.4.cloned.1.call-update) | async-done | bytes 786448 | tf_op jit(solution)/shard_map/reduce_scatter | solution.py:606
  607.0 15.5 attend_back.2
  658.6 18.7 %dynamic-slice_bitcast_fusion = (f32[2,4,2,288,768]{4,3,2,1,0:T(8,128)}, f32[2,4,2,288,768]{4,3,2,1,0:T(8,128)}) fusion(f32[2,2,4,2,288,768]{5,4,3,2,1,0:T(8,128)} %bitcast.411, s32[]{:T(128)S(6)} %select_n.334, s32[]{:T(128)S(6)} %select_n.333), kind=kLoop, calls=%fused_computation.38 | loop fusion | bytes 56623112 | tf_op jit(solution)/shard_map/jit(dynamic_index_in_dim)/squeeze | solution.py:370
  766.3 47.6 %attend_back.3 = (bf16[1024,768]{1,0:T(8,128)(2,1)}, bf16[1024,768]{1,0:T(8,128)(2,1)}, bf16[1024,768]{1,0:T(8,128)(2,1)}) custom-call(bf16[1024,768]{1,0:T(8,128)(2,1)} %get-tuple-element.339.qs_ref, bf16[1024,768]{1,0:T(8,128)(2,1)} %get-tuple-element.340.k_ref, bf16[1024,768]{1,0:T(8,128)(2,1)} %get-tuple-element.341.v_ref, ...), custom_call_target="tpu_custom_call" | custom-call | flops 1000 | bytes 1000 | tf_op jit(solution)/shard_map/attend_back/pallas_call | solution.py:182
  813.9 37.8 %collective-permute-done.3 = f32[2,4,144,768]{3,2,1,0:T(8,128)} collective-permute-done((f32[2,4,144,768]{3,2,1,0:T(8,128)}, f32[2,4,144,768]{3,2,1,0:T(8,128)}, u32[]{:S(2)}, u32[]{:S(2)}) %collective-permute-start.3) | collective-permute-done | bytes 3538976 | tf_op jit(solution)/shard_map/ppermute | solution.py:367
  893.6 33.9 %reduce-scatter.6.cloned.1.call-done = f32[144,768]{1,0:T(8,128)} async-done(((f32[4608,768]{1,0:T(8,128)}), f32[144,768]{1,0:T(8,128)}) %reduce-scatter.6.cloned.1.call-update) | async-done | bytes 442384 | tf_op jit(solution)/shard_map/reduce_scatter | solution.py:642
  937.0 29.9 %collective-permute-done.5 = f32[4,144,768]{2,1,0:T(8,128)} collective-permute-done((f32[4,144,768]{2,1,0:T(8,128)}, f32[4,144,768]{2,1,0:T(8,128)}, u32[]{:S(2)}, u32[]{:S(2)}) %collective-permute-start.5) | collective-permute-done | bytes 1769504 | tf_op jit(solution)/shard_map/ppermute | solution.py:367
  978.2 21.5 %collective-permute-done.7 = f32[288,768]{1,0:T(8,128)} collective-permute-done((f32[288,768]{1,0:T(8,128)}, f32[288,768]{1,0:T(8,128)}, u32[]{:S(2)}, u32[]{:S(2)}) %collective-permute-start.7) | collective-permute-done | bytes 884768 | tf_op jit(solution)/shard_map/ppermute | solution.py:367
  1009.5 33.0 %collective-permute-done.9 = f32[288,768]{1,0:T(8,128)} collective-permute-done((f32[288,768]{1,0:T(8,128)}, f32[288,768]{1,0:T(8,128)}, u32[]{:S(2)}, u32[]{:S(2)}) %collective-permute-start.9) | collective-permute-done | bytes 884768 | tf_op jit(solution)/shard_map/ppermute | solution.py:367
  1053.5 14.5 collective-permute-done.11
  1087.6 16.5 %all-to-all-done.6 = f32[4,144,768]{2,1,0:T(8,128)S(1)} async-done(((f32[4,144,768]{2,1,0:T(8,128)}), f32[4,144,768]{2,1,0:T(8,128)S(1)}, u32[]{:S(2)}, u32[]{:S(2)}) %all-to-all-start.6) | async-done | bytes 1769504 | tf_op jit(solution)/shard_map/all_to_all | solution.py:438
  1104.1 20.1 %reduce-scatter.8.cloned.1.call-done = f32[144,768]{1,0:T(8,128)} async-done(((f32[4608,768]{1,0:T(8,128)}), f32[144,768]{1,0:T(8,128)}) %reduce-scatter.8.cloned.1.call-update) | async-done | bytes 442384 | tf_op jit(solution)/shard_map/reduce_scatter | solution.py:642
  1126.7 81.8 %all_to_all.121 = f32[8,144,768]{2,1,0:T(8,128)S(1)} all-to-all(f32[8,144,768]{2,1,0:T(8,128)S(1)} %fusion.155), channel_id=1, replica_groups=mesh['z'=4,'x'=2,'y'=2,'c'=2] {'z','x'}, dimensions={0} | all-to-all | bytes 7077888 | tf_op jit(solution)/shard_map/all_to_all | solution.py:633
  1232.1 48.9 %collective-permute-done.14 = f32[384,768]{1,0:T(8,128)S(1)} collective-permute-done((f32[384,768]{1,0:T(8,128)S(1)}, f32[384,768]{1,0:T(8,128)S(1)}, u32[]{:S(2)}, u32[]{:S(2)}) %collective-permute-start.14) | collective-permute-done | bytes 1179680 | tf_op jit(solution)/shard_map/ppermute | solution.py:367
  1286.9 14.8 all-to-all-done.8
  1321.7 13.3 all-to-all-done.9
  1357.3 13.8 all-gather.5
  1390.2 82.9 %orthogonal_rows.1 = f32[192,768]{1,0:T(8,128)} custom-call(f32[768,768]{1,0:T(8,128)S(1)} %fusion.228.gram_ref, f32[192,768]{1,0:T(8,128)S(1)} %constant_dynamic-slice_fusion.2.rows_ref), custom_call_target="tpu_custom_call" | custom-call | flops 199999995904 | bytes 4718592 | tf_op jit(solution)/shard_map/orthogonal_rows/pallas_call | solution.py:253
  1525.3 21.2 %multiply_add_fusion = f32[8,768,768]{2,1,0:T(8,128)} fusion(f32[8,768,768]{2,1,0:T(8,128)} %bitcast.420, f32[]{:T(128)S(6)} %mul.806, f32[2,4,768,768]{3,2,1,0:T(8,128)} %param.31), kind=kLoop, calls=%fused_computation.36 | loop fusion | flops 14155776 | bytes 56623108 | tf_op jit(solution)/shard_map/add | solution.py:724
  1546.4 49.7 %all-gather.18.cloned.1.call-done = f32[6144,768]{1,0:T(8,128)} async-done(((f32[192,768]{1,0:T(8,128)}), f32[6144,768]{1,0:T(8,128)}) %all-gather.18.cloned.1.call-update) | async-done | bytes 18874384 | tf_op jit(solution)/shard_map/all_gather | solution.py:723
  1596.2 12.7 copy.203
  (519 shorter events, 538.0 us)
Async XLA Ops:
  7.2 147.7 %all-gather.20.cloned.1.call-start = ((), (), s32[]{:S(2)}) async-start(), calls=%async_computation.19 | async-start | bytes 14598144 | tf_op jit(solution)/shard_map/all_gather | solution.py:487
  9.8 250.1 %all-gather.22.cloned.1.call-start = ((), (), s32[]{:S(2)}) async-start(), calls=%async_computation.20 | async-start | bytes 14598144 | tf_op jit(solution)/shard_map/all_gather | solution.py:570
  13.0 274.1 %copy-start.66 = (s32[1,1024]{1,0:T(1,128)}, s32[1,1024]{1,0:T(1,128)S(1)}, u32[]{:S(2)}) copy-start(s32[1,1024]{1,0:T(1,128)S(1)} %get-tuple-element.624) | copy-start | bytes 12292
  18.1 14.4 all-to-all-start.4
  37.7 79.6 %all-to-all-start.5 = ((bf16[32,40,768]{2,1,0:T(8,128)(2,1)}), bf16[32,40,768]{2,1,0:T(8,128)(2,1)S(1)}, u32[]{:S(2)}, u32[]{:S(2)}) async-start(bf16[32,40,768]{2,1,0:T(8,128)(2,1)} %bitcast.441), calls=%async_computation.5 | async-start | bytes 3932160 | tf_op jit(solution)/shard_map/all_to_all | solution.py:504
  41.2 320.0 %all-gather.14.cloned.1.call-start = ((), (), s32[]{:S(2)}) async-start(), calls=%async_computation.13 | async-start | bytes 6684672 | tf_op jit(solution)/shard_map/all_gather | solution.py:582
  43.8 197.8 %collective-permute-start = (bf16[1000,768]{1,0:T(8,128)(2,1)}, bf16[1000,768]{1,0:T(8,128)(2,1)}, u32[]{:S(2)}, u32[]{:S(2)}) collective-permute-start(bf16[1000,768]{1,0:T(8,128)(2,1)} %slice_bitcast_fusion.18), channel_id=1, source_target_pairs={{0,4},{1,5},{2,6},{3,7},{4,0},{5,1},{6,2},{7,3},{8,12},{9,13},{10,... | collective-permute-start | bytes 4608008 | tf_op jit(solution)/shard_map/ppermute | solution.py:367
  110.9 178.8 %copy-start.87 = (f32[768]{0:T(1024)}, f32[768]{0:T(1024)S(1)}, u32[]{:S(2)}) copy-start(f32[768]{0:T(1024)S(1)} %get-tuple-element.523) | copy-start | bytes 9220
  110.9 188.9 %copy-start.81 = (f32[768]{0:T(1024)}, f32[768]{0:T(1024)S(1)}, u32[]{:S(2)}) copy-start(f32[768]{0:T(1024)S(1)} %get-tuple-element.522) | copy-start | bytes 9220
  301.0 285.5 %reduce-scatter.4.cloned.1.call-start = ((), (), s32[]{:S(2)}) async-start(), calls=%async_computation.14 | async-start | bytes 13369344 | tf_op jit(solution)/shard_map/reduce_scatter | solution.py:606
  452.9 474.6 %reduce-scatter.6.cloned.1.call-start = ((), (), s32[]{:S(2)}) async-start(), calls=%async_computation.15 | async-start | bytes 14598144 | tf_op jit(solution)/shard_map/reduce_scatter | solution.py:642
  602.8 74.5 %collective-permute-start.1 = (f32[1000,768]{1,0:T(8,128)}, f32[1000,768]{1,0:T(8,128)}, u32[]{:S(2)}, u32[]{:S(2)}) collective-permute-start(f32[1000,768]{1,0:T(8,128)} %dynamic-slice_bitcast_fusion.4), channel_id=1, source_target_pairs={{0,4},{1,5},{2,6},{3,7},{4,0},{5,1},{6,2},{7,3},{8,12},{9,13},{10,... | collective-permute-start | bytes 9216008 | tf_op jit(solution)/shard_map/ppermute | solution.py:367
  677.3 28.9 %collective-permute-start.2 = (f32[2,4,2,288,768]{4,3,2,1,0:T(8,128)}, f32[2,4,2,288,768]{4,3,2,1,0:T(8,128)}, u32[]{:S(2)}, u32[]{:S(2)}) collective-permute-start(f32[2,4,2,288,768]{4,3,2,1,0:T(8,128)} %get-tuple-element.358), channel_id=1, source_target_pairs={{0,1},{1,0},{2,3},{3,2},{4,5},{5,4},{6,7},{7,6},{8,9},{9,8},{10,11... | collective-permute-start | bytes 42467336 | tf_op jit(solution)/shard_map/ppermute | solution.py:367
  759.8 364.4 %reduce-scatter.8.cloned.1.call-start = ((), (), s32[]{:S(2)}) async-start(), calls=%async_computation.16 | async-start | bytes 14598144 | tf_op jit(solution)/shard_map/reduce_scatter | solution.py:642
  759.8 91.9 %collective-permute-start.3 = (f32[2,4,144,768]{3,2,1,0:T(8,128)}, f32[2,4,144,768]{3,2,1,0:T(8,128)}, u32[]{:S(2)}, u32[]{:S(2)}) collective-permute-start(f32[2,4,144,768]{3,2,1,0:T(8,128)} %dynamic-slice_bitcast_fusion.3), channel_id=1, source_target_pairs={{0,4},{1,5},{2,6},{3,7},{4,0},{5,1},{6,2},{7,3},{8,12},{9,13},{10,... | collective-permute-start | bytes 10616840 | tf_op jit(solution)/shard_map/ppermute | solution.py:367
  760.4 91.6 %collective-permute-start.4 = (f32[4,2,144,768]{3,2,1,0:T(8,128)}, f32[4,2,144,768]{3,2,1,0:T(8,128)}, u32[]{:S(2)}, u32[]{:S(2)}) collective-permute-start(f32[4,2,144,768]{3,2,1,0:T(8,128)} %dynamic-slice_bitcast_fusion.2), channel_id=1, source_target_pairs={{0,2},{1,3},{2,0},{3,1},{4,6},{5,7},{6,4},{7,5},{8,10},{9,11},{10,... | collective-permute-start | bytes 10616840 | tf_op jit(solution)/shard_map/ppermute | solution.py:367
  927.5 39.4 %collective-permute-start.5 = (f32[4,144,768]{2,1,0:T(8,128)}, f32[4,144,768]{2,1,0:T(8,128)}, u32[]{:S(2)}, u32[]{:S(2)}) collective-permute-start(f32[4,144,768]{2,1,0:T(8,128)} %dynamic-slice_bitcast_fusion.6), channel_id=1, source_target_pairs={{0,2},{1,3},{2,0},{3,1},{4,6},{5,7},{6,4},{7,5},{8,10},{9,11},{10,... | collective-permute-start | bytes 5308424 | tf_op jit(solution)/shard_map/ppermute | solution.py:367
  928.9 39.1 %collective-permute-start.6 = (f32[4,144,768]{2,1,0:T(8,128)}, f32[4,144,768]{2,1,0:T(8,128)}, u32[]{:S(2)}, u32[]{:S(2)}) collective-permute-start(f32[4,144,768]{2,1,0:T(8,128)} %dynamic-slice_bitcast_fusion.5), channel_id=1, source_target_pairs={{0,4},{1,5},{2,6},{3,7},{4,0},{5,1},{6,2},{7,3},{8,12},{9,13},{10,... | collective-permute-start | bytes 5308424 | tf_op jit(solution)/shard_map/ppermute | solution.py:367
  973.1 26.7 %collective-permute-start.7 = (f32[288,768]{1,0:T(8,128)}, f32[288,768]{1,0:T(8,128)}, u32[]{:S(2)}, u32[]{:S(2)}) collective-permute-start(f32[288,768]{1,0:T(8,128)} %get-tuple-element.387), channel_id=1, source_target_pairs={{0,8},{1,9},{2,10},{3,11},{4,12},{5,13},{6,14},{7,15}} | collective-permute-start | bytes 2654216 | tf_op jit(solution)/shard_map/ppermute | solution.py:367
  976.6 23.1 %collective-permute-start.8 = (f32[288,768]{1,0:T(8,128)}, f32[288,768]{1,0:T(8,128)}, u32[]{:S(2)}, u32[]{:S(2)}) collective-permute-start(f32[288,768]{1,0:T(8,128)} %get-tuple-element.388), channel_id=1, source_target_pairs={{24,16},{25,17},{26,18},{27,19},{28,20},{29,21},{30,22},{31,23}} | collective-permute-start | bytes 2654216 | tf_op jit(solution)/shard_map/ppermute | solution.py:367
  1002.6 39.9 %collective-permute-start.9 = (f32[288,768]{1,0:T(8,128)}, f32[288,768]{1,0:T(8,128)}, u32[]{:S(2)}, u32[]{:S(2)}) collective-permute-start(f32[288,768]{1,0:T(8,128)} %get-tuple-element.391), channel_id=1, source_target_pairs={{0,8},{1,9},{2,10},{3,11},{4,12},{5,13},{6,14},{7,15},{8,16},{9,17... | collective-permute-start | bytes 2654216 | tf_op jit(solution)/shard_map/ppermute | solution.py:367
  1007.9 34.6 %collective-permute-start.10 = (f32[288,768]{1,0:T(8,128)}, f32[288,768]{1,0:T(8,128)}, u32[]{:S(2)}, u32[]{:S(2)}) collective-permute-start(f32[288,768]{1,0:T(8,128)} %get-tuple-element.392), channel_id=1, source_target_pairs={{16,8},{17,9},{18,10},{19,11},{20,12},{21,13},{22,14},{23,15},{24,... | collective-permute-start | bytes 2654216 | tf_op jit(solution)/shard_map/ppermute | solution.py:367
  1045.4 22.7 %collective-permute-start.11 = (f32[288,768]{1,0:T(8,128)}, f32[288,768]{1,0:T(8,128)}, u32[]{:S(2)}, u32[]{:S(2)}) collective-permute-start(f32[288,768]{1,0:T(8,128)} %get-tuple-element.395), channel_id=1, source_target_pairs={{0,8},{1,9},{2,10},{3,11},{4,12},{5,13},{6,14},{7,15},{8,16},{9,17... | collective-permute-start | bytes 2654216 | tf_op jit(solution)/shard_map/ppermute | solution.py:367
  1052.1 16.3 %collective-permute-start.12 = (f32[288,768]{1,0:T(8,128)}, f32[288,768]{1,0:T(8,128)}, u32[]{:S(2)}, u32[]{:S(2)}) collective-permute-start(f32[288,768]{1,0:T(8,128)} %get-tuple-element.396), channel_id=1, source_target_pairs={{8,0},{9,1},{10,2},{11,3},{12,4},{13,5},{14,6},{15,7},{16,8},{17,9... | collective-permute-start | bytes 2654216 | tf_op jit(solution)/shard_map/ppermute | solution.py:367
  1072.2 31.8 %all-to-all-start.6 = ((f32[4,144,768]{2,1,0:T(8,128)}), f32[4,144,768]{2,1,0:T(8,128)S(1)}, u32[]{:S(2)}, u32[]{:S(2)}) async-start(f32[4,144,768]{2,1,0:T(8,128)} %bitcast_multiply_fusion.1), calls=%async_computation.8 | async-start | bytes 3538944 | tf_op jit(solution)/shard_map/all_to_all | solution.py:438
  1208.5 93.2 %all-to-all-start.8 = ((f32[32,40,768]{2,1,0:T(8,128)}), f32[32,40,768]{2,1,0:T(8,128)}, u32[]{:S(2)}, u32[]{:S(2)}) async-start(f32[32,40,768]{2,1,0:T(8,128)} %bitcast.439), calls=%async_computation.11 | async-start | bytes 7864320 | tf_op jit(solution)/shard_map/all_to_all | solution.py:511
  1212.1 261.0 %all-gather.16.cloned.1.call-start = ((), (), s32[]{:S(2)}) async-start(), calls=%async_computation.17 | async-start | bytes 19464192 | tf_op jit(solution)/shard_map/all_gather | solution.py:715
  1227.3 2.9 collective-permute-start.13
  1230.4 50.5 %collective-permute-start.14 = (f32[384,768]{1,0:T(8,128)S(1)}, f32[384,768]{1,0:T(8,128)S(1)}, u32[]{:S(2)}, u32[]{:S(2)}) collective-permute-start(f32[384,768]{1,0:T(8,128)S(1)} %bitcast_add_fusion.5), channel_id=1, source_target_pairs={{0,2},{1,3},{2,0},{3,1},{4,6},{5,7},{6,4},{7,5},{8,10},{9,11},{10,... | collective-permute-start | bytes 3538952 | tf_op jit(solution)/shard_map/ppermute | solution.py:367
  1281.1 3.0 collective-permute-start.15
  1304.1 30.9 %all-to-all-start.9 = ((f32[4,144,768]{2,1,0:T(8,128)}), f32[4,144,768]{2,1,0:T(8,128)}, u32[]{:S(2)}, u32[]{:S(2)}) async-start(f32[4,144,768]{2,1,0:T(8,128)} %bitcast_multiply_fusion), calls=%async_computation.12 | async-start | bytes 3538944 | tf_op jit(solution)/shard_map/all_to_all | solution.py:444
  1308.5 287.6 %all-gather.18.cloned.1.call-start = ((), (), s32[]{:S(2)}) async-start(), calls=%async_computation.18 | async-start | bytes 19464192 | tf_op jit(solution)/shard_map/all_gather | solution.py:723
  (126 other events, 2539.9 us)
Sparse Core Ops, SparseCore 0:
  11.6 143.2 all-gather.19
  158.5 101.3 all-gather.21
  301.1 59.9 all-gather.13
  453.0 133.4 reduce-scatter.3
  759.9 167.5 reduce-scatter.5
  933.9 190.2 reduce-scatter.7
  1302.7 126.5 all-gather.15
  1473.2 122.8 all-gather.17

commit v4 on v3

--- a/solution.py
+++ b/solution.py
@@ -301,7 +301,7 @@
     return result, saved
 
 
-def ffn_back(grad_out, saved, weights, gains, cut, between):
+def ffn_back(grad_out, saved, weights, gains, cut, between, emit):
     _, _, w_gu, w_down = parts_of(weights)
     _, _, _, _, attended, middle, normed_ffn, gate_up, activated = saved
     grad_low = grad_out.astype(bf16)
@@ -310,7 +310,9 @@
     _, pull_act = jax.vjp(silu_up, gate_up[:, :FF], gate_up[:, FF:])
     grad_gate_up = jnp.concatenate(pull_act(grad_act), axis=1).astype(bf16)
     grad_gate_up, grad_down = between((grad_gate_up, grad_down))
-    grad_gu = [tn(grad_gate_up[:, :cut], normed_ffn), tn(grad_gate_up[:, cut:], normed_ffn)]
+    grad_gu_end = tn(grad_gate_up[:, cut:], normed_ffn)
+    grad_gate_up = emit(grad_gate_up, grad_gu_end, grad_down)
+    grad_gu = [tn(grad_gate_up[:, :cut], normed_ffn), grad_gu_end]
     _, pull_ffn = jax.vjp(rms_scale, middle, gains[1])
     grad_middle, grad_gain = pull_ffn(nn(grad_gate_up, w_gu))
     grad_middle = grad_out + grad_middle
@@ -618,6 +620,9 @@
         def same(value):
             return value
 
+        def keep(value, *others):
+            return value
+
         def stat_of_owner(work_0, work_1):
             y, c = lax.axis_index("y"), lax.axis_index("c")
             starts = ((jnp.arange(2) * 2 + y) * n_dp + at_dp) * cols + c * half
@@ -642,7 +647,7 @@
             return lax.psum_scatter(rows, work_axes if paired else OWNERS, scatter_dimension=0, tiled=True)
 
         middle_1, branch, out_1, gu_1, down_1, gain_f1 = ffn_back(
-            grad_final, saved_1, mats_1, norm_gains[2:4], cut, same
+            grad_final, saved_1, mats_1, norm_gains[2:4], cut, same, keep
         )
         grad_1, qkv_1, gain_a1 = attention_back(
             middle_1, branch, saved_1, slots, mats_1, norm_gains[2:4], docs, tables, same, same
@@ -653,17 +658,22 @@
             grad_1, head_sent = lax.optimization_barrier((grad_1, head_sent))
             grad_head = take(head_part, 0, x) + head_sent
             grad_1 = start(grad_1, lane_1)
+            early_0 = None
+
+            def emit_early(value, gu_end, down):
+                nonlocal early_0
+                value, early_0 = lax.optimization_barrier((value, jnp.concatenate([gu_end, down], axis=0)))
+                early_0 = rows_sum(early_0)
+                return value
+
             middle_0, branch, out_0, gu_0, down_0, gain_f0 = ffn_back(
-                grad_1, saved_0, mats_0, norm_gains[0:2], cut, lambda v: tick(v, lane_1)
+                grad_1, saved_0, mats_0, norm_gains[0:2], cut, lambda v: tick(v, lane_1), emit_early
             )
-            early_0 = jnp.concatenate([gu_0[1], down_0], axis=0)
-            middle_0, branch, early_0 = lax.optimization_barrier((middle_0, branch, early_0))
-            early_0 = rows_sum(early_0)
             grad_0, qkv_0, gain_a0 = attention_back(
-                middle_0, branch, saved_0, None, mats_0, norm_gains[0:2], docs, tables,
-                same, lambda v: tick(v, lane_1),
+                middle_0, branch, saved_0, None, mats_0, norm_gains[0:2], docs, tables, same, same
             )
             late_0 = jnp.concatenate([qkv_0, out_0, gu_0[0]], axis=0)
+            grad_0, late_0 = tick((grad_0, late_0), lane_1)
             grad_0, late_0, early_0 = lax.optimization_barrier((grad_0, late_0, early_0))
             late_0 = rows_sum(late_0)
             sent = embed_send(hit_0, grad_0)
@@ -681,7 +691,7 @@
         else:
             own_1 = rows_sum(jnp.concatenate([qkv_1, out_1, *gu_1, down_1], axis=0))
             middle_0, branch, out_0, gu_0, down_0, gain_f0 = ffn_back(
-                grad_1, saved_0, mats_0, norm_gains[0:2], cut, same
+                grad_1, saved_0, mats_0, norm_gains[0:2], cut, same, keep
             )
             grad_0, qkv_0, gain_a0 = attention_back(
                 middle_0, branch, saved_0, None, mats_0, norm_gains[0:2], docs, tables, same, same
@@ -697,6 +707,8 @@
         square = jnp.sum(held * held) + jnp.sum(grad_embed * grad_embed) + jnp.sum(grad_head * grad_head)
         scalars = jnp.stack([square, loss_part, count.astype(f32)])
         small = jnp.concatenate([gain_part, jnp.broadcast_to(scalars[:, None], (3, D))], axis=0)
+        if paired:
+            own_sum, small = lax.optimization_barrier((own_sum, small))
         small = jnp.sum(lax.all_gather(small, ("x", "y", "c"), axis=0), axis=0)
         small = jnp.sum(lax.all_gather(small, "z", axis=0), axis=0)
         gain_sum = small[: 2 * LAYERS + 1]
@@ -716,10 +728,9 @@
         product = stat_decay * old_product + stat_scale * nn(own_sum, own_basis, highest)
         gram = tn(product, product, highest)
         rows = lax.dynamic_slice_in_dim(product, basis_start, basis_rows)
-        rows, gram, own_0 = lax.optimization_barrier((rows, gram, own_0))
+        new_rows = orthogonal_rows(gram, rows)
+        new_rows, stat_sums, own_0 = lax.optimization_barrier((new_rows, stat_sums, own_0))
         own_mats = jnp.stack([own_0, own_1])
-        new_rows = orthogonal_rows(gram, rows)
-        new_rows, stat_sums = lax.optimization_barrier((new_rows, stat_sums))
         new_bases = lax.all_gather(new_rows, DATA, axis=0, tiled=True).reshape(soap_bases.shape)
         new_stats = (stat_decay * flat_stats + stat_scale * stat_sums).reshape(soap_stats.shape)
 

time: 1620 us -> 1610 us (level)
  waiting for transfers between devices: 550 us -> 509 us
  blocking collectives: 184 us -> 214 us
    ppermute x16, waiting for transfers between devices: 192 us -> 152 us  [moved(): return lax.ppermute(value, DATA, [(int(s), int(d)) for s, d in pairs])]
    all_to_all x0 -> x1, blocking collectives: none -> 28.8 us  [from_work(): lax.all_to_all(pieces.reshape(-1, D), FS, 0, 0, tiled=True)]
    reduce_scatter x2, waiting for transfers between devices: 54 us -> 75 us  [rows_sum(): lax.psum_scatter(rows, work_axes if paired else OWNERS, scatter_dimension...]
    unnamed x261 -> x259, local copies, waits for them, and re-layouts: 41.1 us -> 41 us
  transfers between devices with their start and end apart: 29 -> 28, of which waited for: 22 -> 18; matrix products, arithmetic and copies ran while one was open for 24% -> 25% of each run, Pallas kernels for 12% -> 12%
where the time goes in v4:
time: 1610 us; the launch traced here: 1600 us
  waiting for transfers between devices  509 us (32%)
  matrix products  324 us (20%)
  blocking collectives  214 us (13%)
  Pallas kernels  207 us (13%)
  other arithmetic  174 us (11%)
  local copies, waits for them, and re-layouts  87.7 us (5%)
  starting transfers between devices  50.2 us (3%)
  between operations  30.2 us (2%)
    dot_general x51, matrix products, dot(): lax.dot_general(a, b, (dims, ((), ())), precision=precision, preferred_el...  289 us
    ppermute x16, waiting for transfers between devices, moved(): return lax.ppermute(value, DATA, [(int(s), int(d)) for s, d in pairs])  152 us
    reduce_scatter x1, waiting for transfers between devices, shards(): lax.psum_scatter(nn(grad_logits, head), HEAD_GROUP, scatter_dimension=0,...  113 us
    pallas_call x1, Pallas kernels, orthogonal_rows(): pl.pallas_call(orthogonal_kernel, out_shape=jax.ShapeDtypeStruct(rows.sha...  82.9 us
    all_to_all x1, blocking collectives, stat_of_owner(): columns = lax.all_to_all(jnp.stack(to_owner), DP, 0, 0, tiled=True)  81.8 us
    reduce_scatter x2, waiting for transfers between devices, rows_sum(): lax.psum_scatter(rows, work_axes if paired else OWNERS, scatter_dimension...  75 us
    pallas_call x2, Pallas kernels, attend_back(): pl.pallas_call(attend_back_kernel, grid=(PAIRS,), in_specs=[column(n_q),...  63 us
    pallas_call x2, Pallas kernels, attend(): pl.pallas_call(attend_kernel, grid=(PAIRS,), in_specs=[column(n_q), colum...  61.3 us
  transfers between devices with their start and end apart: 28, of which 18 were waited for; matrix products, arithmetic and copies ran while one was open for 25% of the time, Pallas kernels for 12%

profile of v4, /device:TPU:0, one launch (start us, length us, event | category | flops | bytes accessed | tf_op | source)
XLA Modules:
  0.0 1597.2 jit_solution(7195366888769859186)
XLA Ops:
  48.2 60.3 %all_gather.42 = s32[2,4096]{1,0:T(2,128)} all-gather(s32[2,256]{1,0:T(2,128)S(1)} %pad_add_fusion), channel_id=1, replica_groups=mesh['z'=4,'x'=2,'y'=2,'c'=2] {'z','y','c'}, dimensions={1}, use_global_device_ids=true | all-gather | bytes 34816 | tf_op jit(solution)/shard_map/all_gather | solution.py:568
  130.6 24.3 %all-gather.20.cloned.1.call-done = bf16[1,9216,768]{2,1,0:T(8,128)(2,1)} async-done(((bf16[1,288,768]{2,1,0:T(8,128)(2,1)}), bf16[1,9216,768]{2,1,0:T(8,128)(2,1)}) %all-gather.20.cloned.1.call-update) | async-done | bytes 14155792 | tf_op jit(solution)/shard_map/all_gather | solution.py:489
  167.2 46.1 %attend.2 = (bf16[1024,768]{1,0:T(8,128)(2,1)}, bf16[1024,768]{1,0:T(8,128)(2,1)}, bf16[1024,768]{1,0:T(8,128)(2,1)}, bf16[1024,768]{1,0:T(8,128)(2,1)}, f32[6,2,1024]{2,1,0:T(2,128)}) custom-call(f32[1024,768]{1,0:T(8,128)} %fusion.119.q_ref, f32[1024,1536]{1,0:T(8,128)} %fusion.73.k_ref.v_ref, f32[1024,1536]{1,0:T(8,128)} %fusion.73.k_ref.v_ref, ...), custom_call_target="tpu_custom_call" | custom-call | flops 1000 | bytes 1000 | tf_op jit(solution)/shard_map/attend/pallas_call | solution.py:165
  244.8 15.1 all-gather.22.cloned.1.call-done
  270.1 15.2 attend.3
  307.7 53.5 %all-gather.14.cloned.1.call-done = bf16[4096,768]{1,0:T(8,128)(2,1)} async-done(((bf16[256,768]{1,0:T(8,128)(2,1)}), bf16[4096,768]{1,0:T(8,128)(2,1)}) %all-gather.14.cloned.1.call-update) | async-done | bytes 6291472 | tf_op jit(solution)/shard_map/all_gather | solution.py:584
  361.2 21.9 %fusion.225 = (f32[4096]{0:T(1024)S(1)}, f32[4096,2000]{0,1:T(8,128)}) fusion(bf16[4096,768]{1,0:T(8,128)(2,1)} %all-gather.14.cloned.1.call-done, bf16[1000,768]{1,0:T(8,128)(2,1)} %get-tuple-element.581, bf16[1000,768]{1,0:T(8,128)(2,1)} %get-tuple-element.580), kind=kOutput, calls=%fused_computation.454 | convolution fusion | flops 12597243904 | bytes 42147840 | tf_op jit(solution)/shard_map/dot_general | solution.py:53
  383.1 18.0 %exponential_reduce_fusion = (f32[4096]{0:T(1024)S(1)}, f32[4096]{0:T(1024)S(1)}) fusion(f32[4096,2000]{0,1:T(8,128)} %get-tuple-element.638, f32[4096]{0:T(1024)S(1)} %get-tuple-element.637, s32[4096]{0:T(1024)S(1)} %bitcast.444, s32[2000]{0:T(1024)S(1)} %copy-done.66), kind=kLoop, calls=%fused_computation.35 | loop fusion | flops 40951808 | bytes 32841536 | tf_op jit(solution)/shard_map/reduce_sum | solution.py:590
  407.5 13.9 all-gather.7
  434.1 18.9 %fusion.97 = f32[4096,768]{1,0:T(8,128)} fusion(bf16[4096,2000]{0,1:T(8,128)(2,1)} %fusion.28, bf16[1000,768]{1,0:T(8,128)(2,1)S(1)} %copy-done.51, bf16[1000,768]{1,0:T(8,128)(2,1)S(1)} %copy-done.50), kind=kOutput, calls=%fused_computation.189 | convolution fusion | flops 12589056000 | bytes 32038912 | tf_op jit(solution)/shard_map/dot_general | solution.py:53
  453.1 20.0 %fusion.226 = f32[2000,768]{1,0:T(8,128)} fusion(bf16[4096,2000]{0,1:T(8,128)(2,1)} %fusion.28, bf16[4096,768]{1,0:T(8,128)(2,1)} %all-gather.14.cloned.1.call-done), kind=kOutput, calls=%fused_computation.455 | convolution fusion | flops 12582912000 | bytes 28819456 | tf_op jit(solution)/shard_map/dot_general | solution.py:53
  473.1 113.5 %reduce-scatter.4.cloned.1.call-done = f32[256,768]{1,0:T(8,128)} async-done(((f32[4096,768]{1,0:T(8,128)}), f32[256,768]{1,0:T(8,128)}) %reduce-scatter.4.cloned.1.call-update) | async-done | bytes 786448 | tf_op jit(solution)/shard_map/reduce_scatter | solution.py:608
  607.0 15.5 attend_back.2
  658.6 18.7 %dynamic-slice_bitcast_fusion.1 = (f32[2,4,2,288,768]{4,3,2,1,0:T(8,128)}, f32[2,4,2,288,768]{4,3,2,1,0:T(8,128)}) fusion(f32[2,2,4,2,288,768]{5,4,3,2,1,0:T(8,128)} %bitcast.409, s32[]{:T(128)S(6)} %select_n.333, s32[]{:T(128)S(6)} %select_n.335), kind=kLoop, calls=%fused_computation.39 | loop fusion | bytes 56623112 | tf_op jit(solution)/shard_map/jit(dynamic_index_in_dim)/squeeze | solution.py:372
  739.7 13.0 multiply_reduce_fusion.1
  759.5 47.5 %attend_back.3 = (bf16[1024,768]{1,0:T(8,128)(2,1)}, bf16[1024,768]{1,0:T(8,128)(2,1)}, bf16[1024,768]{1,0:T(8,128)(2,1)}) custom-call(bf16[1024,768]{1,0:T(8,128)(2,1)} %get-tuple-element.359.qs_ref, bf16[1024,768]{1,0:T(8,128)(2,1)} %get-tuple-element.360.k_ref, bf16[1024,768]{1,0:T(8,128)(2,1)} %get-tuple-element.361.v_ref, ...), custom_call_target="tpu_custom_call" | custom-call | flops 1000 | bytes 1000 | tf_op jit(solution)/shard_map/attend_back/pallas_call | solution.py:182
  850.4 54.5 %reduce-scatter.6.cloned.1.call-done = f32[144,768]{1,0:T(8,128)} async-done(((f32[4608,768]{1,0:T(8,128)}), f32[144,768]{1,0:T(8,128)}) %reduce-scatter.6.cloned.1.call-update) | async-done | bytes 442384 | tf_op jit(solution)/shard_map/reduce_scatter | solution.py:647
  914.7 30.0 %collective-permute-done.5 = f32[4,144,768]{2,1,0:T(8,128)} collective-permute-done((f32[4,144,768]{2,1,0:T(8,128)}, f32[4,144,768]{2,1,0:T(8,128)}, u32[]{:S(2)}, u32[]{:S(2)}) %collective-permute-start.5) | collective-permute-done | bytes 1769504 | tf_op jit(solution)/shard_map/ppermute | solution.py:369
  955.9 21.3 %collective-permute-done.7 = f32[288,768]{1,0:T(8,128)} collective-permute-done((f32[288,768]{1,0:T(8,128)}, f32[288,768]{1,0:T(8,128)}, u32[]{:S(2)}, u32[]{:S(2)}) %collective-permute-start.7) | collective-permute-done | bytes 884768 | tf_op jit(solution)/shard_map/ppermute | solution.py:369
  986.9 33.1 %collective-permute-done.9 = f32[288,768]{1,0:T(8,128)} collective-permute-done((f32[288,768]{1,0:T(8,128)}, f32[288,768]{1,0:T(8,128)}, u32[]{:S(2)}, u32[]{:S(2)}) %collective-permute-start.9) | collective-permute-done | bytes 884768 | tf_op jit(solution)/shard_map/ppermute | solution.py:369
  1031.2 14.5 collective-permute-done.11
  1065.3 16.9 %all-to-all-done.6 = f32[4,144,768]{2,1,0:T(8,128)S(1)} async-done(((f32[4,144,768]{2,1,0:T(8,128)}), f32[4,144,768]{2,1,0:T(8,128)S(1)}, u32[]{:S(2)}, u32[]{:S(2)}) %all-to-all-start.6) | async-done | bytes 1769504 | tf_op jit(solution)/shard_map/all_to_all | solution.py:440
  1082.3 20.5 %reduce-scatter.8.cloned.1.call-done = f32[144,768]{1,0:T(8,128)} async-done(((f32[4608,768]{1,0:T(8,128)}), f32[144,768]{1,0:T(8,128)}) %reduce-scatter.8.cloned.1.call-update) | async-done | bytes 442384 | tf_op jit(solution)/shard_map/reduce_scatter | solution.py:647
  1105.3 81.8 %all_to_all.121 = f32[8,144,768]{2,1,0:T(8,128)S(1)} all-to-all(f32[8,144,768]{2,1,0:T(8,128)S(1)} %fusion.157), channel_id=1, replica_groups=mesh['z'=4,'x'=2,'y'=2,'c'=2] {'z','x'}, dimensions={0} | all-to-all | bytes 7077888 | tf_op jit(solution)/shard_map/all_to_all | solution.py:638
  1210.7 48.8 %collective-permute-done.14 = f32[384,768]{1,0:T(8,128)S(1)} collective-permute-done((f32[384,768]{1,0:T(8,128)S(1)}, f32[384,768]{1,0:T(8,128)S(1)}, u32[]{:S(2)}, u32[]{:S(2)}) %collective-permute-start.14) | collective-permute-done | bytes 1179680 | tf_op jit(solution)/shard_map/ppermute | solution.py:369
  1295.6 28.8 %all_to_all.122 = f32[4,144,768]{2,1,0:T(8,128)S(1)} all-to-all(f32[4,144,768]{2,1,0:T(8,128)S(1)} %bitcast_multiply_fusion), channel_id=1, replica_groups=mesh['z'=4,'x'=2,'y'=2,'c'=2] {'y','c'}, dimensions={0} | all-to-all | bytes 3538944 | tf_op jit(solution)/shard_map/all_to_all | solution.py:446
  1334.1 14.6 all-gather.5
  1367.6 82.9 %orthogonal_rows.1 = f32[192,768]{1,0:T(8,128)} custom-call(f32[768,768]{1,0:T(8,128)S(1)} %fusion.228.gram_ref, f32[192,768]{1,0:T(8,128)S(1)} %constant_dynamic-slice_fusion.2.rows_ref), custom_call_target="tpu_custom_call" | custom-call | flops 199999995904 | bytes 4718592 | tf_op jit(solution)/shard_map/orthogonal_rows/pallas_call | solution.py:253
  1457.7 15.9 multiply_subtract_fusion
  1508.4 14.2 multiply_add_fusion
  1522.6 53.7 %all-gather.18.cloned.1.call-done = f32[6144,768]{1,0:T(8,128)} async-done(((f32[192,768]{1,0:T(8,128)}), f32[6144,768]{1,0:T(8,128)}) %all-gather.18.cloned.1.call-update) | async-done | bytes 18874384 | tf_op jit(solution)/shard_map/all_gather | solution.py:734
  1576.3 12.7 copy.203
  (516 shorter events, 507.3 us)
Async XLA Ops:
  7.2 147.7 %all-gather.20.cloned.1.call-start = ((), (), s32[]{:S(2)}) async-start(), calls=%async_computation.19 | async-start | bytes 14598144 | tf_op jit(solution)/shard_map/all_gather | solution.py:489
  9.8 250.1 %all-gather.22.cloned.1.call-start = ((), (), s32[]{:S(2)}) async-start(), calls=%async_computation.20 | async-start | bytes 14598144 | tf_op jit(solution)/shard_map/all_gather | solution.py:572
  13.0 274.1 %copy-start.62 = (s32[1,1024]{1,0:T(1,128)}, s32[1,1024]{1,0:T(1,128)S(1)}, u32[]{:S(2)}) copy-start(s32[1,1024]{1,0:T(1,128)S(1)} %get-tuple-element.616) | copy-start | bytes 12292
  18.1 14.4 all-to-all-start.4
  37.7 79.6 %all-to-all-start.5 = ((bf16[32,40,768]{2,1,0:T(8,128)(2,1)}), bf16[32,40,768]{2,1,0:T(8,128)(2,1)S(1)}, u32[]{:S(2)}, u32[]{:S(2)}) async-start(bf16[32,40,768]{2,1,0:T(8,128)(2,1)} %bitcast.440), calls=%async_computation.5 | async-start | bytes 3932160 | tf_op jit(solution)/shard_map/all_to_all | solution.py:506
  41.2 320.0 %all-gather.14.cloned.1.call-start = ((), (), s32[]{:S(2)}) async-start(), calls=%async_computation.13 | async-start | bytes 6684672 | tf_op jit(solution)/shard_map/all_gather | solution.py:584
  43.8 197.8 %collective-permute-start = (bf16[1000,768]{1,0:T(8,128)(2,1)}, bf16[1000,768]{1,0:T(8,128)(2,1)}, u32[]{:S(2)}, u32[]{:S(2)}) collective-permute-start(bf16[1000,768]{1,0:T(8,128)(2,1)} %slice_bitcast_fusion.18), channel_id=1, source_target_pairs={{0,4},{1,5},{2,6},{3,7},{4,0},{5,1},{6,2},{7,3},{8,12},{9,13},{10,... | collective-permute-start | bytes 4608008 | tf_op jit(solution)/shard_map/ppermute | solution.py:369
  110.9 178.8 %copy-start.85 = (f32[768]{0:T(1024)}, f32[768]{0:T(1024)S(1)}, u32[]{:S(2)}) copy-start(f32[768]{0:T(1024)S(1)} %get-tuple-element.517) | copy-start | bytes 9220
  110.9 189.0 %copy-start.77 = (f32[768]{0:T(1024)}, f32[768]{0:T(1024)S(1)}, u32[]{:S(2)}) copy-start(f32[768]{0:T(1024)S(1)} %get-tuple-element.516) | copy-start | bytes 9220
  301.1 285.5 %reduce-scatter.4.cloned.1.call-start = ((), (), s32[]{:S(2)}) async-start(), calls=%async_computation.14 | async-start | bytes 13369344 | tf_op jit(solution)/shard_map/reduce_scatter | solution.py:608
  453.0 452.0 %reduce-scatter.6.cloned.1.call-start = ((), (), s32[]{:S(2)}) async-start(), calls=%async_computation.15 | async-start | bytes 14598144 | tf_op jit(solution)/shard_map/reduce_scatter | solution.py:647
  453.1 135.7 %copy-start.110 = (f32[256]{0:T(256)S(1)}, f32[256]{0:T(256)}, u32[]{:S(2)}) copy-start(f32[256]{0:T(256)} %copy-done.109) | copy-start | bytes 3076
  602.8 74.5 %collective-permute-start.1 = (f32[1000,768]{1,0:T(8,128)}, f32[1000,768]{1,0:T(8,128)}, u32[]{:S(2)}, u32[]{:S(2)}) collective-permute-start(f32[1000,768]{1,0:T(8,128)} %dynamic-slice_bitcast_fusion.4), channel_id=1, source_target_pairs={{0,4},{1,5},{2,6},{3,7},{4,0},{5,1},{6,2},{7,3},{8,12},{9,13},{10,... | collective-permute-start | bytes 9216008 | tf_op jit(solution)/shard_map/ppermute | solution.py:369
  677.3 29.0 %collective-permute-start.2 = (f32[2,4,2,288,768]{4,3,2,1,0:T(8,128)}, f32[2,4,2,288,768]{4,3,2,1,0:T(8,128)}, u32[]{:S(2)}, u32[]{:S(2)}) collective-permute-start(f32[2,4,2,288,768]{4,3,2,1,0:T(8,128)} %get-tuple-element.352), channel_id=1, source_target_pairs={{0,1},{1,0},{2,3},{3,2},{4,5},{5,4},{6,7},{7,6},{8,9},{9,8},{10,11... | collective-permute-start | bytes 42467336 | tf_op jit(solution)/shard_map/ppermute | solution.py:369
  737.5 365.3 %reduce-scatter.8.cloned.1.call-start = ((), (), s32[]{:S(2)}) async-start(), calls=%async_computation.16 | async-start | bytes 14598144 | tf_op jit(solution)/shard_map/reduce_scatter | solution.py:647
  737.6 100.7 %collective-permute-start.3 = (f32[2,4,144,768]{3,2,1,0:T(8,128)}, f32[2,4,144,768]{3,2,1,0:T(8,128)}, u32[]{:S(2)}, u32[]{:S(2)}) collective-permute-start(f32[2,4,144,768]{3,2,1,0:T(8,128)} %dynamic-slice_bitcast_fusion.3), channel_id=1, source_target_pairs={{0,4},{1,5},{2,6},{3,7},{4,0},{5,1},{6,2},{7,3},{8,12},{9,13},{10,... | collective-permute-start | bytes 10616840 | tf_op jit(solution)/shard_map/ppermute | solution.py:369
  738.2 100.1 %collective-permute-start.4 = (f32[4,2,144,768]{3,2,1,0:T(8,128)}, f32[4,2,144,768]{3,2,1,0:T(8,128)}, u32[]{:S(2)}, u32[]{:S(2)}) collective-permute-start(f32[4,2,144,768]{3,2,1,0:T(8,128)} %dynamic-slice_bitcast_fusion.2), channel_id=1, source_target_pairs={{0,2},{1,3},{2,0},{3,1},{4,6},{5,7},{6,4},{7,5},{8,10},{9,11},{10,... | collective-permute-start | bytes 10616840 | tf_op jit(solution)/shard_map/ppermute | solution.py:369
  905.0 39.7 %collective-permute-start.5 = (f32[4,144,768]{2,1,0:T(8,128)}, f32[4,144,768]{2,1,0:T(8,128)}, u32[]{:S(2)}, u32[]{:S(2)}) collective-permute-start(f32[4,144,768]{2,1,0:T(8,128)} %dynamic-slice_bitcast_fusion.6), channel_id=1, source_target_pairs={{0,2},{1,3},{2,0},{3,1},{4,6},{5,7},{6,4},{7,5},{8,10},{9,11},{10,... | collective-permute-start | bytes 5308424 | tf_op jit(solution)/shard_map/ppermute | solution.py:369
  906.7 39.1 %collective-permute-start.6 = (f32[4,144,768]{2,1,0:T(8,128)}, f32[4,144,768]{2,1,0:T(8,128)}, u32[]{:S(2)}, u32[]{:S(2)}) collective-permute-start(f32[4,144,768]{2,1,0:T(8,128)} %dynamic-slice_bitcast_fusion.5), channel_id=1, source_target_pairs={{0,4},{1,5},{2,6},{3,7},{4,0},{5,1},{6,2},{7,3},{8,12},{9,13},{10,... | collective-permute-start | bytes 5308424 | tf_op jit(solution)/shard_map/ppermute | solution.py:369
  950.9 26.3 %collective-permute-start.7 = (f32[288,768]{1,0:T(8,128)}, f32[288,768]{1,0:T(8,128)}, u32[]{:S(2)}, u32[]{:S(2)}) collective-permute-start(f32[288,768]{1,0:T(8,128)} %get-tuple-element.381), channel_id=1, source_target_pairs={{0,8},{1,9},{2,10},{3,11},{4,12},{5,13},{6,14},{7,15}} | collective-permute-start | bytes 2654216 | tf_op jit(solution)/shard_map/ppermute | solution.py:369
  954.3 22.9 %collective-permute-start.8 = (f32[288,768]{1,0:T(8,128)}, f32[288,768]{1,0:T(8,128)}, u32[]{:S(2)}, u32[]{:S(2)}) collective-permute-start(f32[288,768]{1,0:T(8,128)} %get-tuple-element.382), channel_id=1, source_target_pairs={{24,16},{25,17},{26,18},{27,19},{28,20},{29,21},{30,22},{31,23}} | collective-permute-start | bytes 2654216 | tf_op jit(solution)/shard_map/ppermute | solution.py:369
  980.0 40.0 %collective-permute-start.9 = (f32[288,768]{1,0:T(8,128)}, f32[288,768]{1,0:T(8,128)}, u32[]{:S(2)}, u32[]{:S(2)}) collective-permute-start(f32[288,768]{1,0:T(8,128)} %get-tuple-element.385), channel_id=1, source_target_pairs={{0,8},{1,9},{2,10},{3,11},{4,12},{5,13},{6,14},{7,15},{8,16},{9,17... | collective-permute-start | bytes 2654216 | tf_op jit(solution)/shard_map/ppermute | solution.py:369
  985.3 34.7 %collective-permute-start.10 = (f32[288,768]{1,0:T(8,128)}, f32[288,768]{1,0:T(8,128)}, u32[]{:S(2)}, u32[]{:S(2)}) collective-permute-start(f32[288,768]{1,0:T(8,128)} %get-tuple-element.386), channel_id=1, source_target_pairs={{16,8},{17,9},{18,10},{19,11},{20,12},{21,13},{22,14},{23,15},{24,... | collective-permute-start | bytes 2654216 | tf_op jit(solution)/shard_map/ppermute | solution.py:369
  1022.9 22.8 %collective-permute-start.11 = (f32[288,768]{1,0:T(8,128)}, f32[288,768]{1,0:T(8,128)}, u32[]{:S(2)}, u32[]{:S(2)}) collective-permute-start(f32[288,768]{1,0:T(8,128)} %get-tuple-element.389), channel_id=1, source_target_pairs={{0,8},{1,9},{2,10},{3,11},{4,12},{5,13},{6,14},{7,15},{8,16},{9,17... | collective-permute-start | bytes 2654216 | tf_op jit(solution)/shard_map/ppermute | solution.py:369
  1029.7 16.0 %collective-permute-start.12 = (f32[288,768]{1,0:T(8,128)}, f32[288,768]{1,0:T(8,128)}, u32[]{:S(2)}, u32[]{:S(2)}) collective-permute-start(f32[288,768]{1,0:T(8,128)} %get-tuple-element.390), channel_id=1, source_target_pairs={{8,0},{9,1},{10,2},{11,3},{12,4},{13,5},{14,6},{15,7},{16,8},{17,9... | collective-permute-start | bytes 2654216 | tf_op jit(solution)/shard_map/ppermute | solution.py:369
  1049.7 32.6 %all-to-all-start.6 = ((f32[4,144,768]{2,1,0:T(8,128)}), f32[4,144,768]{2,1,0:T(8,128)S(1)}, u32[]{:S(2)}, u32[]{:S(2)}) async-start(f32[4,144,768]{2,1,0:T(8,128)} %bitcast_multiply_fusion.1), calls=%async_computation.8 | async-start | bytes 3538944 | tf_op jit(solution)/shard_map/all_to_all | solution.py:440
  1187.1 93.2 %all-to-all-start.8 = ((f32[32,40,768]{2,1,0:T(8,128)}), f32[32,40,768]{2,1,0:T(8,128)}, u32[]{:S(2)}, u32[]{:S(2)}) async-start(f32[32,40,768]{2,1,0:T(8,128)} %bitcast.438), calls=%async_computation.11 | async-start | bytes 7864320 | tf_op jit(solution)/shard_map/all_to_all | solution.py:513
  1190.6 259.9 %all-gather.16.cloned.1.call-start = ((), (), s32[]{:S(2)}) async-start(), calls=%async_computation.17 | async-start | bytes 19464192 | tf_op jit(solution)/shard_map/all_gather | solution.py:727
  1205.9 2.9 collective-permute-start.13
  1209.0 50.5 %collective-permute-start.14 = (f32[384,768]{1,0:T(8,128)S(1)}, f32[384,768]{1,0:T(8,128)S(1)}, u32[]{:S(2)}, u32[]{:S(2)}) collective-permute-start(f32[384,768]{1,0:T(8,128)S(1)} %bitcast_add_fusion.5), channel_id=1, source_target_pairs={{0,2},{1,3},{2,0},{3,1},{4,6},{5,7},{6,4},{7,5},{8,10},{9,11},{10,... | collective-permute-start | bytes 3538952 | tf_op jit(solution)/shard_map/ppermute | solution.py:369
  1260.6 13.1 collective-permute-start.15
  1294.1 282.2 %all-gather.18.cloned.1.call-start = ((), (), s32[]{:S(2)}) async-start(), calls=%async_computation.18 | async-start | bytes 19464192 | tf_op jit(solution)/shard_map/all_gather | solution.py:734
  (124 other events, 2798.9 us)
Sparse Core Ops, SparseCore 0:
  11.6 143.2 all-gather.19
  158.5 101.3 all-gather.21
  301.2 59.9 all-gather.13
  453.1 133.3 reduce-scatter.3
  737.6 167.2 reduce-scatter.5
  911.4 191.3 reduce-scatter.7
  1294.2 128.4 all-gather.15
  1450.6 125.5 all-gather.17
